TPU v7x, 512 devices: a whole 4x8x8 slice. The times are simulated.
512 devices in a mesh: stn: 64 (over z, y_hi, x), tm: 8 (over y_lo, core).
Axes of the slice: x: 4, y: 8 (y_hi: 2, y_lo: 4; y = y_hi * 4 + y_lo), z: 8, core: 2. Of those that a mesh axis runs over, the one named last changes fastest.
Arguments:
- voltages: bfloat16 [512, 256, 2, 2048], P('stn', 'tm'), may hold values from -12 to 12
- gains: float32 [2, 512, 2048], P(None, 'stn'), may hold values from -4 to 4
Outputs:
- visibilities: float32 [512, 128, 2, 512], P('tm', 'stn')
All inputs are finite; a program needn't handle non-finite values.
Results may differ from a plain program's by a relative error of at most 0.0011.
Values may be sent and summed in bfloat16 or wider, within the bound.
No kernel may reach another device: no remote copies, remote signals or barrier semaphores. Data moves between devices by JAX's collectives and lax.ppermute only.
A program may use at most 128 MiB of HBM per device.

v0:
```python
import jax
import jax.numpy as jnp
from jax import lax
from jax.sharding import PartitionSpec as P

RADIX_A = 16
RADIX_B = 128
CHANNELS = 2048
TAPS = 16
AVG = 16


def shifted(block, axis, distance):
    devices = range(lax.axis_size(axis))
    route = [(i - distance, i) for i in devices if i - distance in devices]
    return lax.ppermute(block, axis, route)


def window_table():
    position = jnp.arange(TAPS * CHANNELS, dtype=jnp.float32) + 0.5
    shape_part = jnp.sinc((position - TAPS * CHANNELS / 2) / CHANNELS)
    taper = jnp.sin(jnp.pi * position / (TAPS * CHANNELS)) ** 2
    return (shape_part * taper).reshape(TAPS, CHANNELS)


def section_matrix(length):
    index = jnp.arange(length, dtype=jnp.int32)
    angle = (index[:, None] * index[None, :] % length).astype(jnp.float32) * (2.0 * jnp.pi / length)
    cosine, sine = (jnp.cos(angle), jnp.sin(angle))
    from_real = jnp.stack([cosine, -sine], axis=1)
    from_imag = jnp.stack([sine, cosine], axis=1)
    return jnp.stack([from_real, from_imag], axis=0)


def transform(stacked):
    first = jnp.arange(RADIX_A, dtype=jnp.int32)
    second = jnp.arange(RADIX_B, dtype=jnp.int32)
    angle_twist = (first[:, None] * second[None, :]).astype(jnp.float32) * (2.0 * jnp.pi / CHANNELS)
    cos_twist, sin_twist = (jnp.cos(angle_twist), jnp.sin(angle_twist))
    level = lax.Precision.HIGH
    section = jnp.einsum("ifsmn,smtk->iftkn", stacked, section_matrix(RADIX_A), precision=level)
    twisted_real = section[:, :, 0] * cos_twist + section[:, :, 1] * sin_twist
    twisted_imag = section[:, :, 1] * cos_twist - section[:, :, 0] * sin_twist
    twisted = jnp.stack([twisted_real, twisted_imag], axis=2)
    result = jnp.einsum("iftkn,tnuq->ifukq", twisted, section_matrix(RADIX_B), precision=level)
    return (result[:, :, 0] * CHANNELS ** (-0.5), result[:, :, 1] * CHANNELS ** (-0.5))


def rotate(values):
    return jnp.stack([-values[:, :, :, :, 1], values[:, :, :, :, 0]], axis=4)


def gram_rows(row_part, columns, rotated):
    pattern = "nfagrpq,mfagrpq->napm"
    real_part = jnp.einsum(pattern, row_part, columns, preferred_element_type=jnp.float32)
    imag_part = jnp.einsum(pattern, row_part, rotated, preferred_element_type=jnp.float32)
    merged = jnp.stack([real_part, imag_part], axis=3)
    return merged.reshape(merged.shape[0], merged.shape[1] * merged.shape[2], 2, merged.shape[4])


def on_device(voltages, gains):
    inputs_dev, frames_dev = (voltages.shape[0], voltages.shape[1])
    history = voltages[:, frames_dev - (TAPS - 1) :]
    earlier = shifted(history, "tm", 1)
    extended = jnp.concatenate([earlier, voltages], axis=1)
    window = window_table()
    filtered = extended[:, 0:frames_dev].astype(jnp.float32) * window[0]
    for t in range(1, TAPS):
        filtered = filtered + extended[:, t : t + frames_dev].astype(jnp.float32) * window[t]
    out_real, out_imag = transform(filtered.reshape(inputs_dev, frames_dev, 2, RADIX_A, RADIX_B))
    station_count = lax.axis_size("stn")
    time_count = lax.axis_size("tm")
    channels_dev = CHANNELS // station_count
    channels_sub = channels_dev // time_count
    layout = (inputs_dev, frames_dev, station_count, time_count, channels_sub)
    natural_real = jnp.transpose(out_real, (0, 1, 3, 2)).reshape(layout)
    natural_imag = jnp.transpose(out_imag, (0, 1, 3, 2)).reshape(layout)
    gain_real = gains[0].reshape(inputs_dev, 1, station_count, time_count, channels_sub)
    gain_imag = gains[1].reshape(inputs_dev, 1, station_count, time_count, channels_sub)
    equal_real = (natural_real * gain_real - natural_imag * gain_imag).astype(jnp.bfloat16)
    equal_imag = (natural_real * gain_imag + natural_imag * gain_real).astype(jnp.bfloat16)
    spectra = jnp.stack([equal_real, equal_imag], axis=4).reshape(
        inputs_dev, frames_dev, 2 * CHANNELS
    )
    total = inputs_dev * station_count
    piece = min(channels_sub, AVG)
    per_out = channels_sub // piece
    gather_count = AVG // piece
    groups = time_count // gather_count
    scale = 1.0 / (frames_dev * time_count * AVG)
    turned = lax.all_to_all(spectra, "stn", split_axis=2, concat_axis=0, tiled=True)
    values = turned.reshape(total, frames_dev, groups, gather_count, 2, per_out, piece)
    rotated = rotate(values)
    summed = lax.psum_scatter(
        gram_rows(values, values, rotated), "tm", scatter_dimension=0, tiled=True
    )
    return summed * scale


def solution(mesh):
    return jax.shard_map(
        on_device,
        mesh=mesh,
        in_specs=(P("stn", "tm", None, None), P(None, "stn", None)),
        out_specs=P("tm", "stn", None, None),
        check_vma=False,
    )
```

profile of v0, /device:TPU:1, one launch (start us, length us, event | category | flops | bytes accessed | tf_op | source)
XLA Modules:
  0.0 386.9 jit_solution(15084850660086704466)
XLA Ops:
  6.5 0.0 copy-start
  6.5 0.0 all-reduce.3.cloned.1.call-start
  6.5 3.0 slice.138
  9.5 4.6 %collective-permute-start = (bf16[8,15,2,2048]{3,2,1,0:T(2,128)(2,1)}, bf16[8,15,2,2048]{3,2,1,0:T(2,128)(2,1)}, u32[]{:S(2)}, u32[]{:S(2)}) collective-permute-start(bf16[8,15,2,2048]{3,2,1,0:T(2,128)(2,1)} %slice.138), channel_id=1, source_target_pairs={{0,1},{1,2},{2,3},{3,4},{4,5},{5,6},{6,7},{8,9},{9,10},{10,11},{11... | collective-permute-start | bytes 2949128 | tf_op jit(solution)/shard_map/ppermute | solution.py:16
  14.1 0.1 fusion.69
  14.2 0.1 fusion.71
  14.2 0.3 fusion.60
  14.5 0.9 fusion.76
  15.4 0.3 copy.26
  15.7 1.3 copy.28
  17.0 0.1 fusion.64
  17.1 0.3 fusion.58
  17.4 0.6 fusion.26
  18.1 7.4 %collective-permute-done = bf16[8,15,2,2048]{3,2,1,0:T(2,128)(2,1)} collective-permute-done((bf16[8,15,2,2048]{3,2,1,0:T(2,128)(2,1)}, bf16[8,15,2,2048]{3,2,1,0:T(2,128)(2,1)}, u32[]{:S(2)}, u32[]{:S(2)}) %collective-permute-start) | collective-permute-done | bytes 983072 | tf_op jit(solution)/shard_map/ppermute | solution.py:16
  25.4 1.9 constant_dynamic-update-slice_fusion.1
  27.3 0.0 copy-done
  27.3 2.1 constant_dynamic-update-slice_fusion
  29.4 34.0 %multiply_add_fusion = f32[8,32,2,2048]{3,2,1,0:T(2,128)} fusion(bf16[8,32,2,2048]{3,2,1,0:T(2,128)(2,1)S(1)} %copy-done, bf16[8,47,2,2048]{3,2,1,0:T(2,128)(2,1)S(1)} %constant_dynamic-update-slice_fusion, f32[2048]{0:T(1024)S(1)} %get-tuple-element.16, f32[2048]{0:T(1024)S(1)} %get-tuple-element.17, f32[2048]{0:T(1024)S(1)} %get-tuple-element.18, ...), kind=kLoop, calls=%fused_computation.12 | loop fusion | flops 49283072 | bytes 37879808 | tf_op jit(solution)/shard_map/add | solution.py:69
  63.4 6.5 %reshape.326 = f32[8,32,2,16,128,1]{4,3,2,1,0,5:T(8,128)} reshape(f32[8,32,2,2048]{3,2,1,0:T(2,128)} %multiply_add_fusion) | data formatting | bytes 8388608 | tf_op jit(solution)/shard_map/reshape | solution.py:70
  69.9 4.1 %convolution_bitcast_fusion = f32[8,32,2,16,128]{4,3,1,0,2:T(8,128)S(1)} fusion(f32[8,32,2,16,128,1]{4,3,2,1,0,5:T(8,128)} %reshape.326, f32[1,16,2,16]{1,3,0,2:T(8,128)S(1)} %get-tuple-element.34, f32[1,16,2,16]{1,3,0,2:T(8,128)S(1)} %get-tuple-element.33), kind=kOutput, calls=%fused_computation.14 | convolution fusion | flops 201327616 | bytes 8392704 | tf_op jit(solution)/shard_map/ifsmn,smtk->iftkn/dot_general | solution.py:41
  74.0 0.6 multiply_add_fusion.1
  74.6 0.4 pad_maximum_fusion.1
  75.0 3.0 fusion.7
  78.0 2.1 fusion.11
  80.1 8.5 %copy.25 = f32[8,32,128,16]{1,0,3,2:T(8,128)} copy(f32[8,32,128,16]{2,1,3,0:T(8,128)} %get-tuple-element.11) | data formatting | bytes 4194304 | tf_op jit(solution)/shard_map/transpose | solution.py:76
  88.6 7.5 %copy.27 = f32[8,32,128,16]{1,0,3,2:T(8,128)} copy(f32[8,32,128,16]{2,1,3,0:T(8,128)S(1)} %get-tuple-element.12) | data formatting | bytes 4194304 | tf_op jit(solution)/shard_map/transpose | solution.py:77
  96.1 9.2 %subtract_convert_fusion = (bf16[8,32,64,8,1,4]{1,0,5,3,2,4:T(8,128)(2,1)S(1)}, bf16[8,32,64,8,1,4]{1,0,5,3,2,4:T(8,128)(2,1)}) fusion(f32[8,32,64,8,1,4]{1,0,5,3,2,4:T(8,128)} %bitcast.88, f32[8,32,64,8,1,4]{1,0,5,3,2,4:T(8,128)} %bitcast.87, f32[8,64,8,4]{0,3,2,1:T(4,128)} %bitcast.95, f32[8,64,8,4]{0,3,2,1:T(4,128)S(1)} %bitcast.94), kind=kLoop, calls=%fused_computation.6 | loop fusion | flops 4194304 | bytes 6422528 | tf_op jit(solution)/shard_map/convert_element_type | solution.py:80
  105.3 7.3 %pad_maximum_fusion = bf16[8,32,64,8,2,4]{1,0,5,3,2,4:T(8,128)(2,1)} fusion(bf16[8,32,64,8,1,4]{1,0,5,3,2,4:T(8,128)(2,1)} %get-tuple-element.6, bf16[8,32,64,8,1,4]{1,0,5,3,2,4:T(8,128)(2,1)S(1)} %get-tuple-element.5), kind=kLoop, calls=%fused_computation | loop fusion | flops 1048576 | bytes 4194304 | tf_op jit(solution)/shard_map/stack | solution.py:82
  112.6 9.2 %copy.29 = bf16[8,32,64,8,2,4]{1,0,5,4,3,2:T(8,128)(2,1)} copy(bf16[8,32,64,8,2,4]{1,0,5,3,2,4:T(8,128)(2,1)} %pad_maximum_fusion) | data formatting | bytes 4194304 | tf_op jit(solution)/shard_map/stack | solution.py:82
  121.8 12.2 %reshape.335 = bf16[64,2,8192]{2,1,0:T(2,128)(2,1)S(1)} reshape(bf16[4096,8,32]{2,1,0:T(8,128)(2,1)} %bitcast.89) | data formatting | bytes 4194304
  134.0 63.5 %all_to_all.15 = bf16[64,2,8192]{2,1,0:T(2,128)(2,1)} all-to-all(bf16[64,2,8192]{2,1,0:T(2,128)(2,1)S(1)} %reshape.335), channel_id=1, replica_groups=mesh['stn'=64,'tm'=8] {'stn'}, dimensions={0} | all-to-all | bytes 4194304 | tf_op jit(solution)/shard_map/all_to_all | solution.py:91
  197.6 11.7 %reshape.336 = bf16[4096,8,32]{2,1,0:T(8,128)(2,1)} reshape(bf16[64,2,8192]{2,1,0:T(2,128)(2,1)} %all_to_all.15) | data formatting | bytes 4194304
  209.3 9.0 %copy.30 = bf16[8,32,64,64]{1,0,2,3:T(8,128)(2,1)} copy(bf16[8,32,64,64]{1,0,3,2:T(8,128)(2,1)} %bitcast.90) | data formatting | bytes 4194304 | tf_op jit(solution)/shard_map/all_to_all | solution.py:91
  218.3 5.9 %fusion.75 = (bf16[512,32,2,4,1,1,4]{1,0,6,4,3,2,5:T(8,128)(2,1)}, bf16[512,32,2,4,1,1,4]{1,0,6,4,3,2,5:T(8,128)(2,1)}) fusion(bf16[512,32,2,4,2,1,4]{1,0,6,4,3,2,5:T(8,128)(2,1)} %bitcast.91), kind=kLoop, calls=%fused_computation.105 | loop fusion | bytes 4194304 | tf_op jit(solution)/shard_map/slice | solution.py:50
  224.2 3.5 copy.49
  227.6 1.3 neg.63
  228.9 3.5 copy.50
  232.4 10.3 %fusion.14 = f32[512,2,1,1,512]{0,4,1,3,2:T(8,128)S(1)} fusion(bf16[512,32,2,4,2,4]{1,0,5,4,3,2:T(8,128)(2,1)} %bitcast.92), kind=kOutput, calls=%fused_computation.24 | convolution fusion | flops 1073741824 | bytes 4194304 | tf_op jit(solution)/shard_map/nfagrpq,mfagrpq->napm/dot_general | solution.py:55
  242.7 9.3 %fusion.17 = f32[512,2,1,1,512]{0,4,1,3,2:T(8,128)S(1)} fusion(bf16[512,32,2,4,2,4]{1,0,5,4,3,2:T(8,128)(2,1)} %bitcast.93, bf16[512,32,2,4,1,1,4]{0,1,4,2,6,3,5:T(8,128)(2,1)S(1)} %copy.50, bf16[512,32,2,4,1,1,4]{0,1,4,2,6,3,5:T(8,128)(2,1)} %neg.63), kind=kOutput, calls=%fused_computation.25 | convolution fusion | flops 1074790400 | bytes 6291456 | tf_op jit(solution)/shard_map/nfagrpq,mfagrpq->napm/dot_general | solution.py:56
  252.0 2.4 maximum_bitcast_fusion
  254.5 7.3 %copy.36 = f32[512,2,2,512]{3,2,1,0:T(2,128)} copy(f32[512,2,2,512]{0,3,1,2:T(8,128)} %maximum_bitcast_fusion) | data formatting | bytes 8388608 | tf_op jit(solution)/shard_map/reshape | solution.py:58
  261.8 0.0 all-reduce.3.cloned.1.call-update
  261.8 1.3 dynamic-slice
  263.7 114.2 %all-reduce.3.cloned.1.call-done = f32[512,2,2,512]{3,2,1,0:T(2,128)} async-done(((f32[512,2,2,512]{3,2,1,0:T(2,128)}), f32[512,2,2,512]{3,2,1,0:T(2,128)}) %all-reduce.3.cloned.1.call-update) | async-done | bytes 4194320
  378.0 2.1 dynamic-slice_multiply_fusion
  (3 shorter events, 0.0 us)
Async XLA Ops:
  6.5 20.8 %copy-start = (bf16[8,32,2,2048]{3,2,1,0:T(2,128)(2,1)S(1)}, bf16[8,32,2,2048]{3,2,1,0:T(2,128)(2,1)}, u32[]{:S(2)}) copy-start(bf16[8,32,2,2048]{3,2,1,0:T(2,128)(2,1)} %param.2) | copy-start | bytes 6291460
  6.5 371.4 %all-reduce.3.cloned.1.call-start = ((), (), s32[]{:S(2)}) async-start(), calls=%async_computation.1 | async-start | bytes 8388608
  9.5 15.9 %collective-permute-start = (bf16[8,15,2,2048]{3,2,1,0:T(2,128)(2,1)}, bf16[8,15,2,2048]{3,2,1,0:T(2,128)(2,1)}, u32[]{:S(2)}, u32[]{:S(2)}) collective-permute-start(bf16[8,15,2,2048]{3,2,1,0:T(2,128)(2,1)} %slice.138), channel_id=1, source_target_pairs={{0,1},{1,2},{2,3},{3,4},{4,5},{5,6},{6,7},{8,9},{9,10},{10,11},{11... | collective-permute-start | bytes 2949128 | tf_op jit(solution)/shard_map/ppermute | solution.py:16
Sparse Core Ops, SparseCore 0:
  261.9 115.9 all-reduce.2
where the time goes:
time: 389 us; the launch traced here: 387 us
  waiting for transfers between devices  122 us (31%)
  local copies, waits for them, and re-layouts  95.5 us (25%)
  blocking collectives  63.5 us (16%)
  other arithmetic  60.7 us (16%)
  matrix products  26.7 us (7%)
  between operations  14.2 us (4%)
  starting transfers between devices  4.59 us (1%)
    unnamed x2, waiting for transfers between devices  114 us
    all_to_all x1, blocking collectives, on_device(): lax.all_to_all(spectra, 'stn', split_axis=2, concat_axis=0, tiled=True)  63.5 us
    unnamed x8, local copies, waits for them, and re-layouts  34.1 us
    add x1, other arithmetic, on_device(): filtered + extended[:, t:t + frames_dev].astype(jnp.float32) * window[t]  34 us
    dot_general x1, matrix products, gram_rows(): jnp.einsum(pattern, row_part, columns, preferred_element_type=jnp.float32)  10.3 us
    dot_general x1, matrix products, gram_rows(): jnp.einsum(pattern, row_part, rotated, preferred_element_type=jnp.float32)  9.3 us
    convert_element_type x1, other arithmetic, on_device(): (natural_real * gain_real - natural_imag * gain_imag).astype(jnp.bfloat16)  9.19 us
    another operation x1, local copies, waits for them, and re-layouts, on_device(): jnp.stack([equal_real, equal_imag], axis=4)  9.19 us
  transfers between devices with their start and end apart: 2, of which 2 were waited for; matrix products, arithmetic and copies ran while one was open for 1% of the time, Pallas kernels for 0%

commit v1 on v0

v1 whole, which is shorter than its diff:
```python
import functools

import jax
import jax.numpy as jnp
import ml_dtypes
import numpy as np
from jax import lax
from jax.experimental import pallas as pl
from jax.experimental.pallas import tpu as pltpu
from jax.sharding import Mesh, PartitionSpec as P

CHANNELS = 2048
TAPS = 16
AVG = 16
RADIX = 16
LANES = 128
HALF = 16
INPUTS_DEV = 8
STATIONS = 64
CHIPS = 4
MIB = 1024 * 1024
BF16 = jnp.bfloat16
F32 = jnp.float32


def window_table():
    position = np.arange(TAPS * CHANNELS, dtype=np.float64) + 0.5
    shape_part = np.sinc((position - TAPS * CHANNELS / 2) / CHANNELS)
    taper = np.sin(np.pi * position / (TAPS * CHANNELS)) ** 2
    table = (shape_part * taper).reshape(TAPS, 1, CHANNELS).astype(np.float32)
    return np.ascontiguousarray(np.broadcast_to(table, (TAPS, 8, CHANNELS)))


def twist_table():
    k1 = np.arange(RADIX)[:, None]
    n2 = np.arange(LANES)[None, :]
    angle = 2.0 * np.pi * ((k1 * n2) % CHANNELS) / CHANNELS
    table = np.stack([np.cos(angle), -np.sin(angle)], axis=1).astype(np.float32)
    return np.ascontiguousarray(np.broadcast_to(table[:, :, None, :], (RADIX, 2, 8, LANES)))


def section_tables():
    n2 = np.arange(LANES)[:, None]
    k2 = np.arange(LANES)[None, :]
    angle = 2.0 * np.pi * ((n2 * k2) % LANES) / LANES
    cosine, sine = np.cos(angle), np.sin(angle)
    full = np.block([[cosine, -sine], [sine, cosine]]) * CHANNELS**-0.5
    full = full.astype(np.float32)
    high = full.astype(ml_dtypes.bfloat16)
    low = (full - high.astype(np.float32)).astype(ml_dtypes.bfloat16)
    return np.stack([high, low])


def order_tables():
    turn = np.zeros((256, 256), np.float32)
    mix = np.zeros((256, 256), np.float32)
    for c in range(2):
        for k2 in range(LANES):
            turn[2 * k2 + c, c * LANES + k2] = 1.0
    for i in range(INPUTS_DEV):
        for q in range(32):
            mix[q * INPUTS_DEV + i, i * 32 + q] = 1.0
    return np.stack([turn, mix]).astype(ml_dtypes.bfloat16)


def radix4(values):
    (ar, ai), (br, bi), (cr, ci), (dr, di) = values
    pr, pi, mr, mi = ar + cr, ai + ci, ar - cr, ai - ci
    qr, qi, nr, ni = br + dr, bi + di, br - dr, bi - di
    return [(pr + qr, pi + qi), (mr + ni, mi - nr), (pr - qr, pi - qi), (mr - ni, mi + nr)]


def radix16(values):
    table = [[None] * 4 for _ in range(4)]
    for b in range(4):
        for c, (re, im) in enumerate(radix4([values[4 * a + b] for a in range(4)])):
            turn = b * c
            if turn == 0:
                table[b][c] = (re, im)
            elif turn == 4:
                table[b][c] = (im, -re)
            elif turn == 2:
                root = np.float32(np.sqrt(0.5))
                table[b][c] = ((re + im) * root, (im - re) * root)
            elif turn == 6:
                root = np.float32(np.sqrt(0.5))
                table[b][c] = ((im - re) * root, -(re + im) * root)
            else:
                cosine = np.float32(np.cos(2.0 * np.pi * turn / 16))
                sine = np.float32(np.sin(2.0 * np.pi * turn / 16))
                table[b][c] = (re * cosine + im * sine, im * cosine - re * sine)
    result = [None] * 16
    for c in range(4):
        for d, pair in enumerate(radix4([table[b][c] for b in range(4)])):
            result[c + 4 * d] = pair
    return result


def front_kernel(
    hist_ref, cur_ref, gain_ref, window_ref, twist_ref, section_ref, order_ref, *refs
):
    out_ref, ext, filtered, stage, equal, turned = refs[-6:]
    i = pl.program_id(0)
    for n1 in range(RADIX):
        lanes = slice(n1 * LANES, (n1 + 1) * LANES)
        for c in range(2):
            ext[n1, c, 0:HALF, :] = hist_ref[c, 0, :, lanes].astype(F32)
            ext[n1, c, HALF : 2 * HALF, :] = cur_ref[c, 0, :, lanes].astype(F32)
    for n1 in range(RADIX):
        lanes = slice(n1 * LANES, (n1 + 1) * LANES)
        sums = [None] * 4
        for t in range(TAPS):
            weight = window_ref[t, :, lanes]
            for c in range(2):
                for block in range(2):
                    begin = block * 8 + 1 + t
                    term = ext[n1, c, begin : begin + 8, :] * weight
                    slot = 2 * c + block
                    sums[slot] = term if sums[slot] is None else sums[slot] + term
        for c in range(2):
            for block in range(2):
                filtered[block, n1, c] = sums[2 * c + block]
    for block in range(2):
        values = [(filtered[block, n1, 0], filtered[block, n1, 1]) for n1 in range(RADIX)]
        for k1, (re, im) in enumerate(radix16(values)):
            cosine, sine = twist_ref[k1, 0], twist_ref[k1, 1]
            rows = slice(k1 * HALF + block * 8, k1 * HALF + block * 8 + 8)
            stage[rows, 0:LANES] = re * cosine - im * sine
            stage[rows, LANES : 2 * LANES] = re * sine + im * cosine
    whole = stage[...]
    high = whole.astype(BF16)
    low = (whole - high.astype(F32)).astype(BF16)
    dot = functools.partial(jnp.dot, preferred_element_type=F32)
    stage[...] = (
        dot(high, section_ref[0]) + dot(high, section_ref[1]) + dot(low, section_ref[0])
    )
    for k1 in range(RADIX):
        rows = slice(k1 * HALF, (k1 + 1) * HALF)
        re, im = stage[rows, 0:LANES], stage[rows, LANES : 2 * LANES]
        gain_re, gain_im = gain_ref[0, k1, 0:1, :], gain_ref[0, k1, 1:2, :]
        equal[rows, 0:LANES] = (re * gain_re - im * gain_im).astype(BF16)
        equal[rows, LANES : 2 * LANES] = (re * gain_im + im * gain_re).astype(BF16)
    turned[i] = lax.dot_general(
        order_ref[0], equal[...], (((1,), (1,)), ((), ())), preferred_element_type=F32
    ).astype(BF16)

    @pl.when(i == INPUTS_DEV - 1)
    def _():
        for group in range(8):
            piece = turned[:, group * 32 : (group + 1) * 32, :].reshape(256, 256)
            mixed = dot(order_ref[1], piece).astype(BF16)
            rows = slice(group * 16, (group + 1) * 16)
            for h in range(2):
                out_ref[rows, h, 0] = mixed[:, h * LANES : (h + 1) * LANES].reshape(16, 16, LANES)


def front(history, current, current_block, gains, tables, half, earlier):
    window, twist, section, order = tables
    out_shape = (LANES, 2, 2, 16, LANES)

    def frames(array, block):
        return pl.BlockSpec((2, 1, HALF, CHANNELS), lambda i: (0, i, block, 0))

    def fixed(array):
        return pl.BlockSpec(array.shape, lambda i: (0,) * array.ndim)

    in_specs = [
        frames(history, 0),
        frames(current, current_block),
        pl.BlockSpec((1, RADIX, 2, LANES), lambda i: (i, 0, 0, 0)),
        fixed(window),
        fixed(twist),
        fixed(section),
        fixed(order),
    ]
    operands = [history, current, gains, window, twist, section, order]
    aliases = {}
    if earlier is not None:
        in_specs.append(pl.BlockSpec(memory_space=pl.ANY))
        operands.append(earlier)
        aliases = {7: 0}
    return pl.pallas_call(
        front_kernel,
        grid=(INPUTS_DEV,),
        in_specs=in_specs,
        out_specs=pl.BlockSpec((LANES, 2, 1, 16, LANES), lambda i: (0, 0, half, 0, 0)),
        out_shape=jax.ShapeDtypeStruct(out_shape, BF16),
        scratch_shapes=[
            pltpu.VMEM((RADIX, 2, 2 * HALF, LANES), F32),
            pltpu.VMEM((2, RADIX, 2, 8, LANES), F32),
            pltpu.VMEM((256, 256), F32),
            pltpu.VMEM((256, 256), BF16),
            pltpu.VMEM((INPUTS_DEV, 256, 256), BF16),
        ],
        input_output_aliases=aliases,
        compiler_params=pltpu.CompilerParams(vmem_limit_bytes=32 * MIB),
        cost_estimate=pl.CostEstimate(
            flops=1400000000, bytes_accessed=6 * MIB, transcendentals=0
        ),
    )(*operands)


def gram_kernel(place_ref, spectra_ref, keep_ref, send_ref, parts):
    chip, core = place_ref[0], place_ref[1]
    depth = CHIPS * 2 * LANES
    for l in range(CHIPS):
        for half in range(2):
            slab = spectra_ref[:, l, half].astype(F32).reshape(STATIONS, 2, 8, LANES)
            begin = (l * 2 + half) * LANES
            for c in range(2):
                parts[c, :, begin : begin + LANES] = (
                    slab[:, c].reshape(STATIONS * 8, LANES).astype(BF16)
                )
    scale = 1.0 / 4096.0

    def product(a, b):
        return lax.dot_general(a, b, (((1,), (1,)), ((), ())), preferred_element_type=F32)

    for block in range(CHIPS):
        rows = slice(block * 128, (block + 1) * 128)
        re = (product(parts[0, rows], parts[0]) + product(parts[1, rows], parts[1])) * scale
        im = (product(parts[1, rows], parts[0]) - product(parts[0, rows], parts[1])) * scale
        other = jnp.bitwise_xor(chip, block)
        slot = 2 * jnp.bitwise_and(other, 1) + jnp.right_shift(other, 1)
        for c in range(2):
            part = slice(c * 64, (c + 1) * 64)

            @pl.when(core == c)
            def _():
                keep_ref[slot, 0] = re[part]
                keep_ref[slot, 1] = im[part]

            @pl.when(core != c)
            def _():
                send_ref[slot, 0] = re[part]
                send_ref[slot, 1] = im[part]


def gram(spectra):
    place = jnp.stack([lax.axis_index("l"), lax.axis_index("c")]).astype(jnp.int32)
    shape = jax.ShapeDtypeStruct((CHIPS, 2, 64, 512), F32)
    return pl.pallas_call(
        gram_kernel,
        in_specs=[
            pl.BlockSpec(memory_space=pltpu.SMEM),
            pl.BlockSpec(memory_space=pltpu.VMEM),
        ],
        out_specs=[pl.BlockSpec(memory_space=pltpu.VMEM)] * 2,
        out_shape=[shape, shape],
        scratch_shapes=[pltpu.VMEM((2, 512, CHIPS * 2 * LANES), BF16)],
        compiler_params=pltpu.CompilerParams(vmem_limit_bytes=32 * MIB),
        cost_estimate=pl.CostEstimate(
            flops=2200000000, bytes_accessed=4 * MIB, transcendentals=0
        ),
    )(place, spectra)


def on_device(voltages, gains):
    tables = (
        jnp.asarray(window_table()),
        jnp.asarray(twist_table()),
        jnp.asarray(section_tables()),
        jnp.asarray(order_tables()),
    )
    split = jnp.transpose(voltages, (2, 0, 1, 3))
    last = split[:, :, HALF:]
    forward = [(t, t + 1) for t in range(2 * CHIPS - 1)]
    history = lax.ppermute(last, ("l", "c"), forward)
    weights = jnp.transpose(gains.reshape(2, INPUTS_DEV, LANES, RADIX), (1, 3, 0, 2))
    ready = front(split, split, 1, weights, tables, 1, None)
    ready = front(history, split, 0, weights, tables, 0, ready)
    chunks = ready.reshape(4 * STATIONS, 2, 16, LANES)
    arrived = lax.all_to_all(chunks, ("z", "h", "x", "l"), 0, 0, tiled=True)
    keep, send = gram(arrived.reshape(STATIONS, CHIPS, 2, 16, LANES))
    total = keep + lax.ppermute(send, "c", [(0, 1), (1, 0)])
    total = total[:2] + lax.ppermute(total[2:], "l", [(l, l ^ 1) for l in range(CHIPS)])
    own = total[0]
    other = lax.ppermute(total[1], "l", [(l, l ^ 2) for l in range(CHIPS)])
    first = lax.axis_index("l") < 2
    both = jnp.stack([jnp.where(first, own, other), jnp.where(first, other, own)])
    return jnp.transpose(both, (2, 0, 1, 3))


def solution(mesh):
    fine = Mesh(mesh.devices.reshape(8, 2, 4, CHIPS, 2), ("z", "h", "x", "l", "c"))
    station, time = ("z", "h", "x"), ("l", "c")
    return jax.shard_map(
        on_device,
        mesh=fine,
        in_specs=(P(station, time, None, None), P(None, station, None)),
        out_specs=P(time, station, None, None),
        check_vma=False,
    )
```

time: 389 us -> 151 us (0.39)
  local copies, waits for them, and re-layouts: 95.5 us -> 10.8 us
  blocking collectives: 63.5 us -> 0 us
  other arithmetic: 60.7 us -> 0.45 us
  waiting for transfers between devices: 122 us -> 76.5 us
  starting transfers between devices: 4.59 us -> 39.2 us
  matrix products: 26.7 us -> 0 us
  Pallas kernels: 0 us -> 23 us
  between operations: 14.2 us -> 0.18 us
    unnamed x2 -> x0, waiting for transfers between devices: 114 us -> none
    all_to_all x1 -> x0, blocking collectives: 63.5 us -> none  [on_device(): lax.all_to_all(spectra, 'stn', split_axis=2, concat_axis=0, tiled=True)]
    all_to_all x0 -> x1, waiting for transfers between devices: none -> 49.8 us  [on_device(): arrived = lax.all_to_all(chunks, ('z', 'h', 'x', 'l'), 0, 0, tiled=True)]
    add x2, other arithmetic: 34.6 us -> 0.29 us  [the longest x1 0.21 us: on_device(): total = keep + lax.ppermute(send, 'c', [(0, 1), (1, 0)])]
    unnamed x8 -> x13, local copies, waits for them, and re-layouts: 34.1 us -> 5.66 us
    dot_general x4 -> x0, matrix products: 26.7 us -> none  [the longest x1 10.3 us: gram_rows(): jnp.einsum(pattern, row_part, columns, preferred_element_type=jnp.float32)]
    pallas_call x0 -> x3, Pallas kernels: none -> 23 us  [the longest x2 16.3 us: front(): pl.pallas_call(front_kernel, grid=(INPUTS_DEV,), in_specs=in_specs, out_s...]
    all_to_all x0 -> x1, starting transfers between devices: none -> 21.5 us  [on_device(): arrived = lax.all_to_all(chunks, ('z', 'h', 'x', 'l'), 0, 0, tiled=True)]
  transfers between devices with their start and end apart: 2 -> 5, of which waited for: 2 -> 4; matrix products, arithmetic and copies ran while one was open for 1% -> 2% of each run, Pallas kernels for 0% -> 5%
where the time goes in v1:
time: 151 us; the launch traced here: 150 us
  waiting for transfers between devices  76.5 us (51%)
  starting transfers between devices  39.2 us (26%)
  Pallas kernels  23 us (15%)
  local copies, waits for them, and re-layouts  10.8 us (7%)
    all_to_all x1, waiting for transfers between devices, on_device(): arrived = lax.all_to_all(chunks, ('z', 'h', 'x', 'l'), 0, 0, tiled=True)  49.8 us
    all_to_all x1, starting transfers between devices, on_device(): arrived = lax.all_to_all(chunks, ('z', 'h', 'x', 'l'), 0, 0, tiled=True)  21.5 us
    pallas_call x2, Pallas kernels, front(): pl.pallas_call(front_kernel, grid=(INPUTS_DEV,), in_specs=in_specs, out_s...  16.3 us
    ppermute x1, waiting for transfers between devices, on_device(): other = lax.ppermute(total[1], 'l', [(l, l ^ 2) for l in range(CHIPS)])  12.4 us
    ppermute x1, waiting for transfers between devices, on_device(): lax.ppermute(total[2:], 'l', [(l, l ^ 1) for l in range(CHIPS)])  12 us
    pallas_call x1, Pallas kernels, gram(): pl.pallas_call(gram_kernel, in_specs=[pl.BlockSpec(memory_space=pltpu.SME...  6.69 us
    ppermute x1, starting transfers between devices, on_device(): total = keep + lax.ppermute(send, 'c', [(0, 1), (1, 0)])  5.78 us
    unnamed x13, local copies, waits for them, and re-layouts  5.66 us
  transfers between devices with their start and end apart: 5, of which 4 were waited for; matrix products, arithmetic and copies ran while one was open for 2% of the time, Pallas kernels for 5%

profile of v1, /device:TPU:1, one launch (start us, length us, event | category | flops | bytes accessed | tf_op | source)
XLA Modules:
  0.0 150.1 jit_solution(7333394966176648490)
XLA Ops:
  0.0 2.5 %copy.14 = bf16[8,32,2,2048]{3,1,0,2:T(8,128)(2,1)S(1)} copy(bf16[8,32,2,2048]{3,2,1,0:T(2,128)(2,1)} %param.6) | data formatting | bytes 4194304 | tf_op args[0]
  2.5 0.0 copy-start.5
  2.5 0.0 copy-start.1
  2.5 0.0 copy-start.2
  2.5 1.0 slice.20
  3.6 4.6 %collective-permute-start = (bf16[2,8,16,2048]{3,2,1,0:T(8,128)(2,1)}, bf16[2,8,16,2048]{3,2,1,0:T(8,128)(2,1)}, u32[]{:S(2)}, u32[]{:S(2)}) collective-permute-start(bf16[2,8,16,2048]{3,2,1,0:T(8,128)(2,1)} %slice.20), channel_id=1, source_target_pairs={{0,1},{1,2},{2,3},{3,4},{4,5},{5,6},{6,7},{8,9},{9,10},{10,11},{11... | collective-permute-start | bytes 3145736 | tf_op jit(solution)/shard_map/ppermute | solution.py:268
  8.1 0.0 copy-done.5
  8.2 1.3 reshape.9
  9.5 1.5 %copy.11 = f32[2,8,128,16]{2,0,3,1:T(2,128)S(1)} copy(f32[2,8,128,16]{3,2,1,0:T(8,128)} %reshape.9) | data formatting | bytes 262144 | tf_op jit(solution)/shard_map/reshape | solution.py:269
  11.0 0.0 copy-done.1
  11.0 0.0 copy-done.2
  11.0 0.0 copy-start.3
  11.1 0.9 copy-done.3
  12.0 0.0 copy-start.4
  12.0 0.9 copy-done.4
  12.9 7.7 %shard_map.64.refs_0_ = bf16[128,2,2,16,128]{4,3,2,1,0:T(8,128)(2,1)S(1)} custom-call(bf16[2,8,32,2048]{3,2,1,0:T(8,128)(2,1)S(1)} %bitcast.23, bf16[2,8,32,2048]{3,2,1,0:T(8,128)(2,1)S(1)} %bitcast.24, f32[8,16,2,128]{3,2,1,0:T(2,128)S(1)} %bitcast.28, f32[16,8,2048]{2,1,0:T(8,128)S(1)} %copy-done.1, f32[16,2,8,128]{3,2,1,0:T(8,128)S(1)} %copy-done.4, ...), custom_call_target="tpu_custom_call" | custom-call | flops 1400000000 | bytes 6291456 | tf_op jit(solution)/shard_map/pallas_call | solution.py:182
  20.6 0.0 collective-permute-done.hist_ref
  20.6 8.6 %shard_map.65 = bf16[128,2,2,16,128]{4,3,2,1,0:T(8,128)(2,1)S(1)} custom-call(bf16[2,8,16,2048]{3,2,1,0:T(8,128)(2,1)} %collective-permute-done.hist_ref, bf16[2,8,32,2048]{3,2,1,0:T(8,128)(2,1)S(1)} %bitcast.25, f32[8,16,2,128]{3,2,1,0:T(2,128)S(1)} %bitcast.29, f32[16,8,2048]{2,1,0:T(8,128)S(1)} %copy-done.1, ...), custom_call_target="tpu_custom_call", output_to_operand_aliasing={{}: (7, {})} | custom-call | flops 1400000000 | bytes 6291456 | tf_op jit(solution)/shard_map/pallas_call | solution.py:182
  29.2 0.0 copy-start
  29.2 1.3 copy-done
  30.5 21.5 %all-to-all-start = ((bf16[256,2,16,128]{3,2,1,0:T(8,128)(2,1)}), bf16[256,2,16,128]{3,2,1,0:T(8,128)(2,1)S(1)}, u32[]{:S(2)}, u32[]{:S(2)}) async-start(bf16[256,2,16,128]{3,2,1,0:T(8,128)(2,1)} %bitcast.26), calls=%async_computation | async-start | bytes 4194304 | tf_op jit(solution)/shard_map/all_to_all | solution.py:273
  52.0 0.1 pad_add_fusion.place_ref
  52.1 49.8 %all-to-all-done = bf16[256,2,16,128]{3,2,1,0:T(8,128)(2,1)S(1)} async-done(((bf16[256,2,16,128]{3,2,1,0:T(8,128)(2,1)}), bf16[256,2,16,128]{3,2,1,0:T(8,128)(2,1)S(1)}, u32[]{:S(2)}, u32[]{:S(2)}) %all-to-all-start) | async-done | bytes 2097184 | tf_op jit(solution)/shard_map/all_to_all | solution.py:273
  101.9 6.7 %shard_map.66 = (f32[4,2,64,512]{3,2,1,0:T(8,128)S(1)}, f32[4,2,64,512]{3,2,1,0:T(8,128)S(1)}) custom-call(s32[2]{0:T(128)S(1)} %pad_add_fusion.place_ref, bf16[64,4,2,16,128]{4,3,2,1,0:T(8,128)(2,1)S(1)} %bitcast.27), custom_call_target="tpu_custom_call" | custom-call | flops 2200000000 | bytes 4194304 | tf_op jit(solution)/shard_map/pallas_call | solution.py:242
  108.6 5.8 %collective-permute-start.1 = (f32[4,2,64,512]{3,2,1,0:T(8,128)S(1)}, f32[4,2,64,512]{3,2,1,0:T(8,128)S(1)}, u32[]{:S(2)}, u32[]{:S(2)}) collective-permute-start(f32[4,2,64,512]{3,2,1,0:T(8,128)S(1)} %get-tuple-element.8), channel_id=1, source_target_pairs={{0,1},{1,0},{2,3},{3,2},{4,5},{5,4},{6,7},{7,6},{8,9},{9,8},{10,11... | collective-permute-start | bytes 3145736 | tf_op jit(solution)/shard_map/ppermute | solution.py:275
  114.4 2.3 %collective-permute-done.1 = f32[4,2,64,512]{3,2,1,0:T(8,128)S(1)} collective-permute-done((f32[4,2,64,512]{3,2,1,0:T(8,128)S(1)}, f32[4,2,64,512]{3,2,1,0:T(8,128)S(1)}, u32[]{:S(2)}, u32[]{:S(2)}) %collective-permute-start.1) | collective-permute-done | bytes 1048608 | tf_op jit(solution)/shard_map/ppermute | solution.py:275
  116.7 0.2 add.6
  116.9 4.0 %collective-permute-start.2 = (f32[2,2,64,512]{3,2,1,0:T(8,128)S(1)}, f32[2,2,64,512]{3,2,1,0:T(8,128)S(1)}, u32[]{:S(2)}, u32[]{:S(2)}) collective-permute-start(f32[2,2,64,512]{3,2,1,0:T(8,128)S(1)} %slice.22), channel_id=1, source_target_pairs={{0,2},{2,0},{4,6},{6,4},{1,3},{3,1},{5,7},{7,5},{8,10},{10,8},{12,... | collective-permute-start | bytes 1572872 | tf_op jit(solution)/shard_map/ppermute | solution.py:276
  120.9 12.0 %collective-permute-done.2 = f32[2,2,64,512]{3,2,1,0:T(8,128)S(1)} collective-permute-done((f32[2,2,64,512]{3,2,1,0:T(8,128)S(1)}, f32[2,2,64,512]{3,2,1,0:T(8,128)S(1)}, u32[]{:S(2)}, u32[]{:S(2)}) %collective-permute-start.2) | collective-permute-done | bytes 524320 | tf_op jit(solution)/shard_map/ppermute | solution.py:276
  132.9 0.1 slice_add_fusion
  133.0 3.3 %collective-permute-start.3 = (f32[2,64,512]{2,1,0:T(8,128)S(1)}, f32[2,64,512]{2,1,0:T(8,128)S(1)}, u32[]{:S(2)}, u32[]{:S(2)}) collective-permute-start(f32[2,64,512]{2,1,0:T(8,128)S(1)} %slice_bitcast_fusion), channel_id=1, source_target_pairs={{0,4},{2,6},{4,0},{6,2},{1,5},{3,7},{5,1},{7,3},{8,12},{10,14},{12... | collective-permute-start | bytes 786440 | tf_op jit(solution)/shard_map/ppermute | solution.py:278
  136.4 12.4 %collective-permute-done.3 = f32[2,64,512]{2,1,0:T(8,128)S(1)} collective-permute-done((f32[2,64,512]{2,1,0:T(8,128)S(1)}, f32[2,64,512]{2,1,0:T(8,128)S(1)}, u32[]{:S(2)}, u32[]{:S(2)}) %collective-permute-start.3) | collective-permute-done | bytes 262176 | tf_op jit(solution)/shard_map/ppermute | solution.py:278
  148.9 1.2 copy.12
  (4 shorter events, 0.1 us)
Async XLA Ops:
  2.5 5.7 %copy-start.5 = (f32[2,8,2048]{2,1,0:T(8,128)S(1)}, f32[2,8,2048]{2,1,0:T(8,128)}, u32[]{:S(2)}) copy-start(f32[2,8,2048]{2,1,0:T(8,128)} %param.7) | copy-start | bytes 393220
  2.5 8.5 %copy-start.1 = (f32[16,8,2048]{2,1,0:T(8,128)S(1)}, f32[16,8,2048]{2,1,0:T(8,128)}, u32[]{:S(2)}) copy-start(f32[16,8,2048]{2,1,0:T(8,128)} %constant.18.clone.window_ref) | copy-start | bytes 3145732
  2.5 8.5 %copy-start.2 = (bf16[2,256,256]{2,1,0:T(8,128)(2,1)S(1)}, bf16[2,256,256]{2,1,0:T(8,128)(2,1)}, u32[]{:S(2)}) copy-start(bf16[2,256,256]{2,1,0:T(8,128)(2,1)} %constant.20.clone.section_ref) | copy-start | bytes 786436
  3.6 17.1 %collective-permute-start = (bf16[2,8,16,2048]{3,2,1,0:T(8,128)(2,1)}, bf16[2,8,16,2048]{3,2,1,0:T(8,128)(2,1)}, u32[]{:S(2)}, u32[]{:S(2)}) collective-permute-start(bf16[2,8,16,2048]{3,2,1,0:T(8,128)(2,1)} %slice.20), channel_id=1, source_target_pairs={{0,1},{1,2},{2,3},{3,4},{4,5},{5,6},{6,7},{8,9},{9,10},{10,11},{11... | collective-permute-start | bytes 3145736 | tf_op jit(solution)/shard_map/ppermute | solution.py:268
  11.0 1.0 copy-start.3
  12.0 0.9 copy-start.4
  29.2 1.3 copy-start
  30.5 71.4 %all-to-all-start = ((bf16[256,2,16,128]{3,2,1,0:T(8,128)(2,1)}), bf16[256,2,16,128]{3,2,1,0:T(8,128)(2,1)S(1)}, u32[]{:S(2)}, u32[]{:S(2)}) async-start(bf16[256,2,16,128]{3,2,1,0:T(8,128)(2,1)} %bitcast.26), calls=%async_computation | async-start | bytes 4194304 | tf_op jit(solution)/shard_map/all_to_all | solution.py:273
  108.6 8.0 %collective-permute-start.1 = (f32[4,2,64,512]{3,2,1,0:T(8,128)S(1)}, f32[4,2,64,512]{3,2,1,0:T(8,128)S(1)}, u32[]{:S(2)}, u32[]{:S(2)}) collective-permute-start(f32[4,2,64,512]{3,2,1,0:T(8,128)S(1)} %get-tuple-element.8), channel_id=1, source_target_pairs={{0,1},{1,0},{2,3},{3,2},{4,5},{5,4},{6,7},{7,6},{8,9},{9,8},{10,11... | collective-permute-start | bytes 3145736 | tf_op jit(solution)/shard_map/ppermute | solution.py:275
  116.9 16.0 %collective-permute-start.2 = (f32[2,2,64,512]{3,2,1,0:T(8,128)S(1)}, f32[2,2,64,512]{3,2,1,0:T(8,128)S(1)}, u32[]{:S(2)}, u32[]{:S(2)}) collective-permute-start(f32[2,2,64,512]{3,2,1,0:T(8,128)S(1)} %slice.22), channel_id=1, source_target_pairs={{0,2},{2,0},{4,6},{6,4},{1,3},{3,1},{5,7},{7,5},{8,10},{10,8},{12,... | collective-permute-start | bytes 1572872 | tf_op jit(solution)/shard_map/ppermute | solution.py:276
  133.0 15.7 %collective-permute-start.3 = (f32[2,64,512]{2,1,0:T(8,128)S(1)}, f32[2,64,512]{2,1,0:T(8,128)S(1)}, u32[]{:S(2)}, u32[]{:S(2)}) collective-permute-start(f32[2,64,512]{2,1,0:T(8,128)S(1)} %slice_bitcast_fusion), channel_id=1, source_target_pairs={{0,4},{2,6},{4,0},{6,2},{1,5},{3,7},{5,1},{7,3},{8,12},{10,14},{12... | collective-permute-start | bytes 786440 | tf_op jit(solution)/shard_map/ppermute | solution.py:278

commit v2 on v1

v2 whole, which is shorter than its diff:
```python
import functools

import jax
import jax.numpy as jnp
import ml_dtypes
import numpy as np
from jax import lax
from jax.experimental import pallas as pl
from jax.experimental.pallas import tpu as pltpu
from jax.sharding import Mesh, PartitionSpec as P

CHANNELS = 2048
TAPS = 16
AVG = 16
RADIX = 16
LANES = 128
HALF = 16
INPUTS_DEV = 8
STATIONS = 64
CHIPS = 4
MIB = 1024 * 1024
BF16 = jnp.bfloat16
F32 = jnp.float32


def vector_table():
    position = np.arange(TAPS * CHANNELS, dtype=np.float64) + 0.5
    shape_part = np.sinc((position - TAPS * CHANNELS / 2) / CHANNELS)
    taper = np.sin(np.pi * position / (TAPS * CHANNELS)) ** 2
    window = (shape_part * taper).reshape(TAPS, CHANNELS)
    k1 = np.arange(RADIX)[:, None]
    n2 = np.arange(LANES)[None, :]
    angle = 2.0 * np.pi * ((k1 * n2) % CHANNELS) / CHANNELS
    return np.concatenate([window, np.cos(angle), -np.sin(angle)], axis=1).astype(np.float32)


def matrix_table():
    n2 = np.arange(LANES)[:, None]
    k2 = np.arange(LANES)[None, :]
    angle = 2.0 * np.pi * ((n2 * k2) % LANES) / LANES
    cosine, sine = np.cos(angle), np.sin(angle)
    full = np.block([[cosine, -sine], [sine, cosine]]) * CHANNELS**-0.5
    full = full.astype(np.float32)
    high = full.astype(ml_dtypes.bfloat16)
    low = (full - high.astype(np.float32)).astype(ml_dtypes.bfloat16)
    turn = np.zeros((256, 256), np.float32)
    mix = np.zeros((256, 256), np.float32)
    comb = np.zeros((256, 256), np.float32)
    for c in range(2):
        for k2 in range(LANES):
            turn[2 * k2 + c, c * LANES + k2] = 1.0
    for i in range(INPUTS_DEV):
        for q in range(32):
            mix[q * INPUTS_DEV + i, i * 32 + q] = 1.0
    for k1 in range(RADIX):
        for j in range(8):
            comb[j * RADIX + k1, k1 * 8 + j] = 1.0
    orders = np.stack([turn, mix, comb]).astype(ml_dtypes.bfloat16)
    return np.concatenate([np.stack([high, low]), orders])


def radix4(values):
    (ar, ai), (br, bi), (cr, ci), (dr, di) = values
    pr, pi, mr, mi = ar + cr, ai + ci, ar - cr, ai - ci
    qr, qi, nr, ni = br + dr, bi + di, br - dr, bi - di
    return [(pr + qr, pi + qi), (mr + ni, mi - nr), (pr - qr, pi - qi), (mr - ni, mi + nr)]


def radix16(values):
    table = [[None] * 4 for _ in range(4)]
    for b in range(4):
        for c, (re, im) in enumerate(radix4([values[4 * a + b] for a in range(4)])):
            turn = b * c
            if turn == 0:
                table[b][c] = (re, im)
            elif turn == 4:
                table[b][c] = (im, -re)
            elif turn == 2:
                root = np.float32(np.sqrt(0.5))
                table[b][c] = ((re + im) * root, (im - re) * root)
            elif turn == 6:
                root = np.float32(np.sqrt(0.5))
                table[b][c] = ((im - re) * root, -(re + im) * root)
            else:
                cosine = np.float32(np.cos(2.0 * np.pi * turn / 16))
                sine = np.float32(np.sin(2.0 * np.pi * turn / 16))
                table[b][c] = (re * cosine + im * sine, im * cosine - re * sine)
    result = [None] * 16
    for c in range(4):
        for d, pair in enumerate(radix4([table[b][c] for b in range(4)])):
            result[c + 4 * d] = pair
    return result


def arrange_gains(gain_ref, matrix_ref, arranged_ref):
    comb = matrix_ref[4, 0:LANES, 0:LANES]
    dot = functools.partial(jnp.dot, preferred_element_type=F32)
    both = gain_ref[...].reshape(2 * INPUTS_DEV, CHANNELS)
    high = both.astype(BF16)
    rest = both - high.astype(F32)
    middle = rest.astype(BF16)
    low = (rest - middle.astype(F32)).astype(BF16)
    pieces = []
    for tile in range(RADIX):
        lanes = slice(tile * LANES, (tile + 1) * LANES)
        pieces.append(
            dot(low[:, lanes], comb) + dot(middle[:, lanes], comb) + dot(high[:, lanes], comb)
        )
    group = lax.broadcasted_iota(jnp.int32, (2 * INPUTS_DEV, LANES), 1) // 8
    for bit in (1, 2, 4, 8):
        clear = jnp.bitwise_and(group, bit) == 0
        for tile in range(RADIX):
            if tile & bit == 0:
                a, b = pieces[tile], pieces[tile | bit]
                pieces[tile] = jnp.where(clear, a, pltpu.roll(b, 8 * bit, 1))
                pieces[tile | bit] = jnp.where(clear, pltpu.roll(a, LANES - 8 * bit, 1), b)
    for k1 in range(RADIX):
        arranged_ref[k1] = pieces[k1]


def filter_transform(hist_ref, cur_ref, gain_ref, matrix_ref, turned, scratch):
    window, twist, ext, filtered, stage, equal = scratch
    i = pl.program_id(0)
    dot = functools.partial(jnp.dot, preferred_element_type=F32)
    for n1 in range(RADIX):
        lanes = slice(n1 * LANES, (n1 + 1) * LANES)
        for c in range(2):
            ext[n1, c, 0:HALF, :] = hist_ref[c, 0, :, lanes].astype(F32)
            ext[n1, c, HALF : 2 * HALF, :] = cur_ref[c, 0, :, lanes].astype(F32)
    for n1 in range(RADIX):
        lanes = slice(n1 * LANES, (n1 + 1) * LANES)
        weights = [window[t, :, lanes] for t in range(TAPS)]
        for c in range(2):
            sums = [None, None]
            for begin in range(1, 9 + TAPS):
                rows = ext[n1, c, begin : begin + 8, :]
                for block in range(2):
                    t = begin - 1 - 8 * block
                    if 0 <= t < TAPS:
                        term = rows * weights[t]
                        sums[block] = term if t == 0 else sums[block] + term
            for block in range(2):
                filtered[block, n1, c] = sums[block]
    for block in range(2):
        values = [(filtered[block, n1, 0], filtered[block, n1, 1]) for n1 in range(RADIX)]
        for k1, (re, im) in enumerate(radix16(values)):
            cosine, sine = twist[k1, 0], twist[k1, 1]
            rows = slice(k1 * HALF + block * 8, k1 * HALF + block * 8 + 8)
            stage[rows, 0:LANES] = re * cosine - im * sine
            stage[rows, LANES : 2 * LANES] = re * sine + im * cosine
    whole = stage[...]
    high = whole.astype(BF16)
    low = (whole - high.astype(F32)).astype(BF16)
    stage[...] = dot(high, matrix_ref[0]) + dot(high, matrix_ref[1]) + dot(low, matrix_ref[0])
    for k1 in range(RADIX):
        rows = slice(k1 * HALF, (k1 + 1) * HALF)
        re, im = stage[rows, 0:LANES], stage[rows, LANES : 2 * LANES]
        gain_re = gain_ref[k1, pl.ds(i, 1), :]
        gain_im = gain_ref[k1, pl.ds(INPUTS_DEV + i, 1), :]
        equal[rows, 0:LANES] = (re * gain_re - im * gain_im).astype(BF16)
        equal[rows, LANES : 2 * LANES] = (re * gain_im + im * gain_re).astype(BF16)
    turned[i] = lax.dot_general(
        matrix_ref[2], equal[...], (((1,), (1,)), ((), ())), preferred_element_type=F32
    ).astype(BF16)


def spread_tables(vector_ref, window, twist):
    for t in range(TAPS):
        window[t] = jnp.broadcast_to(vector_ref[t : t + 1, 0:CHANNELS], (8, CHANNELS))
        for c in range(2):
            begin = CHANNELS + c * LANES
            twist[t, c] = jnp.broadcast_to(
                vector_ref[t : t + 1, begin : begin + LANES], (8, LANES)
            )


def mixed_group(matrix_ref, turned, group):
    piece = turned[:, group * 32 : (group + 1) * 32, :].reshape(256, 256)
    return jnp.dot(matrix_ref[3], piece, preferred_element_type=F32).astype(BF16)


def late_kernel(
    hist_ref, cur_ref, gain_ref, vector_ref, matrix_ref, mixed_ref, arranged_ref, turned, *scratch
):
    i = pl.program_id(0)

    @pl.when(i == 0)
    def _():
        spread_tables(vector_ref, scratch[0], scratch[1])
        arrange_gains(gain_ref, matrix_ref, arranged_ref)

    filter_transform(hist_ref, cur_ref, arranged_ref, matrix_ref, turned, scratch)

    @pl.when(i == INPUTS_DEV - 1)
    def _():
        for group in range(8):
            mixed_ref[group] = mixed_group(matrix_ref, turned, group)


def early_kernel(
    hist_ref, cur_ref, arranged_ref, vector_ref, matrix_ref, mixed_ref, out_ref, turned, *scratch
):
    i = pl.program_id(0)

    @pl.when(i == 0)
    def _():
        spread_tables(vector_ref, scratch[0], scratch[1])

    filter_transform(hist_ref, cur_ref, arranged_ref, matrix_ref, turned, scratch)

    @pl.when(i == INPUTS_DEV - 1)
    def _():
        for group in range(8):
            rows = slice(group * 16, (group + 1) * 16)
            early = mixed_group(matrix_ref, turned, group)
            for h in range(2):
                lanes = slice(h * LANES, (h + 1) * LANES)
                out_ref[rows, h, 0] = early[:, lanes].reshape(16, 16, LANES)
                out_ref[rows, h, 1] = mixed_ref[group, :, lanes].reshape(16, 16, LANES)


def frame_spec():
    return pl.BlockSpec((2, 1, HALF, CHANNELS), lambda i: (0, i, 0, 0))


def whole_spec(shape):
    return pl.BlockSpec(shape, lambda i: (0,) * len(shape))


def front(body, operands, out_shapes):
    many = isinstance(out_shapes, tuple)
    specs = [whole_spec(s.shape) for s in (out_shapes if many else (out_shapes,))]
    return pl.pallas_call(
        body,
        grid=(INPUTS_DEV,),
        in_specs=[frame_spec(), frame_spec()] + [whole_spec(a.shape) for a in operands[2:]],
        out_specs=tuple(specs) if many else specs[0],
        out_shape=out_shapes,
        scratch_shapes=[
            pltpu.VMEM((INPUTS_DEV, 256, 256), BF16),
            pltpu.VMEM((TAPS, 8, CHANNELS), F32),
            pltpu.VMEM((RADIX, 2, 8, LANES), F32),
            pltpu.VMEM((RADIX, 2, 2 * HALF, LANES), F32),
            pltpu.VMEM((2, RADIX, 2, 8, LANES), F32),
            pltpu.VMEM((256, 256), F32),
            pltpu.VMEM((256, 256), BF16),
        ],
        compiler_params=pltpu.CompilerParams(vmem_limit_bytes=32 * MIB),
        cost_estimate=pl.CostEstimate(
            flops=1400000000, bytes_accessed=6 * MIB, transcendentals=0
        ),
    )(*operands)


def gram_rows(place_ref, parts_ref, side, out_ref):
    wanted = jnp.bitwise_xor(place_ref[0], side)
    depth = CHIPS * 2 * LANES
    rows = [
        parts_ref[pl.ds(pl.multiple_of(block * 128 + wanted * 64, 64), 64), :]
        for block in range(CHIPS)
    ]
    same = jnp.concatenate(rows, axis=0)
    cross = jnp.concatenate([same[:, depth:], -same[:, :depth]], axis=1)
    both = jnp.concatenate([same, cross], axis=0)
    result = lax.dot_general(
        both, parts_ref[...], (((1,), (1,)), ((), ())), preferred_element_type=F32
    ) * (1.0 / 4096.0)
    for block in range(CHIPS):
        for part in range(2):
            begin = part * 256 + block * 64
            out_ref[block, part] = result[begin : begin + 64]


def send_kernel(place_ref, spectra_ref, send_ref, parts_ref):
    depth = CHIPS * 2 * LANES
    for l in range(CHIPS):
        for half in range(2):
            slab = spectra_ref[:, l, half].astype(F32).reshape(STATIONS, 2, 8, LANES)
            for c in range(2):
                begin = c * depth + (l * 2 + half) * LANES
                parts_ref[:, begin : begin + LANES] = (
                    slab[:, c].reshape(STATIONS * 8, LANES).astype(BF16)
                )
    gram_rows(place_ref, parts_ref, 1, send_ref)


def keep_kernel(place_ref, parts_ref, keep_ref):
    gram_rows(place_ref, parts_ref, 0, keep_ref)


def gram(body, operands, out_shapes):
    return pl.pallas_call(
        body,
        in_specs=[pl.BlockSpec(memory_space=pltpu.SMEM), pl.BlockSpec(memory_space=pltpu.VMEM)],
        out_specs=jax.tree.map(lambda _: pl.BlockSpec(memory_space=pltpu.VMEM), out_shapes),
        out_shape=out_shapes,
        compiler_params=pltpu.CompilerParams(vmem_limit_bytes=32 * MIB),
        cost_estimate=pl.CostEstimate(
            flops=1100000000, bytes_accessed=4 * MIB, transcendentals=0
        ),
    )(*operands)


def span_sum(total):
    chip, core = lax.axis_index("l"), lax.axis_index("c")
    block = lax.broadcasted_iota(jnp.int32, total.shape, 0)
    part = lax.broadcasted_iota(jnp.int32, total.shape, 1)
    row = lax.broadcasted_iota(jnp.int32, total.shape, 2)
    column = lax.broadcasted_iota(jnp.int32, total.shape, 3)
    largest = jnp.maximum(jnp.max(jnp.abs(total)), 1e-30)
    exponent = jnp.ceil(jnp.log2(largest))
    own = (part == 1) & (column == 128 * block + 64 * core + row)
    scaled = jnp.where(own, exponent, total * jnp.exp2(13.0 - exponent)).astype(jnp.float16)
    arrived = lax.all_to_all(scaled, "l", 0, 0, tiled=True).astype(F32)
    first = 128 * chip + 64 * core
    exponents = lax.dynamic_slice(arrived, (0, 1, 0, first), (CHIPS, 1, 1, 1))
    own = (part == 1) & (column == first + row)
    values = jnp.where(own, 0.0, arrived) / jnp.exp2(13.0 - exponents)
    both = jnp.stack([values[0] + values[1], values[2] + values[3]])
    return jnp.transpose(both, (2, 0, 1, 3))


def on_device(voltages, gains):
    vectors = jnp.asarray(vector_table())
    matrices = jnp.asarray(matrix_table())
    late = jnp.transpose(voltages[:, HALF:], (2, 0, 1, 3))
    early = jnp.transpose(voltages[:, :HALF], (2, 0, 1, 3))
    forward = [(t, t + 1) for t in range(2 * CHIPS - 1)]
    history = lax.ppermute(late, ("l", "c"), forward)
    mixed, arranged = front(
        late_kernel,
        [early, late, gains, vectors, matrices],
        (
            jax.ShapeDtypeStruct((8, 256, 256), BF16),
            jax.ShapeDtypeStruct((RADIX, 2 * INPUTS_DEV, LANES), F32),
        ),
    )
    ready = front(
        early_kernel,
        [history, early, arranged, vectors, matrices, mixed],
        jax.ShapeDtypeStruct((LANES, 2, 2, 16, LANES), BF16),
    )
    chunks = ready.reshape(4 * STATIONS, 2, 16, LANES)
    arrived = lax.all_to_all(chunks, ("z", "h", "x", "l"), 0, 0, tiled=True)
    place = lax.axis_index("c").astype(jnp.int32).reshape(1)
    rows_shape = jax.ShapeDtypeStruct((CHIPS, 2, 64, 512), F32)
    parts_shape = jax.ShapeDtypeStruct((512, 2 * CHIPS * 2 * LANES), BF16)
    spectra = arrived.reshape(STATIONS, CHIPS, 2, 16, LANES)
    send, parts = gram(send_kernel, [place, spectra], (rows_shape, parts_shape))
    received = lax.ppermute(send, "c", [(0, 1), (1, 0)])
    keep = gram(keep_kernel, [place, parts], rows_shape)
    return span_sum(keep + received)


def solution(mesh):
    fine = Mesh(mesh.devices.reshape(8, 2, 4, CHIPS, 2), ("z", "h", "x", "l", "c"))
    station, time = ("z", "h", "x"), ("l", "c")
    return jax.shard_map(
        on_device,
        mesh=fine,
        in_specs=(P(station, time, None, None), P(None, station, None)),
        out_specs=P(time, station, None, None),
        check_vma=False,
    )
```

time: 151 us -> 137 us (0.907)
  waiting for transfers between devices: 76.5 us -> 65.1 us
  starting transfers between devices: 39.2 us -> 36 us
  local copies, waits for them, and re-layouts: 10.8 us -> 7.86 us
  other arithmetic: 0.45 us -> 2.64 us
    ppermute x4 -> x2, waiting for transfers between devices: 26.6 us -> 1.06 us  [the longest x1 1.06 us: on_device(): history = lax.ppermute(late, ('l', 'c'), forward)]
    all_to_all x0 -> x1, waiting for transfers between devices: none -> 14.3 us  [span_sum(): arrived = lax.all_to_all(scaled, 'l', 0, 0, tiled=True).astype(F32)]
    ppermute x4 -> x2, starting transfers between devices: 17.7 us -> 10.7 us  [the longest x1 6.1 us: on_device(): received = lax.ppermute(send, 'c', [(0, 1), (1, 0)])]
    all_to_all x0 -> x1, starting transfers between devices: none -> 3.79 us  [span_sum(): arrived = lax.all_to_all(scaled, 'l', 0, 0, tiled=True).astype(F32)]
    reshape x2 -> x0, local copies, waits for them, and re-layouts: 2.87 us -> none  [on_device(): gains.reshape(2, INPUTS_DEV, LANES, RADIX)]
    unnamed x13 -> x12, local copies, waits for them, and re-layouts: 5.66 us -> 3.63 us
    slice x2 -> x1, local copies, waits for them, and re-layouts: 1.08 us -> 3.03 us  [on_device(): early = jnp.transpose(voltages[:, :HALF], (2, 0, 1, 3))]
    pallas_call x3 -> x4, Pallas kernels: 23 us -> 24.1 us  [the longest x2 21.1 us: front(): pl.pallas_call(body, grid=(INPUTS_DEV,), in_specs=[frame_spec(), frame_sp...]
  transfers between devices with their start and end apart: 5 -> 4, of which waited for: 4 -> 3; matrix products, arithmetic and copies ran while one was open for 2% -> 0% of each run, Pallas kernels for 5% -> 8%
where the time goes in v2:
time: 137 us
  waiting for transfers between devices  65.1 us (48%)
  starting transfers between devices  36 us (26%)
  Pallas kernels  24.1 us (18%)
  local copies, waits for them, and re-layouts  7.86 us (6%)
  other arithmetic  2.64 us (2%)
    all_to_all x1, waiting for transfers between devices, on_device(): arrived = lax.all_to_all(chunks, ('z', 'h', 'x', 'l'), 0, 0, tiled=True)  49.7 us
    all_to_all x1, starting transfers between devices, on_device(): arrived = lax.all_to_all(chunks, ('z', 'h', 'x', 'l'), 0, 0, tiled=True)  21.5 us
    pallas_call x2, Pallas kernels, front(): pl.pallas_call(body, grid=(INPUTS_DEV,), in_specs=[frame_spec(), frame_sp...  21.1 us
    all_to_all x1, waiting for transfers between devices, span_sum(): arrived = lax.all_to_all(scaled, 'l', 0, 0, tiled=True).astype(F32)  14.3 us
    ppermute x1, starting transfers between devices, on_device(): received = lax.ppermute(send, 'c', [(0, 1), (1, 0)])  6.1 us
    ppermute x1, starting transfers between devices, on_device(): history = lax.ppermute(late, ('l', 'c'), forward)  4.59 us
    all_to_all x1, starting transfers between devices, span_sum(): arrived = lax.all_to_all(scaled, 'l', 0, 0, tiled=True).astype(F32)  3.79 us
    unnamed x12, local copies, waits for them, and re-layouts  3.63 us
  transfers between devices with their start and end apart: 4, of which 3 were waited for; matrix products, arithmetic and copies ran while one was open for 0% of the time, Pallas kernels for 8%

profile of v2, /device:TPU:1, one launch (start us, length us, event | category | flops | bytes accessed | tf_op | source)
XLA Modules:
  0.0 136.6 jit_solution(16417249863065424316)
XLA Ops:
  0.0 3.0 %fusion.2 = (bf16[8,16,2,2048]{3,2,1,0:T(2,128)(2,1)S(1)}, bf16[8,16,2,2048]{3,2,1,0:T(2,128)(2,1)S(1)}) fusion(bf16[8,32,2,2048]{3,2,1,0:T(2,128)(2,1)} %param.4), kind=kLoop, calls=%fused_computation.16 | loop fusion | bytes 4194304 | tf_op jit(solution)/shard_map/slice | solution.py:327
  3.0 0.0 copy-start
  3.1 0.0 copy-start.1
  3.1 0.0 copy-start.2
  3.1 0.4 copy.16
  3.4 4.6 %collective-permute-start = (bf16[2,8,16,2048]{3,2,1,0:T(8,128)(2,1)S(1)}, bf16[2,8,16,2048]{3,2,1,0:T(8,128)(2,1)S(1)}, u32[]{:S(2)}, u32[]{:S(2)}) collective-permute-start(bf16[2,8,16,2048]{3,2,1,0:T(8,128)(2,1)S(1)} %bitcast.14), channel_id=1, source_target_pairs={{0,1},{1,2},{2,3},{3,4},{4,5},{5,6},{6,7},{8,9},{9,10},{10,11},{11... | collective-permute-start | bytes 3145736 | tf_op jit(solution)/shard_map/ppermute | solution.py:329
  8.0 0.4 copy.15
  8.4 0.0 copy-done
  8.4 0.0 copy-done.1
  8.4 0.0 copy-done.2
  8.4 10.3 %shard_map.46 = (bf16[8,256,256]{2,1,0:T(8,128)(2,1)S(1)}, f32[16,16,128]{2,1,0:T(8,128)S(1)}) custom-call(bf16[2,8,16,2048]{3,2,1,0:T(8,128)(2,1)S(1)} %bitcast.11, bf16[2,8,16,2048]{3,2,1,0:T(8,128)(2,1)S(1)} %bitcast.15, f32[2,8,2048]{2,1,0:T(8,128)S(1)} %copy-done.2, f32[16,2304]{1,0:T(8,128)S(1)} %copy-done.1, bf16[5,256,256]{2,1,0:T(8,128)(2,1)S(1)} %copy-done), custom_call_target="tpu_custom_call" | custom-call | flops 1400000000 | bytes 6291456 | tf_op jit(solution)/shard_map/pallas_call | solution.py:233
  18.7 1.1 collective-permute-done.hist_ref
  19.8 10.8 %shard_map.47 = bf16[128,2,2,16,128]{4,3,2,1,0:T(8,128)(2,1)} custom-call(bf16[2,8,16,2048]{3,2,1,0:T(8,128)(2,1)S(1)} %collective-permute-done.hist_ref, bf16[2,8,16,2048]{3,2,1,0:T(8,128)(2,1)S(1)} %bitcast.12, f32[16,16,128]{2,1,0:T(8,128)S(1)} %get-tuple-element.9.arranged_ref, f32[16,2304]{1,0:T(8,128)S(1)} %copy-done.1, ...), custom_call_target="tpu_custom_call" | custom-call | flops 1400000000 | bytes 6291456 | tf_op jit(solution)/shard_map/pallas_call | solution.py:233
  30.6 21.5 %all-to-all-start = ((bf16[256,2,16,128]{3,2,1,0:T(8,128)(2,1)}), bf16[256,2,16,128]{3,2,1,0:T(8,128)(2,1)S(1)}, u32[]{:S(2)}, u32[]{:S(2)}) async-start(bf16[256,2,16,128]{3,2,1,0:T(8,128)(2,1)} %bitcast.3), calls=%async_computation | async-start | bytes 4194304 | tf_op jit(solution)/shard_map/all_to_all | solution.py:344
  52.1 49.7 %all-to-all-done = bf16[256,2,16,128]{3,2,1,0:T(8,128)(2,1)S(1)} async-done(((bf16[256,2,16,128]{3,2,1,0:T(8,128)(2,1)}), bf16[256,2,16,128]{3,2,1,0:T(8,128)(2,1)S(1)}, u32[]{:S(2)}, u32[]{:S(2)}) %all-to-all-start) | async-done | bytes 2097184 | tf_op jit(solution)/shard_map/all_to_all | solution.py:344
  101.8 1.7 %shard_map.48 = (f32[4,2,64,512]{3,2,1,0:T(8,128)S(1)}, bf16[512,2048]{1,0:T(8,128)(2,1)S(1)}) custom-call(s32[1]{0:T(128)} %bitcast.place_ref, bf16[64,4,2,16,128]{4,3,2,1,0:T(8,128)(2,1)S(1)} %bitcast.13), custom_call_target="tpu_custom_call" | custom-call | flops 1100000000 | bytes 4194304 | tf_op jit(solution)/shard_map/pallas_call | solution.py:292
  103.5 0.0 copy-start.3
  103.5 1.3 copy-done.3
  104.8 6.1 %collective-permute-start.1 = (f32[4,2,64,512]{3,2,1,0:T(8,128)S(1)}, f32[4,2,64,512]{3,2,1,0:T(8,128)S(1)}, u32[]{:S(2)}, u32[]{:S(2)}) collective-permute-start(f32[4,2,64,512]{3,2,1,0:T(8,128)S(1)} %get-tuple-element.12), channel_id=1, source_target_pairs={{0,1},{1,0},{2,3},{3,2},{4,5},{5,4},{6,7},{7,6},{8,9},{9,8},{10,11... | collective-permute-start | bytes 3145736 | tf_op jit(solution)/shard_map/ppermute | solution.py:350
  111.0 0.0 copy-start.4
  111.0 1.6 %copy-done.4 = bf16[512,2048]{1,0:T(8,128)(2,1)S(1)} copy-done((bf16[512,2048]{1,0:T(8,128)(2,1)S(1)}, bf16[512,2048]{1,0:T(8,128)(2,1)}, u32[]{:S(2)}) %copy-start.4) | copy-done | bytes 2097176
  112.6 1.3 shard_map.49
  113.8 0.0 collective-permute-done.1
  113.9 0.8 abs_reduce_fusion
  115.4 1.1 select_convert_fusion
  116.5 3.8 %all-to-all-start.1 = ((f16[4,2,64,512]{3,2,1,0:T(8,128)(2,1)}), f16[4,2,64,512]{3,2,1,0:T(8,128)(2,1)S(1)}, u32[]{:S(2)}, u32[]{:S(2)}) async-start(f16[4,2,64,512]{3,2,1,0:T(8,128)(2,1)} %select_convert_fusion), calls=%async_computation.1 | async-start | bytes 1048576 | tf_op jit(solution)/shard_map/all_to_all | solution.py:314
  120.3 14.3 %all-to-all-done.1 = f16[4,2,64,512]{3,2,1,0:T(8,128)(2,1)S(1)} async-done(((f16[4,2,64,512]{3,2,1,0:T(8,128)(2,1)}), f16[4,2,64,512]{3,2,1,0:T(8,128)(2,1)S(1)}, u32[]{:S(2)}, u32[]{:S(2)}) %all-to-all-start.1) | async-done | bytes 524320 | tf_op jit(solution)/shard_map/all_to_all | solution.py:314
  134.7 0.1 convert_element_type.7
  134.8 0.2 exponential_reduce_fusion
  135.0 0.2 select_divide_fusion
  135.2 0.1 slice_add_fusion.1
  135.4 1.2 copy.10
  (4 shorter events, 0.1 us)
Async XLA Ops:
  3.0 5.4 %copy-start = (bf16[5,256,256]{2,1,0:T(8,128)(2,1)S(1)}, bf16[5,256,256]{2,1,0:T(8,128)(2,1)}, u32[]{:S(2)}) copy-start(bf16[5,256,256]{2,1,0:T(8,128)(2,1)} %constant.14.clone.matrix_ref) | copy-start | bytes 1966084
  3.1 5.4 %copy-start.1 = (f32[16,2304]{1,0:T(8,128)S(1)}, f32[16,2304]{1,0:T(8,128)}, u32[]{:S(2)}) copy-start(f32[16,2304]{1,0:T(8,128)} %constant.13.clone.vector_ref) | copy-start | bytes 442372
  3.1 5.4 %copy-start.2 = (f32[2,8,2048]{2,1,0:T(8,128)S(1)}, f32[2,8,2048]{2,1,0:T(8,128)}, u32[]{:S(2)}) copy-start(f32[2,8,2048]{2,1,0:T(8,128)} %gain_ref.1) | copy-start | bytes 393220
  3.4 16.3 %collective-permute-start = (bf16[2,8,16,2048]{3,2,1,0:T(8,128)(2,1)S(1)}, bf16[2,8,16,2048]{3,2,1,0:T(8,128)(2,1)S(1)}, u32[]{:S(2)}, u32[]{:S(2)}) collective-permute-start(bf16[2,8,16,2048]{3,2,1,0:T(8,128)(2,1)S(1)} %bitcast.14), channel_id=1, source_target_pairs={{0,1},{1,2},{2,3},{3,4},{4,5},{5,6},{6,7},{8,9},{9,10},{10,11},{11... | collective-permute-start | bytes 3145736 | tf_op jit(solution)/shard_map/ppermute | solution.py:329
  30.6 71.2 %all-to-all-start = ((bf16[256,2,16,128]{3,2,1,0:T(8,128)(2,1)}), bf16[256,2,16,128]{3,2,1,0:T(8,128)(2,1)S(1)}, u32[]{:S(2)}, u32[]{:S(2)}) async-start(bf16[256,2,16,128]{3,2,1,0:T(8,128)(2,1)} %bitcast.3), calls=%async_computation | async-start | bytes 4194304 | tf_op jit(solution)/shard_map/all_to_all | solution.py:344
  103.5 1.3 copy-start.3
  104.8 9.0 %collective-permute-start.1 = (f32[4,2,64,512]{3,2,1,0:T(8,128)S(1)}, f32[4,2,64,512]{3,2,1,0:T(8,128)S(1)}, u32[]{:S(2)}, u32[]{:S(2)}) collective-permute-start(f32[4,2,64,512]{3,2,1,0:T(8,128)S(1)} %get-tuple-element.12), channel_id=1, source_target_pairs={{0,1},{1,0},{2,3},{3,2},{4,5},{5,4},{6,7},{7,6},{8,9},{9,8},{10,11... | collective-permute-start | bytes 3145736 | tf_op jit(solution)/shard_map/ppermute | solution.py:350
  111.0 1.6 %copy-start.4 = (bf16[512,2048]{1,0:T(8,128)(2,1)S(1)}, bf16[512,2048]{1,0:T(8,128)(2,1)}, u32[]{:S(2)}) copy-start(bf16[512,2048]{1,0:T(8,128)(2,1)} %copy-done.3) | copy-start | bytes 6291460
  116.5 18.1 %all-to-all-start.1 = ((f16[4,2,64,512]{3,2,1,0:T(8,128)(2,1)}), f16[4,2,64,512]{3,2,1,0:T(8,128)(2,1)S(1)}, u32[]{:S(2)}, u32[]{:S(2)}) async-start(f16[4,2,64,512]{3,2,1,0:T(8,128)(2,1)} %select_convert_fusion), calls=%async_computation.1 | async-start | bytes 1048576 | tf_op jit(solution)/shard_map/all_to_all | solution.py:314

commit v3 on v2

--- a/solution.py
+++ b/solution.py
@@ -16,6 +16,8 @@
 LANES = 128
 HALF = 16
 INPUTS_DEV = 8
+GROUP = 8
+STEPS = 4
 STATIONS = 64
 CHIPS = 4
 MIB = 1024 * 1024
@@ -118,29 +120,27 @@
         arranged_ref[k1] = pieces[k1]
 
 
-def filter_transform(hist_ref, cur_ref, gain_ref, matrix_ref, turned, scratch):
-    window, twist, ext, filtered, stage, equal = scratch
-    i = pl.program_id(0)
-    dot = functools.partial(jnp.dot, preferred_element_type=F32)
+def analyse(hist_ref, cur_ref, j, stage, scratch):
+    window, twist, ext, filtered = scratch
     for n1 in range(RADIX):
         lanes = slice(n1 * LANES, (n1 + 1) * LANES)
         for c in range(2):
-            ext[n1, c, 0:HALF, :] = hist_ref[c, 0, :, lanes].astype(F32)
-            ext[n1, c, HALF : 2 * HALF, :] = cur_ref[c, 0, :, lanes].astype(F32)
+            ext[n1, c, 0:HALF, :] = hist_ref[c, j, :, lanes].astype(F32)
+            ext[n1, c, HALF : 2 * HALF, :] = cur_ref[c, j, :, lanes].astype(F32)
     for n1 in range(RADIX):
         lanes = slice(n1 * LANES, (n1 + 1) * LANES)
-        weights = [window[t, :, lanes] for t in range(TAPS)]
+        sums = [None] * 4
+        for t in range(TAPS):
+            weight = window[t, :, lanes]
+            for c in range(2):
+                for block in range(2):
+                    begin = block * 8 + 1 + t
+                    term = ext[n1, c, begin : begin + 8, :] * weight
+                    slot = 2 * c + block
+                    sums[slot] = term if t == 0 else sums[slot] + term
         for c in range(2):
-            sums = [None, None]
-            for begin in range(1, 9 + TAPS):
-                rows = ext[n1, c, begin : begin + 8, :]
-                for block in range(2):
-                    t = begin - 1 - 8 * block
-                    if 0 <= t < TAPS:
-                        term = rows * weights[t]
-                        sums[block] = term if t == 0 else sums[block] + term
             for block in range(2):
-                filtered[block, n1, c] = sums[block]
+                filtered[block, n1, c] = sums[2 * c + block]
     for block in range(2):
         values = [(filtered[block, n1, 0], filtered[block, n1, 1]) for n1 in range(RADIX)]
         for k1, (re, im) in enumerate(radix16(values)):
@@ -148,20 +148,43 @@
             rows = slice(k1 * HALF + block * 8, k1 * HALF + block * 8 + 8)
             stage[rows, 0:LANES] = re * cosine - im * sine
             stage[rows, LANES : 2 * LANES] = re * sine + im * cosine
-    whole = stage[...]
+
+
+def finish(gain_ref, matrix_ref, turned, first, stage, result, equal):
+    dot = functools.partial(jnp.dot, preferred_element_type=F32)
+    whole = stage[first * 256 : (first + GROUP) * 256]
     high = whole.astype(BF16)
     low = (whole - high.astype(F32)).astype(BF16)
-    stage[...] = dot(high, matrix_ref[0]) + dot(high, matrix_ref[1]) + dot(low, matrix_ref[0])
-    for k1 in range(RADIX):
-        rows = slice(k1 * HALF, (k1 + 1) * HALF)
-        re, im = stage[rows, 0:LANES], stage[rows, LANES : 2 * LANES]
-        gain_re = gain_ref[k1, pl.ds(i, 1), :]
-        gain_im = gain_ref[k1, pl.ds(INPUTS_DEV + i, 1), :]
-        equal[rows, 0:LANES] = (re * gain_re - im * gain_im).astype(BF16)
-        equal[rows, LANES : 2 * LANES] = (re * gain_im + im * gain_re).astype(BF16)
-    turned[i] = lax.dot_general(
+    result[...] = dot(high, matrix_ref[0]) + dot(high, matrix_ref[1]) + dot(low, matrix_ref[0])
+    for i in range(GROUP):
+        for k1 in range(RADIX):
+            rows = slice(i * 256 + k1 * HALF, i * 256 + (k1 + 1) * HALF)
+            re, im = result[rows, 0:LANES], result[rows, LANES : 2 * LANES]
+            place = first + i
+            gain_re = gain_ref[k1, place : place + 1, :]
+            gain_im = gain_ref[k1, INPUTS_DEV + place : INPUTS_DEV + place + 1, :]
+            equal[rows, 0:LANES] = (re * gain_re - im * gain_im).astype(BF16)
+            equal[rows, LANES : 2 * LANES] = (re * gain_im + im * gain_re).astype(BF16)
+    across = lax.dot_general(
         matrix_ref[2], equal[...], (((1,), (1,)), ((), ())), preferred_element_type=F32
     ).astype(BF16)
+    for i in range(GROUP):
+        turned[first + i] = across[:, i * 256 : (i + 1) * 256]
+
+
+def filter_transform(hist_ref, cur_ref, gain_ref, matrix_ref, turned, scratch):
+    window, twist, ext, filtered, stage, result, equal = scratch
+    step = pl.program_id(0)
+    for j in range(INPUTS_DEV // STEPS):
+        rows = pl.ds(pl.multiple_of((step * (INPUTS_DEV // STEPS) + j) * 256, 256), 256)
+        analyse(
+            hist_ref, cur_ref, j, stage.at[rows], (window, twist, ext.at[j], filtered.at[j])
+        )
+
+    @pl.when(step == STEPS - 1)
+    def _():
+        for first in range(0, INPUTS_DEV, GROUP):
+            finish(gain_ref, matrix_ref, turned, first, stage, result, equal)
 
 
 def spread_tables(vector_ref, window, twist):
@@ -191,7 +214,7 @@
 
     filter_transform(hist_ref, cur_ref, arranged_ref, matrix_ref, turned, scratch)
 
-    @pl.when(i == INPUTS_DEV - 1)
+    @pl.when(i == STEPS - 1)
     def _():
         for group in range(8):
             mixed_ref[group] = mixed_group(matrix_ref, turned, group)
@@ -208,7 +231,7 @@
 
     filter_transform(hist_ref, cur_ref, arranged_ref, matrix_ref, turned, scratch)
 
-    @pl.when(i == INPUTS_DEV - 1)
+    @pl.when(i == STEPS - 1)
     def _():
         for group in range(8):
             rows = slice(group * 16, (group + 1) * 16)
@@ -219,8 +242,31 @@
                 out_ref[rows, h, 1] = mixed_ref[group, :, lanes].reshape(16, 16, LANES)
 
 
+def load_kernel(voltages_ref, late_ref, early_ref, sems):
+    copies = [
+        pltpu.make_async_copy(voltages_ref.at[:, pl.ds(HALF, HALF)], late_ref, sems.at[0]),
+        pltpu.make_async_copy(voltages_ref.at[:, pl.ds(0, HALF)], early_ref, sems.at[1]),
+    ]
+    for copy in copies:
+        copy.start()
+    for copy in copies:
+        copy.wait()
+
+
+def load(voltages):
+    shape = jax.ShapeDtypeStruct((INPUTS_DEV, HALF, 2, CHANNELS), BF16)
+    return pl.pallas_call(
+        load_kernel,
+        in_specs=[pl.BlockSpec(memory_space=pl.ANY)],
+        out_specs=[pl.BlockSpec(memory_space=pltpu.VMEM)] * 2,
+        out_shape=[shape, shape],
+        scratch_shapes=[pltpu.SemaphoreType.DMA((2,))],
+        compiler_params=pltpu.CompilerParams(vmem_limit_bytes=16 * MIB),
+    )(voltages)
+
+
 def frame_spec():
-    return pl.BlockSpec((2, 1, HALF, CHANNELS), lambda i: (0, i, 0, 0))
+    return pl.BlockSpec((2, INPUTS_DEV // STEPS, HALF, CHANNELS), lambda i: (0, i, 0, 0))
 
 
 def whole_spec(shape):
@@ -232,7 +278,7 @@
     specs = [whole_spec(s.shape) for s in (out_shapes if many else (out_shapes,))]
     return pl.pallas_call(
         body,
-        grid=(INPUTS_DEV,),
+        grid=(STEPS,),
         in_specs=[frame_spec(), frame_spec()] + [whole_spec(a.shape) for a in operands[2:]],
         out_specs=tuple(specs) if many else specs[0],
         out_shape=out_shapes,
@@ -240,10 +286,11 @@
             pltpu.VMEM((INPUTS_DEV, 256, 256), BF16),
             pltpu.VMEM((TAPS, 8, CHANNELS), F32),
             pltpu.VMEM((RADIX, 2, 8, LANES), F32),
-            pltpu.VMEM((RADIX, 2, 2 * HALF, LANES), F32),
-            pltpu.VMEM((2, RADIX, 2, 8, LANES), F32),
-            pltpu.VMEM((256, 256), F32),
-            pltpu.VMEM((256, 256), BF16),
+            pltpu.VMEM((INPUTS_DEV // STEPS, RADIX, 2, 2 * HALF, LANES), F32),
+            pltpu.VMEM((INPUTS_DEV // STEPS, 2, RADIX, 2, 8, LANES), F32),
+            pltpu.VMEM((INPUTS_DEV * 256, 256), F32),
+            pltpu.VMEM((GROUP * 256, 256), F32),
+            pltpu.VMEM((GROUP * 256, 256), BF16),
         ],
         compiler_params=pltpu.CompilerParams(vmem_limit_bytes=32 * MIB),
         cost_estimate=pl.CostEstimate(
@@ -271,7 +318,7 @@
             out_ref[block, part] = result[begin : begin + 64]
 
 
-def send_kernel(place_ref, spectra_ref, send_ref, parts_ref):
+def gram_kernel(side, place_ref, spectra_ref, out_ref, parts_ref):
     depth = CHIPS * 2 * LANES
     for l in range(CHIPS):
         for half in range(2):
@@ -281,24 +328,21 @@
                 parts_ref[:, begin : begin + LANES] = (
                     slab[:, c].reshape(STATIONS * 8, LANES).astype(BF16)
                 )
-    gram_rows(place_ref, parts_ref, 1, send_ref)
-
-
-def keep_kernel(place_ref, parts_ref, keep_ref):
-    gram_rows(place_ref, parts_ref, 0, keep_ref)
-
-
-def gram(body, operands, out_shapes):
+    gram_rows(place_ref, parts_ref, side, out_ref)
+
+
+def gram(side, place, spectra):
     return pl.pallas_call(
-        body,
+        functools.partial(gram_kernel, side),
         in_specs=[pl.BlockSpec(memory_space=pltpu.SMEM), pl.BlockSpec(memory_space=pltpu.VMEM)],
-        out_specs=jax.tree.map(lambda _: pl.BlockSpec(memory_space=pltpu.VMEM), out_shapes),
-        out_shape=out_shapes,
-        compiler_params=pltpu.CompilerParams(vmem_limit_bytes=32 * MIB),
+        out_specs=pl.BlockSpec(memory_space=pltpu.VMEM),
+        out_shape=jax.ShapeDtypeStruct((CHIPS, 2, 64, 512), F32),
+        scratch_shapes=[pltpu.VMEM((512, 2 * CHIPS * 2 * LANES), BF16)],
+        compiler_params=pltpu.CompilerParams(vmem_limit_bytes=24 * MIB),
         cost_estimate=pl.CostEstimate(
             flops=1100000000, bytes_accessed=4 * MIB, transcendentals=0
         ),
-    )(*operands)
+    )(place, spectra)
 
 
 def span_sum(total):
@@ -323,8 +367,7 @@
 def on_device(voltages, gains):
     vectors = jnp.asarray(vector_table())
     matrices = jnp.asarray(matrix_table())
-    late = jnp.transpose(voltages[:, HALF:], (2, 0, 1, 3))
-    early = jnp.transpose(voltages[:, :HALF], (2, 0, 1, 3))
+    late, early = (jnp.transpose(half, (2, 0, 1, 3)) for half in load(voltages))
     forward = [(t, t + 1) for t in range(2 * CHIPS - 1)]
     history = lax.ppermute(late, ("l", "c"), forward)
     mixed, arranged = front(
@@ -343,12 +386,9 @@
     chunks = ready.reshape(4 * STATIONS, 2, 16, LANES)
     arrived = lax.all_to_all(chunks, ("z", "h", "x", "l"), 0, 0, tiled=True)
     place = lax.axis_index("c").astype(jnp.int32).reshape(1)
-    rows_shape = jax.ShapeDtypeStruct((CHIPS, 2, 64, 512), F32)
-    parts_shape = jax.ShapeDtypeStruct((512, 2 * CHIPS * 2 * LANES), BF16)
     spectra = arrived.reshape(STATIONS, CHIPS, 2, 16, LANES)
-    send, parts = gram(send_kernel, [place, spectra], (rows_shape, parts_shape))
-    received = lax.ppermute(send, "c", [(0, 1), (1, 0)])
-    keep = gram(keep_kernel, [place, parts], rows_shape)
+    received = lax.ppermute(gram(1, place, spectra), "c", [(0, 1), (1, 0)])
+    keep = gram(0, place, spectra)
     return span_sum(keep + received)
 
 

time: 137 us -> 131 us (0.956)
  Pallas kernels: 24.1 us -> 18.1 us
  local copies, waits for them, and re-layouts: 7.86 us -> 3.51 us
  waiting for transfers between devices: 65.1 us -> 68.5 us
    pallas_call x4 -> x5, Pallas kernels: 24.1 us -> 18.1 us  [the longest x2 14.4 us: front(): pl.pallas_call(body, grid=(STEPS,), in_specs=[frame_spec(), frame_spec()]...]
    ppermute x1, waiting for transfers between devices: 1.06 us -> 4.35 us  [on_device(): history = lax.ppermute(late, ('l', 'c'), forward)]
    slice x1 -> x0, local copies, waits for them, and re-layouts: 3.03 us -> none  [on_device(): early = jnp.transpose(voltages[:, :HALF], (2, 0, 1, 3))]
    unnamed x12 -> x8, local copies, waits for them, and re-layouts: 3.63 us -> 1.61 us
  transfers between devices with their start and end apart: 4 -> 4, of which waited for: 3 -> 4; matrix products, arithmetic and copies ran while one was open for 0% -> 0% of each run, Pallas kernels for 8% -> 7%
where the time goes in v3:
time: 131 us
  waiting for transfers between devices  68.5 us (52%)
  starting transfers between devices  36 us (27%)
  Pallas kernels  18.1 us (14%)
  other arithmetic  3.89 us (3%)
  local copies, waits for them, and re-layouts  3.51 us (3%)
    all_to_all x1, waiting for transfers between devices, on_device(): arrived = lax.all_to_all(chunks, ('z', 'h', 'x', 'l'), 0, 0, tiled=True)  49.5 us
    all_to_all x1, starting transfers between devices, on_device(): arrived = lax.all_to_all(chunks, ('z', 'h', 'x', 'l'), 0, 0, tiled=True)  21.7 us
    pallas_call x2, Pallas kernels, front(): pl.pallas_call(body, grid=(STEPS,), in_specs=[frame_spec(), frame_spec()]...  14.4 us
    all_to_all x1, waiting for transfers between devices, span_sum(): arrived = lax.all_to_all(scaled, 'l', 0, 0, tiled=True).astype(F32)  14 us
    ppermute x1, starting transfers between devices, on_device(): received = lax.ppermute(gram(1, place, spectra), 'c', [(0, 1), (1, 0)])  5.93 us
    ppermute x1, starting transfers between devices, on_device(): history = lax.ppermute(late, ('l', 'c'), forward)  4.59 us
    ppermute x1, waiting for transfers between devices, on_device(): history = lax.ppermute(late, ('l', 'c'), forward)  4.35 us
    all_to_all x1, starting transfers between devices, span_sum(): arrived = lax.all_to_all(scaled, 'l', 0, 0, tiled=True).astype(F32)  3.8 us
  transfers between devices with their start and end apart: 4, of which 4 were waited for; matrix products, arithmetic and copies ran while one was open for 0% of the time, Pallas kernels for 7%

profile of v3, /device:TPU:1, one launch (start us, length us, event | category | flops | bytes accessed | tf_op | source)
XLA Modules:
  0.0 130.9 jit_solution(1047144762491544587)
XLA Ops:
  0.0 0.0 copy-start
  0.0 1.6 %copy-done = bf16[8,32,2,2048]{3,2,1,0:T(2,128)(2,1)S(1)} copy-done((bf16[8,32,2,2048]{3,2,1,0:T(2,128)(2,1)S(1)}, bf16[8,32,2,2048]{3,2,1,0:T(2,128)(2,1)}, u32[]{:S(2)}) %copy-start) | copy-done | bytes 2097176
  1.6 0.2 shard_map.46
  1.8 0.0 copy-start.1
  1.8 0.0 copy-start.2
  1.8 0.0 copy-start.3
  1.8 0.4 copy.14
  2.2 4.6 %collective-permute-start = (bf16[2,8,16,2048]{3,2,1,0:T(8,128)(2,1)S(1)}, bf16[2,8,16,2048]{3,2,1,0:T(8,128)(2,1)S(1)}, u32[]{:S(2)}, u32[]{:S(2)}) collective-permute-start(bf16[2,8,16,2048]{3,2,1,0:T(8,128)(2,1)S(1)} %bitcast.15), channel_id=1, source_target_pairs={{0,1},{1,2},{2,3},{3,4},{4,5},{5,6},{6,7},{8,9},{9,10},{10,11},{11... | collective-permute-start | bytes 3145736 | tf_op jit(solution)/shard_map/ppermute | solution.py:372
  6.8 0.4 copy.13
  7.1 0.0 copy-done.1
  7.1 0.0 copy-done.2
  7.1 0.0 copy-done.3
  7.1 7.0 %shard_map.47 = (bf16[8,256,256]{2,1,0:T(8,128)(2,1)S(1)}, f32[16,16,128]{2,1,0:T(8,128)S(1)}) custom-call(bf16[2,8,16,2048]{3,2,1,0:T(8,128)(2,1)S(1)} %bitcast.11, bf16[2,8,16,2048]{3,2,1,0:T(8,128)(2,1)S(1)} %bitcast.16, f32[2,8,2048]{2,1,0:T(8,128)S(1)} %copy-done.3, f32[16,2304]{1,0:T(8,128)S(1)} %copy-done.2, bf16[5,256,256]{2,1,0:T(8,128)(2,1)S(1)} %copy-done.1), custom_call_target="tpu_custom_call" | custom-call | flops 1400000000 | bytes 6291456 | tf_op jit(solution)/shard_map/pallas_call | solution.py:279
  14.1 4.4 %collective-permute-done.hist_ref = bf16[2,8,16,2048]{3,2,1,0:T(8,128)(2,1)S(1)} collective-permute-done((bf16[2,8,16,2048]{3,2,1,0:T(8,128)(2,1)S(1)}, bf16[2,8,16,2048]{3,2,1,0:T(8,128)(2,1)S(1)}, u32[]{:S(2)}, u32[]{:S(2)}) %collective-permute-start) | collective-permute-done | bytes 1048608 | tf_op jit(solution)/shard_map/ppermute | solution.py:372
  18.5 7.5 %shard_map.48 = bf16[128,2,2,16,128]{4,3,2,1,0:T(8,128)(2,1)} custom-call(bf16[2,8,16,2048]{3,2,1,0:T(8,128)(2,1)S(1)} %collective-permute-done.hist_ref, bf16[2,8,16,2048]{3,2,1,0:T(8,128)(2,1)S(1)} %bitcast.12, f32[16,16,128]{2,1,0:T(8,128)S(1)} %get-tuple-element.11.arranged_ref, f32[16,2304]{1,0:T(8,128)S(1)} %copy-done.2, ...), custom_call_target="tpu_custom_call" | custom-call | flops 1400000000 | bytes 6291456 | tf_op jit(solution)/shard_map/pallas_call | solution.py:279
  26.0 21.7 %all-to-all-start = ((bf16[256,2,16,128]{3,2,1,0:T(8,128)(2,1)}), bf16[256,2,16,128]{3,2,1,0:T(8,128)(2,1)S(1)}, u32[]{:S(2)}, u32[]{:S(2)}) async-start(bf16[256,2,16,128]{3,2,1,0:T(8,128)(2,1)} %bitcast.3), calls=%async_computation | async-start | bytes 4194304 | tf_op jit(solution)/shard_map/all_to_all | solution.py:387
  47.6 49.5 %all-to-all-done = bf16[256,2,16,128]{3,2,1,0:T(8,128)(2,1)S(1)} async-done(((bf16[256,2,16,128]{3,2,1,0:T(8,128)(2,1)}), bf16[256,2,16,128]{3,2,1,0:T(8,128)(2,1)S(1)}, u32[]{:S(2)}, u32[]{:S(2)}) %all-to-all-start) | async-done | bytes 2097184 | tf_op jit(solution)/shard_map/all_to_all | solution.py:387
  97.1 1.7 %shard_map.50 = f32[4,2,64,512]{3,2,1,0:T(8,128)S(1)} custom-call(s32[1]{0:T(128)} %bitcast.place_ref, bf16[64,4,2,16,128]{4,3,2,1,0:T(8,128)(2,1)S(1)} %bitcast.13), custom_call_target="tpu_custom_call" | custom-call | flops 1100000000 | bytes 4194304 | tf_op jit(solution)/shard_map/pallas_call | solution.py:335
  98.9 5.9 %collective-permute-start.1 = (f32[4,2,64,512]{3,2,1,0:T(8,128)S(1)}, f32[4,2,64,512]{3,2,1,0:T(8,128)}, u32[]{:S(2)}, u32[]{:S(2)}) collective-permute-start(f32[4,2,64,512]{3,2,1,0:T(8,128)S(1)} %shard_map.50), channel_id=1, source_target_pairs={{0,1},{1,0},{2,3},{3,2},{4,5},{5,4},{6,7},{7,6},{8,9},{9,8},{10,11... | collective-permute-start | bytes 3145736 | tf_op jit(solution)/shard_map/ppermute | solution.py:390
  104.8 1.7 %shard_map.49 = f32[4,2,64,512]{3,2,1,0:T(8,128)S(1)} custom-call(s32[1]{0:T(128)} %bitcast.place_ref, bf16[64,4,2,16,128]{4,3,2,1,0:T(8,128)(2,1)S(1)} %bitcast.14), custom_call_target="tpu_custom_call" | custom-call | flops 1100000000 | bytes 4194304 | tf_op jit(solution)/shard_map/pallas_call | solution.py:335
  106.6 0.6 collective-permute-done.1
  107.2 2.1 %abs_reduce_fusion = (f32[]{:T(128)}, f32[4,2,64,512]{3,2,1,0:T(8,128)S(1)}) fusion(f32[4,2,64,512]{3,2,1,0:T(8,128)S(1)} %shard_map.49, f32[4,2,64,512]{3,2,1,0:T(8,128)} %collective-permute-done.1), kind=kLoop, calls=%fused_computation.4 | loop fusion | flops 786431 | bytes 3145732 | tf_op jit(solution)/shard_map/reduce_max | solution.py:354
  110.0 1.1 select_convert_fusion
  111.1 3.8 %all-to-all-start.1 = ((f16[4,2,64,512]{3,2,1,0:T(8,128)(2,1)}), f16[4,2,64,512]{3,2,1,0:T(8,128)(2,1)S(1)}, u32[]{:S(2)}, u32[]{:S(2)}) async-start(f16[4,2,64,512]{3,2,1,0:T(8,128)(2,1)} %select_convert_fusion), calls=%async_computation.1 | async-start | bytes 1048576 | tf_op jit(solution)/shard_map/all_to_all | solution.py:358
  114.9 14.0 %all-to-all-done.1 = f16[4,2,64,512]{3,2,1,0:T(8,128)(2,1)S(1)} async-done(((f16[4,2,64,512]{3,2,1,0:T(8,128)(2,1)}), f16[4,2,64,512]{3,2,1,0:T(8,128)(2,1)S(1)}, u32[]{:S(2)}, u32[]{:S(2)}) %all-to-all-start.1) | async-done | bytes 524320 | tf_op jit(solution)/shard_map/all_to_all | solution.py:358
  129.0 0.1 convert_element_type.7
  129.1 0.2 exponential_reduce_fusion
  129.3 0.2 select_divide_fusion
  129.5 0.1 slice_add_fusion.1
  129.7 1.2 copy.10
  (4 shorter events, 0.1 us)
Async XLA Ops:
  0.0 1.6 %copy-start = (bf16[8,32,2,2048]{3,2,1,0:T(2,128)(2,1)S(1)}, bf16[8,32,2,2048]{3,2,1,0:T(2,128)(2,1)}, u32[]{:S(2)}) copy-start(bf16[8,32,2,2048]{3,2,1,0:T(2,128)(2,1)} %voltages_ref.1) | copy-start | bytes 6291460
  1.8 5.4 %copy-start.1 = (bf16[5,256,256]{2,1,0:T(8,128)(2,1)S(1)}, bf16[5,256,256]{2,1,0:T(8,128)(2,1)}, u32[]{:S(2)}) copy-start(bf16[5,256,256]{2,1,0:T(8,128)(2,1)} %constant.14.clone.matrix_ref) | copy-start | bytes 1966084
  1.8 5.4 %copy-start.2 = (f32[16,2304]{1,0:T(8,128)S(1)}, f32[16,2304]{1,0:T(8,128)}, u32[]{:S(2)}) copy-start(f32[16,2304]{1,0:T(8,128)} %constant.13.clone.vector_ref) | copy-start | bytes 442372
  1.8 5.4 %copy-start.3 = (f32[2,8,2048]{2,1,0:T(8,128)S(1)}, f32[2,8,2048]{2,1,0:T(8,128)}, u32[]{:S(2)}) copy-start(f32[2,8,2048]{2,1,0:T(8,128)} %gain_ref.1) | copy-start | bytes 393220
  2.2 16.3 %collective-permute-start = (bf16[2,8,16,2048]{3,2,1,0:T(8,128)(2,1)S(1)}, bf16[2,8,16,2048]{3,2,1,0:T(8,128)(2,1)S(1)}, u32[]{:S(2)}, u32[]{:S(2)}) collective-permute-start(bf16[2,8,16,2048]{3,2,1,0:T(8,128)(2,1)S(1)} %bitcast.15), channel_id=1, source_target_pairs={{0,1},{1,2},{2,3},{3,4},{4,5},{5,6},{6,7},{8,9},{9,10},{10,11},{11... | collective-permute-start | bytes 3145736 | tf_op jit(solution)/shard_map/ppermute | solution.py:372
  26.0 71.2 %all-to-all-start = ((bf16[256,2,16,128]{3,2,1,0:T(8,128)(2,1)}), bf16[256,2,16,128]{3,2,1,0:T(8,128)(2,1)S(1)}, u32[]{:S(2)}, u32[]{:S(2)}) async-start(bf16[256,2,16,128]{3,2,1,0:T(8,128)(2,1)} %bitcast.3), calls=%async_computation | async-start | bytes 4194304 | tf_op jit(solution)/shard_map/all_to_all | solution.py:387
  98.9 8.3 %collective-permute-start.1 = (f32[4,2,64,512]{3,2,1,0:T(8,128)S(1)}, f32[4,2,64,512]{3,2,1,0:T(8,128)}, u32[]{:S(2)}, u32[]{:S(2)}) collective-permute-start(f32[4,2,64,512]{3,2,1,0:T(8,128)S(1)} %shard_map.50), channel_id=1, source_target_pairs={{0,1},{1,0},{2,3},{3,2},{4,5},{5,4},{6,7},{7,6},{8,9},{9,8},{10,11... | collective-permute-start | bytes 3145736 | tf_op jit(solution)/shard_map/ppermute | solution.py:390
  111.1 17.8 %all-to-all-start.1 = ((f16[4,2,64,512]{3,2,1,0:T(8,128)(2,1)}), f16[4,2,64,512]{3,2,1,0:T(8,128)(2,1)S(1)}, u32[]{:S(2)}, u32[]{:S(2)}) async-start(f16[4,2,64,512]{3,2,1,0:T(8,128)(2,1)} %select_convert_fusion), calls=%async_computation.1 | async-start | bytes 1048576 | tf_op jit(solution)/shard_map/all_to_all | solution.py:358

commit v4 on v3

--- a/solution.py
+++ b/solution.py
@@ -16,8 +16,8 @@
 LANES = 128
 HALF = 16
 INPUTS_DEV = 8
-GROUP = 8
-STEPS = 4
+GROUP = 4
+STEPS = 2
 STATIONS = 64
 CHIPS = 4
 MIB = 1024 * 1024
@@ -152,7 +152,7 @@
 
 def finish(gain_ref, matrix_ref, turned, first, stage, result, equal):
     dot = functools.partial(jnp.dot, preferred_element_type=F32)
-    whole = stage[first * 256 : (first + GROUP) * 256]
+    whole = stage[...]
     high = whole.astype(BF16)
     low = (whole - high.astype(F32)).astype(BF16)
     result[...] = dot(high, matrix_ref[0]) + dot(high, matrix_ref[1]) + dot(low, matrix_ref[0])
@@ -169,22 +169,26 @@
         matrix_ref[2], equal[...], (((1,), (1,)), ((), ())), preferred_element_type=F32
     ).astype(BF16)
     for i in range(GROUP):
-        turned[first + i] = across[:, i * 256 : (i + 1) * 256]
-
-
-def filter_transform(hist_ref, cur_ref, gain_ref, matrix_ref, turned, scratch):
+        turned[i] = across[:, i * 256 : (i + 1) * 256]
+
+
+def filter_transform(hist_ref, cur_ref, gain_ref, vector_ref, matrix_ref, first, turned, scratch):
     window, twist, ext, filtered, stage, result, equal = scratch
     step = pl.program_id(0)
-    for j in range(INPUTS_DEV // STEPS):
-        rows = pl.ds(pl.multiple_of((step * (INPUTS_DEV // STEPS) + j) * 256, 256), 256)
+
+    @pl.when(step == 0)
+    def _():
+        spread_tables(vector_ref, window, twist)
+
+    for j in range(GROUP // STEPS):
+        rows = pl.ds(pl.multiple_of((step * (GROUP // STEPS) + j) * 256, 256), 256)
         analyse(
             hist_ref, cur_ref, j, stage.at[rows], (window, twist, ext.at[j], filtered.at[j])
         )
 
     @pl.when(step == STEPS - 1)
     def _():
-        for first in range(0, INPUTS_DEV, GROUP):
-            finish(gain_ref, matrix_ref, turned, first, stage, result, equal)
+        finish(gain_ref, matrix_ref, turned, first, stage, result, equal)
 
 
 def spread_tables(vector_ref, window, twist):
@@ -197,56 +201,90 @@
             )
 
 
-def mixed_group(matrix_ref, turned, group):
-    piece = turned[:, group * 32 : (group + 1) * 32, :].reshape(256, 256)
+def mix(matrix_ref, lower, upper, group):
+    part = slice(group * 32, (group + 1) * 32)
+    piece = jnp.concatenate(
+        [lower[:, part, :].reshape(128, 256), upper[:, part, :].reshape(128, 256)], axis=0
+    )
     return jnp.dot(matrix_ref[3], piece, preferred_element_type=F32).astype(BF16)
 
 
-def late_kernel(
-    hist_ref, cur_ref, gain_ref, vector_ref, matrix_ref, mixed_ref, arranged_ref, turned, *scratch
+def mix_all(matrix_ref, lower, upper, out_ref):
+    for group in range(8):
+        rows = slice(group * 16, (group + 1) * 16)
+        mixed = mix(matrix_ref, lower, upper, group)
+        for h in range(2):
+            out_ref[rows, h] = mixed[:, h * LANES : (h + 1) * LANES].reshape(16, 16, LANES)
+
+
+def late_lower_kernel(
+    hist_ref, cur_ref, gain_ref, vector_ref, matrix_ref, turned, arranged_ref, *scratch
 ):
-    i = pl.program_id(0)
-
-    @pl.when(i == 0)
-    def _():
-        spread_tables(vector_ref, scratch[0], scratch[1])
+    @pl.when(pl.program_id(0) == 0)
+    def _():
         arrange_gains(gain_ref, matrix_ref, arranged_ref)
 
-    filter_transform(hist_ref, cur_ref, arranged_ref, matrix_ref, turned, scratch)
-
-    @pl.when(i == STEPS - 1)
-    def _():
-        for group in range(8):
-            mixed_ref[group] = mixed_group(matrix_ref, turned, group)
-
-
-def early_kernel(
-    hist_ref, cur_ref, arranged_ref, vector_ref, matrix_ref, mixed_ref, out_ref, turned, *scratch
+    filter_transform(
+        hist_ref, cur_ref, arranged_ref, vector_ref, matrix_ref, 0, turned, scratch
+    )
+
+
+def late_upper_kernel(
+    hist_ref, cur_ref, gain_ref, vector_ref, matrix_ref, lower_ref, mixed_ref, turned, *scratch
 ):
-    i = pl.program_id(0)
-
-    @pl.when(i == 0)
-    def _():
-        spread_tables(vector_ref, scratch[0], scratch[1])
-
-    filter_transform(hist_ref, cur_ref, arranged_ref, matrix_ref, turned, scratch)
-
-    @pl.when(i == STEPS - 1)
-    def _():
-        for group in range(8):
-            rows = slice(group * 16, (group + 1) * 16)
-            early = mixed_group(matrix_ref, turned, group)
-            for h in range(2):
-                lanes = slice(h * LANES, (h + 1) * LANES)
-                out_ref[rows, h, 0] = early[:, lanes].reshape(16, 16, LANES)
-                out_ref[rows, h, 1] = mixed_ref[group, :, lanes].reshape(16, 16, LANES)
-
-
-def load_kernel(voltages_ref, late_ref, early_ref, sems):
-    copies = [
-        pltpu.make_async_copy(voltages_ref.at[:, pl.ds(HALF, HALF)], late_ref, sems.at[0]),
-        pltpu.make_async_copy(voltages_ref.at[:, pl.ds(0, HALF)], early_ref, sems.at[1]),
-    ]
+    filter_transform(
+        hist_ref, cur_ref, gain_ref, vector_ref, matrix_ref, GROUP, turned, scratch
+    )
+
+    @pl.when(pl.program_id(0) == STEPS - 1)
+    def _():
+        mix_all(matrix_ref, lower_ref, turned, mixed_ref)
+
+
+def early_lower_kernel(hist_ref, cur_ref, gain_ref, vector_ref, matrix_ref, turned, *scratch):
+    filter_transform(hist_ref, cur_ref, gain_ref, vector_ref, matrix_ref, 0, turned, scratch)
+
+
+def early_upper_kernel(
+    hist_ref,
+    cur_ref,
+    gain_ref,
+    vector_ref,
+    matrix_ref,
+    lower_ref,
+    mixed_ref,
+    out_ref,
+    turned,
+    early_ref,
+    sems,
+    *scratch,
+):
+    step = pl.program_id(0)
+    late_copy = pltpu.make_async_copy(mixed_ref, out_ref.at[:, :, 1], sems.at[0])
+    early_copy = pltpu.make_async_copy(early_ref, out_ref.at[:, :, 0], sems.at[1])
+
+    @pl.when(step == 0)
+    def _():
+        late_copy.start()
+
+    filter_transform(
+        hist_ref, cur_ref, gain_ref, vector_ref, matrix_ref, GROUP, turned, scratch
+    )
+
+    @pl.when(step == STEPS - 1)
+    def _():
+        mix_all(matrix_ref, lower_ref, turned, early_ref)
+        early_copy.start()
+        early_copy.wait()
+        late_copy.wait()
+
+
+def load_kernel(voltages_ref, *refs):
+    outs, sems = refs[:4], refs[4]
+    copies = []
+    for n, out in enumerate(outs):
+        source = voltages_ref.at[pl.ds((n % 2) * GROUP, GROUP), pl.ds((1 - n // 2) * HALF, HALF)]
+        copies.append(pltpu.make_async_copy(source, out, sems.at[n]))
     for copy in copies:
         copy.start()
     for copy in copies:
@@ -254,47 +292,47 @@
 
 
 def load(voltages):
-    shape = jax.ShapeDtypeStruct((INPUTS_DEV, HALF, 2, CHANNELS), BF16)
+    shape = jax.ShapeDtypeStruct((GROUP, HALF, 2, CHANNELS), BF16)
     return pl.pallas_call(
         load_kernel,
-        in_specs=[pl.BlockSpec(memory_space=pl.ANY)],
-        out_specs=[pl.BlockSpec(memory_space=pltpu.VMEM)] * 2,
-        out_shape=[shape, shape],
-        scratch_shapes=[pltpu.SemaphoreType.DMA((2,))],
+        in_specs=[pl.BlockSpec(memory_space=pltpu.HBM)],
+        out_specs=[pl.BlockSpec(memory_space=pltpu.VMEM)] * 4,
+        out_shape=[shape] * 4,
+        scratch_shapes=[pltpu.SemaphoreType.DMA((4,))],
         compiler_params=pltpu.CompilerParams(vmem_limit_bytes=16 * MIB),
     )(voltages)
 
 
 def frame_spec():
-    return pl.BlockSpec((2, INPUTS_DEV // STEPS, HALF, CHANNELS), lambda i: (0, i, 0, 0))
+    return pl.BlockSpec((2, GROUP // STEPS, HALF, CHANNELS), lambda i: (0, i, 0, 0))
 
 
 def whole_spec(shape):
     return pl.BlockSpec(shape, lambda i: (0,) * len(shape))
 
 
-def front(body, operands, out_shapes):
-    many = isinstance(out_shapes, tuple)
-    specs = [whole_spec(s.shape) for s in (out_shapes if many else (out_shapes,))]
+def front(body, operands, out_shapes, out_specs=None, own_scratch=()):
+    if out_specs is None:
+        out_specs = [whole_spec(s.shape) for s in out_shapes]
     return pl.pallas_call(
         body,
         grid=(STEPS,),
         in_specs=[frame_spec(), frame_spec()] + [whole_spec(a.shape) for a in operands[2:]],
-        out_specs=tuple(specs) if many else specs[0],
+        out_specs=out_specs,
         out_shape=out_shapes,
         scratch_shapes=[
-            pltpu.VMEM((INPUTS_DEV, 256, 256), BF16),
+            *own_scratch,
             pltpu.VMEM((TAPS, 8, CHANNELS), F32),
             pltpu.VMEM((RADIX, 2, 8, LANES), F32),
-            pltpu.VMEM((INPUTS_DEV // STEPS, RADIX, 2, 2 * HALF, LANES), F32),
-            pltpu.VMEM((INPUTS_DEV // STEPS, 2, RADIX, 2, 8, LANES), F32),
-            pltpu.VMEM((INPUTS_DEV * 256, 256), F32),
+            pltpu.VMEM((GROUP // STEPS, RADIX, 2, 2 * HALF, LANES), F32),
+            pltpu.VMEM((GROUP // STEPS, 2, RADIX, 2, 8, LANES), F32),
+            pltpu.VMEM((GROUP * 256, 256), F32),
             pltpu.VMEM((GROUP * 256, 256), F32),
             pltpu.VMEM((GROUP * 256, 256), BF16),
         ],
         compiler_params=pltpu.CompilerParams(vmem_limit_bytes=32 * MIB),
         cost_estimate=pl.CostEstimate(
-            flops=1400000000, bytes_accessed=6 * MIB, transcendentals=0
+            flops=700000000, bytes_accessed=3 * MIB, transcendentals=0
         ),
     )(*operands)
 
@@ -345,18 +383,44 @@
     )(place, spectra)
 
 
-def span_sum(total):
-    chip, core = lax.axis_index("l"), lax.axis_index("c")
-    block = lax.broadcasted_iota(jnp.int32, total.shape, 0)
-    part = lax.broadcasted_iota(jnp.int32, total.shape, 1)
-    row = lax.broadcasted_iota(jnp.int32, total.shape, 2)
-    column = lax.broadcasted_iota(jnp.int32, total.shape, 3)
-    largest = jnp.maximum(jnp.max(jnp.abs(total)), 1e-30)
-    exponent = jnp.ceil(jnp.log2(largest))
-    own = (part == 1) & (column == 128 * block + 64 * core + row)
-    scaled = jnp.where(own, exponent, total * jnp.exp2(13.0 - exponent)).astype(jnp.float16)
-    arrived = lax.all_to_all(scaled, "l", 0, 0, tiled=True).astype(F32)
-    first = 128 * chip + 64 * core
+def combine_kernel(place_ref, keep_ref, received_ref, out_ref):
+    core = place_ref[0]
+    largest = None
+    for block in range(CHIPS):
+        for part in range(2):
+            total = keep_ref[block, part] + received_ref[block, part]
+            out_ref[block, part] = total
+            here = jnp.max(jnp.abs(total), axis=0, keepdims=True)
+            largest = here if largest is None else jnp.maximum(largest, here)
+    largest = jnp.maximum(jnp.max(largest, axis=1, keepdims=True), 1e-30)
+    exponent = jnp.ceil(jnp.log2(jnp.broadcast_to(largest, (8, LANES))))
+    factor = jnp.exp2(13.0 - exponent)[0:1, 0:1]
+    exponent = exponent[0:1, 0:1]
+    row = lax.broadcasted_iota(jnp.int32, (64, 512), 0)
+    column = lax.broadcasted_iota(jnp.int32, (64, 512), 1)
+    for block in range(CHIPS):
+        own = column == 128 * block + 64 * core + row
+        out_ref[block, 0] = out_ref[block, 0] * factor
+        out_ref[block, 1] = jnp.where(own, exponent, out_ref[block, 1] * factor)
+
+
+def combine(place, keep, received):
+    return pl.pallas_call(
+        combine_kernel,
+        in_specs=[pl.BlockSpec(memory_space=pltpu.SMEM)]
+        + [pl.BlockSpec(memory_space=pltpu.VMEM)] * 2,
+        out_specs=pl.BlockSpec(memory_space=pltpu.VMEM),
+        out_shape=jax.ShapeDtypeStruct(keep.shape, F32),
+        compiler_params=pltpu.CompilerParams(vmem_limit_bytes=16 * MIB),
+    )(place, keep, received)
+
+
+def span_sum(scaled):
+    part = lax.broadcasted_iota(jnp.int32, scaled.shape, 1)
+    row = lax.broadcasted_iota(jnp.int32, scaled.shape, 2)
+    column = lax.broadcasted_iota(jnp.int32, scaled.shape, 3)
+    arrived = lax.all_to_all(scaled.astype(jnp.float16), "l", 0, 0, tiled=True).astype(F32)
+    first = 128 * lax.axis_index("l") + 64 * lax.axis_index("c")
     exponents = lax.dynamic_slice(arrived, (0, 1, 0, first), (CHIPS, 1, 1, 1))
     own = (part == 1) & (column == first + row)
     values = jnp.where(own, 0.0, arrived) / jnp.exp2(13.0 - exponents)
@@ -367,21 +431,41 @@
 def on_device(voltages, gains):
     vectors = jnp.asarray(vector_table())
     matrices = jnp.asarray(matrix_table())
-    late, early = (jnp.transpose(half, (2, 0, 1, 3)) for half in load(voltages))
+    late_lower, late_upper, early_lower, early_upper = (
+        jnp.transpose(piece, (2, 0, 1, 3)) for piece in load(voltages)
+    )
     forward = [(t, t + 1) for t in range(2 * CHIPS - 1)]
-    history = lax.ppermute(late, ("l", "c"), forward)
-    mixed, arranged = front(
-        late_kernel,
-        [early, late, gains, vectors, matrices],
-        (
-            jax.ShapeDtypeStruct((8, 256, 256), BF16),
-            jax.ShapeDtypeStruct((RADIX, 2 * INPUTS_DEV, LANES), F32),
-        ),
-    )
-    ready = front(
-        early_kernel,
-        [history, early, arranged, vectors, matrices, mixed],
-        jax.ShapeDtypeStruct((LANES, 2, 2, 16, LANES), BF16),
+    history_lower = lax.ppermute(late_lower, ("l", "c"), forward)
+    history_upper = lax.ppermute(late_upper, ("l", "c"), forward)
+    turned_shape = jax.ShapeDtypeStruct((GROUP, 256, 256), BF16)
+    turned_scratch = pltpu.VMEM((GROUP, 256, 256), BF16)
+    mixed_shape = jax.ShapeDtypeStruct((LANES, 2, 16, LANES), BF16)
+    lower, arranged = front(
+        late_lower_kernel,
+        [early_lower, late_lower, gains, vectors, matrices],
+        [turned_shape, jax.ShapeDtypeStruct((RADIX, 2 * INPUTS_DEV, LANES), F32)],
+    )
+    (mixed,) = front(
+        late_upper_kernel,
+        [early_upper, late_upper, arranged, vectors, matrices, lower],
+        [mixed_shape],
+        own_scratch=[turned_scratch],
+    )
+    (lower,) = front(
+        early_lower_kernel,
+        [history_lower, early_lower, arranged, vectors, matrices],
+        [turned_shape],
+    )
+    (ready,) = front(
+        early_upper_kernel,
+        [history_upper, early_upper, arranged, vectors, matrices, lower, mixed],
+        [jax.ShapeDtypeStruct((LANES, 2, 2, 16, LANES), BF16)],
+        out_specs=[pl.BlockSpec(memory_space=pl.ANY)],
+        own_scratch=[
+            turned_scratch,
+            pltpu.VMEM((LANES, 2, 16, LANES), BF16),
+            pltpu.SemaphoreType.DMA((2,)),
+        ],
     )
     chunks = ready.reshape(4 * STATIONS, 2, 16, LANES)
     arrived = lax.all_to_all(chunks, ("z", "h", "x", "l"), 0, 0, tiled=True)
@@ -389,7 +473,7 @@
     spectra = arrived.reshape(STATIONS, CHIPS, 2, 16, LANES)
     received = lax.ppermute(gram(1, place, spectra), "c", [(0, 1), (1, 0)])
     keep = gram(0, place, spectra)
-    return span_sum(keep + received)
+    return span_sum(combine(place, keep, received))
 
 
 def solution(mesh):

time: 131 us -> 127 us (0.969)
  waiting for transfers between devices: 68.5 us -> 65.3 us
  other arithmetic: 3.89 us -> 1.58 us
    ppermute x1 -> x2, waiting for transfers between devices: 4.35 us -> 0.01 us  [the longest x1 0.01 us: on_device(): history_lower = lax.ppermute(late_lower, ('l', 'c'), forward)]
    reduce_max x1 -> x0, other arithmetic: 2.07 us -> none  [span_sum(): largest = jnp.maximum(jnp.max(jnp.abs(total)), 1e-30)]
    ppermute x1 -> x2, starting transfers between devices: 4.59 us -> 6.65 us  [the longest x1 4.73 us: on_device(): history_lower = lax.ppermute(late_lower, ('l', 'c'), forward)]
    pallas_call x2 -> x4, Pallas kernels: 14.4 us -> 15 us  [front(): pl.pallas_call(body, grid=(STEPS,), in_specs=[frame_spec(), frame_spec()]...]
  transfers between devices with their start and end apart: 4 -> 5, of which waited for: 4 -> 3; matrix products, arithmetic and copies ran while one was open for 0% -> 0% of each run, Pallas kernels for 7% -> 9%
where the time goes in v4:
time: 127 us; the launch traced here: 126 us
  waiting for transfers between devices  65.3 us (51%)
  starting transfers between devices  36.8 us (29%)
  Pallas kernels  18.9 us (15%)
  local copies, waits for them, and re-layouts  3.48 us (3%)
  other arithmetic  1.58 us (1%)
    all_to_all x1, waiting for transfers between devices, on_device(): arrived = lax.all_to_all(chunks, ('z', 'h', 'x', 'l'), 0, 0, tiled=True)  50.7 us
    all_to_all x1, starting transfers between devices, on_device(): arrived = lax.all_to_all(chunks, ('z', 'h', 'x', 'l'), 0, 0, tiled=True)  21.5 us
    pallas_call x4, Pallas kernels, front(): pl.pallas_call(body, grid=(STEPS,), in_specs=[frame_spec(), frame_spec()]...  15 us
    all_to_all x1, waiting for transfers between devices, span_sum(): lax.all_to_all(scaled.astype(jnp.float16), 'l', 0, 0, tiled=True)  14 us
    ppermute x1, starting transfers between devices, on_device(): received = lax.ppermute(gram(1, place, spectra), 'c', [(0, 1), (1, 0)])  5.02 us
    ppermute x1, starting transfers between devices, on_device(): history_lower = lax.ppermute(late_lower, ('l', 'c'), forward)  4.73 us
    all_to_all x1, starting transfers between devices, span_sum(): lax.all_to_all(scaled.astype(jnp.float16), 'l', 0, 0, tiled=True)  3.61 us
    pallas_call x2, Pallas kernels, gram(): pl.pallas_call(functools.partial(gram_kernel, side), in_specs=[pl.BlockSp...  3.47 us
  transfers between devices with their start and end apart: 5, of which 3 were waited for; matrix products, arithmetic and copies ran while one was open for 0% of the time, Pallas kernels for 9%

profile of v4, /device:TPU:1, one launch (start us, length us, event | category | flops | bytes accessed | tf_op | source)
XLA Modules:
  0.0 126.2 jit_solution(8310468607923449074)
XLA Ops:
  0.0 0.0 copy-start.1
  0.0 1.6 %copy-done.1 = bf16[8,32,2,2048]{3,2,1,0:T(2,128)(2,1)S(1)} copy-done((bf16[8,32,2,2048]{3,2,1,0:T(2,128)(2,1)S(1)}, bf16[8,32,2,2048]{3,2,1,0:T(2,128)(2,1)}, u32[]{:S(2)}) %copy-start.1) | copy-done | bytes 2097176
  1.6 0.2 shard_map.46
  1.8 0.0 copy-start
  1.8 0.0 copy-start.2
  1.8 0.0 copy-start.3
  1.8 0.2 copy.19
  2.0 4.7 %collective-permute-start.1 = (bf16[2,4,16,2048]{3,2,1,0:T(8,128)(2,1)S(1)}, bf16[2,4,16,2048]{3,2,1,0:T(8,128)(2,1)S(1)}, u32[]{:S(2)}, u32[]{:S(2)}) collective-permute-start(bf16[2,4,16,2048]{3,2,1,0:T(8,128)(2,1)S(1)} %bitcast.19), channel_id=1, source_target_pairs={{0,1},{1,2},{2,3},{3,4},{4,5},{5,6},{6,7},{8,9},{9,10},{10,11},{11... | collective-permute-start | bytes 1572872 | tf_op jit(solution)/shard_map/ppermute | solution.py:438
  6.7 0.2 copy.20
  6.9 1.9 %collective-permute-start = (bf16[2,4,16,2048]{3,2,1,0:T(8,128)(2,1)S(1)}, bf16[2,4,16,2048]{3,2,1,0:T(8,128)(2,1)S(1)}, u32[]{:S(2)}, u32[]{:S(2)}) collective-permute-start(bf16[2,4,16,2048]{3,2,1,0:T(8,128)(2,1)S(1)} %bitcast.15), channel_id=1, source_target_pairs={{0,1},{1,2},{2,3},{3,4},{4,5},{5,6},{6,7},{8,9},{9,10},{10,11},{11... | collective-permute-start | bytes 1572872 | tf_op jit(solution)/shard_map/ppermute | solution.py:439
  8.8 0.4 copy_bitcast_fusion.1
  9.2 0.0 copy-done
  9.2 0.0 copy-done.2
  9.2 0.0 copy-done.3
  9.2 3.6 %shard_map.47 = (bf16[4,256,256]{2,1,0:T(8,128)(2,1)S(1)}, f32[16,16,128]{2,1,0:T(8,128)S(1)}) custom-call(bf16[2,4,16,2048]{3,2,1,0:T(8,128)(2,1)S(1)} %get-tuple-element.19.hist_ref.cur_ref, bf16[2,4,16,2048]{3,2,1,0:T(8,128)(2,1)S(1)} %bitcast.20, f32[2,8,2048]{2,1,0:T(8,128)S(1)} %copy-done.3, f32[16,2304]{1,0:T(8,128)S(1)} %copy-done.2, ...), custom_call_target="tpu_custom_call" | custom-call | flops 700000000 | bytes 3145728 | tf_op jit(solution)/shard_map/pallas_call | solution.py:317
  12.8 3.7 %shard_map.49.mixed_ref = bf16[128,2,16,128]{3,2,1,0:T(8,128)(2,1)S(1)} custom-call(bf16[2,4,16,2048]{3,2,1,0:T(8,128)(2,1)S(1)} %get-tuple-element.20.hist_ref.cur_ref, bf16[2,4,16,2048]{3,2,1,0:T(8,128)(2,1)S(1)} %bitcast.16, f32[16,16,128]{2,1,0:T(8,128)S(1)} %get-tuple-element.15.gain_ref, f32[16,2304]{1,0:T(8,128)S(1)} %copy-done.2, ...), custom_call_target="tpu_custom_call" | custom-call | flops 700000000 | bytes 3145728 | tf_op jit(solution)/shard_map/pallas_call | solution.py:317
  16.6 0.0 collective-permute-done.1.hist_ref
  16.6 2.9 %shard_map.48.lower_ref = bf16[4,256,256]{2,1,0:T(8,128)(2,1)S(1)} custom-call(bf16[2,4,16,2048]{3,2,1,0:T(8,128)(2,1)S(1)} %collective-permute-done.1.hist_ref, bf16[2,4,16,2048]{3,2,1,0:T(8,128)(2,1)S(1)} %get-tuple-element.19.hist_ref.cur_ref, f32[16,16,128]{2,1,0:T(8,128)S(1)} %get-tuple-element.15.gain_ref, f32[16,2304]{1,0:T(8,128)S(1)} %copy-done.2, ...), custom_call_target="tpu_custom_call" | custom-call | flops 700000000 | bytes 3145728 | tf_op jit(solution)/shard_map/pallas_call | solution.py:317
  19.5 0.0 collective-permute-done.hist_ref
  19.5 4.8 %shard_map.50 = bf16[128,2,2,16,128]{4,3,2,1,0:T(8,128)(2,1)} custom-call(bf16[2,4,16,2048]{3,2,1,0:T(8,128)(2,1)S(1)} %collective-permute-done.hist_ref, bf16[2,4,16,2048]{3,2,1,0:T(8,128)(2,1)S(1)} %get-tuple-element.20.hist_ref.cur_ref, f32[16,16,128]{2,1,0:T(8,128)S(1)} %get-tuple-element.15.gain_ref, f32[16,2304]{1,0:T(8,128)S(1)} %copy-done.2, ...), custom_call_target="tpu_custom_call" | custom-call | flops 700000000 | bytes 3145728 | tf_op jit(solution)/shard_map/pallas_call | solution.py:317
  24.2 21.5 %all-to-all-start = ((bf16[256,2,16,128]{3,2,1,0:T(8,128)(2,1)}), bf16[256,2,16,128]{3,2,1,0:T(8,128)(2,1)S(1)}, u32[]{:S(2)}, u32[]{:S(2)}) async-start(bf16[256,2,16,128]{3,2,1,0:T(8,128)(2,1)} %bitcast.5), calls=%async_computation | async-start | bytes 4194304 | tf_op jit(solution)/shard_map/all_to_all | solution.py:471
  45.7 50.7 %all-to-all-done = bf16[256,2,16,128]{3,2,1,0:T(8,128)(2,1)S(1)} async-done(((bf16[256,2,16,128]{3,2,1,0:T(8,128)(2,1)}), bf16[256,2,16,128]{3,2,1,0:T(8,128)(2,1)S(1)}, u32[]{:S(2)}, u32[]{:S(2)}) %all-to-all-start) | async-done | bytes 2097184 | tf_op jit(solution)/shard_map/all_to_all | solution.py:471
  96.4 1.7 %shard_map.52 = f32[4,2,64,512]{3,2,1,0:T(8,128)S(1)} custom-call(s32[1]{0:T(128)} %bitcast.place_ref, bf16[64,4,2,16,128]{4,3,2,1,0:T(8,128)(2,1)S(1)} %bitcast.17), custom_call_target="tpu_custom_call" | custom-call | flops 1100000000 | bytes 4194304 | tf_op jit(solution)/shard_map/pallas_call | solution.py:373
  98.2 5.0 %collective-permute-start.2 = (f32[4,2,64,512]{3,2,1,0:T(8,128)S(1)}, f32[4,2,64,512]{3,2,1,0:T(8,128)S(1)}, u32[]{:S(2)}, u32[]{:S(2)}) collective-permute-start(f32[4,2,64,512]{3,2,1,0:T(8,128)S(1)} %shard_map.52), channel_id=1, source_target_pairs={{0,1},{1,0},{2,3},{3,2},{4,5},{5,4},{6,7},{7,6},{8,9},{9,8},{10,11... | collective-permute-start | bytes 3145736 | tf_op jit(solution)/shard_map/ppermute | solution.py:474
  103.2 1.7 %shard_map.51.keep_ref = f32[4,2,64,512]{3,2,1,0:T(8,128)S(1)} custom-call(s32[1]{0:T(128)} %bitcast.place_ref, bf16[64,4,2,16,128]{4,3,2,1,0:T(8,128)(2,1)S(1)} %bitcast.18), custom_call_target="tpu_custom_call" | custom-call | flops 1100000000 | bytes 4194304 | tf_op jit(solution)/shard_map/pallas_call | solution.py:373
  105.0 0.5 collective-permute-done.2.received_ref
  105.5 0.3 shard_map.53
  105.8 0.9 convert_element_type.6
  106.7 3.6 %all-to-all-start.1 = ((f16[4,2,64,512]{3,2,1,0:T(8,128)(2,1)}), f16[4,2,64,512]{3,2,1,0:T(8,128)(2,1)S(1)}, u32[]{:S(2)}, u32[]{:S(2)}) async-start(f16[4,2,64,512]{3,2,1,0:T(8,128)(2,1)} %convert_element_type.6), calls=%async_computation.1 | async-start | bytes 1048576 | tf_op jit(solution)/shard_map/all_to_all | solution.py:422
  110.3 14.0 %all-to-all-done.1 = f16[4,2,64,512]{3,2,1,0:T(8,128)(2,1)S(1)} async-done(((f16[4,2,64,512]{3,2,1,0:T(8,128)(2,1)}), f16[4,2,64,512]{3,2,1,0:T(8,128)(2,1)S(1)}, u32[]{:S(2)}, u32[]{:S(2)}) %all-to-all-start.1) | async-done | bytes 524320 | tf_op jit(solution)/shard_map/all_to_all | solution.py:422
  124.3 0.1 convert_element_type.7
  124.5 0.2 exponential_reduce_fusion
  124.7 0.2 select_divide_fusion
  124.9 0.1 slice_add_fusion.1
  125.0 1.2 copy.14
  (3 shorter events, 0.0 us)
Async XLA Ops:
  0.0 1.6 %copy-start.1 = (bf16[8,32,2,2048]{3,2,1,0:T(2,128)(2,1)S(1)}, bf16[8,32,2,2048]{3,2,1,0:T(2,128)(2,1)}, u32[]{:S(2)}) copy-start(bf16[8,32,2,2048]{3,2,1,0:T(2,128)(2,1)} %voltages_ref.1) | copy-start | bytes 6291460
  1.8 7.4 %copy-start = (bf16[5,256,256]{2,1,0:T(8,128)(2,1)S(1)}, bf16[5,256,256]{2,1,0:T(8,128)(2,1)}, u32[]{:S(2)}) copy-start(bf16[5,256,256]{2,1,0:T(8,128)(2,1)} %constant.30.clone.matrix_ref) | copy-start | bytes 1966084
  1.8 7.4 %copy-start.2 = (f32[16,2304]{1,0:T(8,128)S(1)}, f32[16,2304]{1,0:T(8,128)}, u32[]{:S(2)}) copy-start(f32[16,2304]{1,0:T(8,128)} %constant.29.clone.vector_ref) | copy-start | bytes 442372
  1.8 7.4 %copy-start.3 = (f32[2,8,2048]{2,1,0:T(8,128)S(1)}, f32[2,8,2048]{2,1,0:T(8,128)}, u32[]{:S(2)}) copy-start(f32[2,8,2048]{2,1,0:T(8,128)} %gain_ref.1) | copy-start | bytes 393220
  2.0 14.6 %collective-permute-start.1 = (bf16[2,4,16,2048]{3,2,1,0:T(8,128)(2,1)S(1)}, bf16[2,4,16,2048]{3,2,1,0:T(8,128)(2,1)S(1)}, u32[]{:S(2)}, u32[]{:S(2)}) collective-permute-start(bf16[2,4,16,2048]{3,2,1,0:T(8,128)(2,1)S(1)} %bitcast.19), channel_id=1, source_target_pairs={{0,1},{1,2},{2,3},{3,4},{4,5},{5,6},{6,7},{8,9},{9,10},{10,11},{11... | collective-permute-start | bytes 1572872 | tf_op jit(solution)/shard_map/ppermute | solution.py:438
  6.9 12.6 %collective-permute-start = (bf16[2,4,16,2048]{3,2,1,0:T(8,128)(2,1)S(1)}, bf16[2,4,16,2048]{3,2,1,0:T(8,128)(2,1)S(1)}, u32[]{:S(2)}, u32[]{:S(2)}) collective-permute-start(bf16[2,4,16,2048]{3,2,1,0:T(8,128)(2,1)S(1)} %bitcast.15), channel_id=1, source_target_pairs={{0,1},{1,2},{2,3},{3,4},{4,5},{5,6},{6,7},{8,9},{9,10},{10,11},{11... | collective-permute-start | bytes 1572872 | tf_op jit(solution)/shard_map/ppermute | solution.py:439
  24.2 72.2 %all-to-all-start = ((bf16[256,2,16,128]{3,2,1,0:T(8,128)(2,1)}), bf16[256,2,16,128]{3,2,1,0:T(8,128)(2,1)S(1)}, u32[]{:S(2)}, u32[]{:S(2)}) async-start(bf16[256,2,16,128]{3,2,1,0:T(8,128)(2,1)} %bitcast.5), calls=%async_computation | async-start | bytes 4194304 | tf_op jit(solution)/shard_map/all_to_all | solution.py:471
  98.2 7.3 %collective-permute-start.2 = (f32[4,2,64,512]{3,2,1,0:T(8,128)S(1)}, f32[4,2,64,512]{3,2,1,0:T(8,128)S(1)}, u32[]{:S(2)}, u32[]{:S(2)}) collective-permute-start(f32[4,2,64,512]{3,2,1,0:T(8,128)S(1)} %shard_map.52), channel_id=1, source_target_pairs={{0,1},{1,0},{2,3},{3,2},{4,5},{5,4},{6,7},{7,6},{8,9},{9,8},{10,11... | collective-permute-start | bytes 3145736 | tf_op jit(solution)/shard_map/ppermute | solution.py:474
  106.7 17.7 %all-to-all-start.1 = ((f16[4,2,64,512]{3,2,1,0:T(8,128)(2,1)}), f16[4,2,64,512]{3,2,1,0:T(8,128)(2,1)S(1)}, u32[]{:S(2)}, u32[]{:S(2)}) async-start(f16[4,2,64,512]{3,2,1,0:T(8,128)(2,1)} %convert_element_type.6), calls=%async_computation.1 | async-start | bytes 1048576 | tf_op jit(solution)/shard_map/all_to_all | solution.py:422

commit v5 on v4

--- a/solution.py
+++ b/solution.py
@@ -299,7 +299,7 @@
         out_specs=[pl.BlockSpec(memory_space=pltpu.VMEM)] * 4,
         out_shape=[shape] * 4,
         scratch_shapes=[pltpu.SemaphoreType.DMA((4,))],
-        compiler_params=pltpu.CompilerParams(vmem_limit_bytes=16 * MIB),
+        compiler_params=pltpu.CompilerParams(vmem_limit_bytes=4 * MIB),
     )(voltages)
 
 
@@ -330,15 +330,15 @@
             pltpu.VMEM((GROUP * 256, 256), F32),
             pltpu.VMEM((GROUP * 256, 256), BF16),
         ],
-        compiler_params=pltpu.CompilerParams(vmem_limit_bytes=32 * MIB),
+        compiler_params=pltpu.CompilerParams(vmem_limit_bytes=24 * MIB),
         cost_estimate=pl.CostEstimate(
             flops=700000000, bytes_accessed=3 * MIB, transcendentals=0
         ),
     )(*operands)
 
 
-def gram_rows(place_ref, parts_ref, side, out_ref):
-    wanted = jnp.bitwise_xor(place_ref[0], side)
+def gram_rows(parts_ref, side, out_ref):
+    wanted = jnp.bitwise_xor(lax.axis_index("c"), side)
     depth = CHIPS * 2 * LANES
     rows = [
         parts_ref[pl.ds(pl.multiple_of(block * 128 + wanted * 64, 64), 64), :]
@@ -356,7 +356,7 @@
             out_ref[block, part] = result[begin : begin + 64]
 
 
-def gram_kernel(side, place_ref, spectra_ref, out_ref, parts_ref):
+def gram_kernel(side, spectra_ref, out_ref, parts_ref):
     depth = CHIPS * 2 * LANES
     for l in range(CHIPS):
         for half in range(2):
@@ -366,65 +366,114 @@
                 parts_ref[:, begin : begin + LANES] = (
                     slab[:, c].reshape(STATIONS * 8, LANES).astype(BF16)
                 )
-    gram_rows(place_ref, parts_ref, side, out_ref)
-
-
-def gram(side, place, spectra):
+    gram_rows(parts_ref, side, out_ref)
+
+
+def gram(side, spectra):
     return pl.pallas_call(
         functools.partial(gram_kernel, side),
-        in_specs=[pl.BlockSpec(memory_space=pltpu.SMEM), pl.BlockSpec(memory_space=pltpu.VMEM)],
+        in_specs=[pl.BlockSpec(memory_space=pltpu.VMEM)],
         out_specs=pl.BlockSpec(memory_space=pltpu.VMEM),
         out_shape=jax.ShapeDtypeStruct((CHIPS, 2, 64, 512), F32),
         scratch_shapes=[pltpu.VMEM((512, 2 * CHIPS * 2 * LANES), BF16)],
-        compiler_params=pltpu.CompilerParams(vmem_limit_bytes=24 * MIB),
+        compiler_params=pltpu.CompilerParams(vmem_limit_bytes=16 * MIB),
         cost_estimate=pl.CostEstimate(
             flops=1100000000, bytes_accessed=4 * MIB, transcendentals=0
         ),
-    )(place, spectra)
-
-
-def combine_kernel(place_ref, keep_ref, received_ref, out_ref):
-    core = place_ref[0]
+    )(spectra)
+
+
+def own_mask(chip, core):
+    row = lax.broadcasted_iota(jnp.int32, (64, 512), 0)
+    column = lax.broadcasted_iota(jnp.int32, (64, 512), 1)
+    return column == 128 * chip + 64 * core + row
+
+
+def chip_rows(block, keep_ref, received_ref, own, factor, exponent, out_ref):
+    out_ref[0] = (keep_ref[block, 0] + received_ref[block, 0]) * factor
+    imaginary = (keep_ref[block, 1] + received_ref[block, 1]) * factor
+    out_ref[1] = jnp.where(own, exponent, imaginary)
+
+
+def far_kernel(
+    keep_ref, received_ref, far_ref, farthest_ref, exponent_ref
+):
     largest = None
     for block in range(CHIPS):
         for part in range(2):
             total = keep_ref[block, part] + received_ref[block, part]
-            out_ref[block, part] = total
             here = jnp.max(jnp.abs(total), axis=0, keepdims=True)
             largest = here if largest is None else jnp.maximum(largest, here)
     largest = jnp.maximum(jnp.max(largest, axis=1, keepdims=True), 1e-30)
-    exponent = jnp.ceil(jnp.log2(jnp.broadcast_to(largest, (8, LANES))))
-    factor = jnp.exp2(13.0 - exponent)[0:1, 0:1]
-    exponent = exponent[0:1, 0:1]
-    row = lax.broadcasted_iota(jnp.int32, (64, 512), 0)
-    column = lax.broadcasted_iota(jnp.int32, (64, 512), 1)
-    for block in range(CHIPS):
-        own = column == 128 * block + 64 * core + row
-        out_ref[block, 0] = out_ref[block, 0] * factor
-        out_ref[block, 1] = jnp.where(own, exponent, out_ref[block, 1] * factor)
-
-
-def combine(place, keep, received):
+    exponents = jnp.ceil(jnp.log2(jnp.broadcast_to(largest, (8, LANES))))
+    exponent_ref[...] = exponents
+    factor, exponent = jnp.exp2(13.0 - exponents)[0:1, 0:1], exponents[0:1, 0:1]
+    for step, out_ref in ((2, far_ref), (3, farthest_ref)):
+        block = jnp.bitwise_xor(lax.axis_index("l"), step)
+        own = own_mask(block, lax.axis_index("c"))
+        chip_rows(block, keep_ref, received_ref, own, factor, exponent, out_ref)
+
+
+def near_kernel(keep_ref, received_ref, exponent_ref, own_ref, near_ref):
+    chip = lax.axis_index("l")
+    exponents = exponent_ref[...]
+    factor, exponent = jnp.exp2(13.0 - exponents)[0:1, 0:1], exponents[0:1, 0:1]
+    for part in range(2):
+        own_ref[part] = keep_ref[chip, part] + received_ref[chip, part]
+    block = jnp.bitwise_xor(chip, 1)
+    own = own_mask(block, lax.axis_index("c"))
+    chip_rows(block, keep_ref, received_ref, own, factor, exponent, near_ref)
+
+
+def small(body, operands, out_shapes):
+    vmem = pl.BlockSpec(memory_space=pltpu.VMEM)
     return pl.pallas_call(
-        combine_kernel,
-        in_specs=[pl.BlockSpec(memory_space=pltpu.SMEM)]
-        + [pl.BlockSpec(memory_space=pltpu.VMEM)] * 2,
-        out_specs=pl.BlockSpec(memory_space=pltpu.VMEM),
-        out_shape=jax.ShapeDtypeStruct(keep.shape, F32),
-        compiler_params=pltpu.CompilerParams(vmem_limit_bytes=16 * MIB),
-    )(place, keep, received)
-
-
-def span_sum(scaled):
-    part = lax.broadcasted_iota(jnp.int32, scaled.shape, 1)
-    row = lax.broadcasted_iota(jnp.int32, scaled.shape, 2)
-    column = lax.broadcasted_iota(jnp.int32, scaled.shape, 3)
-    arrived = lax.all_to_all(scaled.astype(jnp.float16), "l", 0, 0, tiled=True).astype(F32)
-    first = 128 * lax.axis_index("l") + 64 * lax.axis_index("c")
-    exponents = lax.dynamic_slice(arrived, (0, 1, 0, first), (CHIPS, 1, 1, 1))
-    own = (part == 1) & (column == first + row)
-    values = jnp.where(own, 0.0, arrived) / jnp.exp2(13.0 - exponents)
-    both = jnp.stack([values[0] + values[1], values[2] + values[3]])
+        body,
+        in_specs=[vmem] * len(operands),
+        out_specs=[vmem] * len(out_shapes),
+        out_shape=[jax.ShapeDtypeStruct(shape, F32) for shape in out_shapes],
+        compiler_params=pltpu.CompilerParams(vmem_limit_bytes=8 * MIB),
+        cost_estimate=pl.CostEstimate(flops=2000000, bytes_accessed=2 * MIB, transcendentals=0),
+    )(*operands)
+
+
+def widened(ref, diagonal):
+    real, imaginary = ref[0], ref[1]
+    top = jnp.where(diagonal[0:8], imaginary[0:8], 0.0)
+    exponent = jnp.sum(top, axis=1, keepdims=True)[0:1]
+    factor = 1.0 / jnp.exp2(13.0 - jnp.broadcast_to(exponent, (8, LANES)))[0:1, 0:1]
+    return real * factor, jnp.where(diagonal, 0.0, imaginary) * factor
+
+
+def other_kernel(far_ref, farthest_ref, out_ref):
+    diagonal = own_mask(lax.axis_index("l"), lax.axis_index("c"))
+    far, farthest = widened(far_ref, diagonal), widened(farthest_ref, diagonal)
+    for part in range(2):
+        out_ref[part] = far[part] + farthest[part]
+
+
+def merge_kernel(own_ref, near_ref, other_ref, out_ref):
+    near = widened(near_ref, own_mask(lax.axis_index("l"), lax.axis_index("c")))
+    mine = jnp.right_shift(lax.axis_index("l"), 1)
+    for part in range(2):
+        out_ref[mine, part] = own_ref[part] + near[part]
+        out_ref[1 - mine, part] = other_ref[part]
+
+
+def span_sum(keep, received):
+    rows = keep.shape[1:]
+
+    def exchange(values, step):
+        route = [(l, l ^ step) for l in range(CHIPS)]
+        return lax.ppermute(values.astype(jnp.float16), "l", route).astype(F32)
+
+    far, farthest, exponent = small(
+        far_kernel, [keep, received], [rows, rows, (8, LANES)]
+    )
+    farthest, far = exchange(farthest, 3), exchange(far, 2)
+    own, near = small(near_kernel, [keep, received, exponent], [rows, rows])
+    (other,) = small(other_kernel, [far, farthest], [rows])
+    (both,) = small(merge_kernel, [own, exchange(near, 1), other], [(2,) + rows])
     return jnp.transpose(both, (2, 0, 1, 3))
 
 
@@ -469,11 +518,9 @@
     )
     chunks = ready.reshape(4 * STATIONS, 2, 16, LANES)
     arrived = lax.all_to_all(chunks, ("z", "h", "x", "l"), 0, 0, tiled=True)
-    place = lax.axis_index("c").astype(jnp.int32).reshape(1)
     spectra = arrived.reshape(STATIONS, CHIPS, 2, 16, LANES)
-    received = lax.ppermute(gram(1, place, spectra), "c", [(0, 1), (1, 0)])
-    keep = gram(0, place, spectra)
-    return span_sum(combine(place, keep, received))
+    received = lax.ppermute(gram(1, spectra), "c", [(0, 1), (1, 0)])
+    return span_sum(gram(0, spectra), received)
 
 
 def solution(mesh):

time: 127 us -> 124 us (0.976)
  blocking collectives: 0 us -> 72 us
  waiting for transfers between devices: 65.3 us -> 8.59 us
  starting transfers between devices: 36.8 us -> 21 us
  other arithmetic: 1.58 us -> 0.12 us
    all_to_all x0 -> x1, blocking collectives: none -> 72 us  [on_device(): arrived = lax.all_to_all(chunks, ('z', 'h', 'x', 'l'), 0, 0, tiled=True)]
    all_to_all x2 -> x0, waiting for transfers between devices: 64.7 us -> none  [the longest x1 50.7 us: on_device(): arrived = lax.all_to_all(chunks, ('z', 'h', 'x', 'l'), 0, 0, tiled=True)]
    all_to_all x2 -> x0, starting transfers between devices: 25.1 us -> none  [the longest x1 21.5 us: on_device(): arrived = lax.all_to_all(chunks, ('z', 'h', 'x', 'l'), 0, 0, tiled=True)]
    ppermute x1 -> x4, starting transfers between devices: 5.02 us -> 14.3 us  [the longest x3 9.27 us: exchange(): return lax.ppermute(values.astype(jnp.float16), 'l', route).astype(F32)]
    ppermute x1 -> x4, waiting for transfers between devices: 0.52 us -> 8.58 us  [the longest x3 7.98 us: exchange(): return lax.ppermute(values.astype(jnp.float16), 'l', route).astype(F32)]
  transfers between devices with their start and end apart: 5 -> 6, of which waited for: 3 -> 2; matrix products, arithmetic and copies ran while one was open for 0% -> 0% of each run, Pallas kernels for 9% -> 10%
where the time goes in v5:
time: 124 us
  blocking collectives  72 us (58%)
  starting transfers between devices  21 us (17%)
  Pallas kernels  18.4 us (15%)
  waiting for transfers between devices  8.59 us (7%)
  local copies, waits for them, and re-layouts  3.48 us (3%)
    all_to_all x1, blocking collectives, on_device(): arrived = lax.all_to_all(chunks, ('z', 'h', 'x', 'l'), 0, 0, tiled=True)  72 us
    pallas_call x4, Pallas kernels, front(): pl.pallas_call(body, grid=(STEPS,), in_specs=[frame_spec(), frame_spec()]...  14.1 us
    ppermute x3, starting transfers between devices, exchange(): return lax.ppermute(values.astype(jnp.float16), 'l', route).astype(F32)  9.27 us
    ppermute x3, waiting for transfers between devices, exchange(): return lax.ppermute(values.astype(jnp.float16), 'l', route).astype(F32)  7.98 us
    ppermute x1, starting transfers between devices, on_device(): received = lax.ppermute(gram(1, spectra), 'c', [(0, 1), (1, 0)])  5.04 us
    ppermute x1, starting transfers between devices, on_device(): history_lower = lax.ppermute(late_lower, ('l', 'c'), forward)  4.73 us
    pallas_call x2, Pallas kernels, gram(): pl.pallas_call(functools.partial(gram_kernel, side), in_specs=[pl.BlockSp...  3.4 us
  transfers between devices with their start and end apart: 6, of which 2 were waited for; matrix products, arithmetic and copies ran while one was open for 0% of the time, Pallas kernels for 10%

profile of v5, /device:TPU:1, one launch (start us, length us, event | category | flops | bytes accessed | tf_op | source)
XLA Modules:
  0.0 123.8 jit_solution(757386640468893101)
XLA Ops:
  0.0 0.0 copy-start.1
  0.0 1.6 %copy-done.1 = bf16[8,32,2,2048]{3,2,1,0:T(2,128)(2,1)S(1)} copy-done((bf16[8,32,2,2048]{3,2,1,0:T(2,128)(2,1)S(1)}, bf16[8,32,2,2048]{3,2,1,0:T(2,128)(2,1)}, u32[]{:S(2)}) %copy-start.1) | copy-done | bytes 2097176
  1.6 0.2 shard_map.46
  1.8 0.0 copy-start
  1.8 0.0 copy-start.2
  1.8 0.0 copy-start.3
  1.8 0.2 copy.14
  2.0 4.7 %collective-permute-start.1 = (bf16[2,4,16,2048]{3,2,1,0:T(8,128)(2,1)S(1)}, bf16[2,4,16,2048]{3,2,1,0:T(8,128)(2,1)S(1)}, u32[]{:S(2)}, u32[]{:S(2)}) collective-permute-start(bf16[2,4,16,2048]{3,2,1,0:T(8,128)(2,1)S(1)} %bitcast.19), channel_id=1, source_target_pairs={{0,1},{1,2},{2,3},{3,4},{4,5},{5,6},{6,7},{8,9},{9,10},{10,11},{11... | collective-permute-start | bytes 1572872 | tf_op jit(solution)/shard_map/ppermute | solution.py:487
  6.7 0.2 copy.15
  6.9 1.9 %collective-permute-start = (bf16[2,4,16,2048]{3,2,1,0:T(8,128)(2,1)S(1)}, bf16[2,4,16,2048]{3,2,1,0:T(8,128)(2,1)S(1)}, u32[]{:S(2)}, u32[]{:S(2)}) collective-permute-start(bf16[2,4,16,2048]{3,2,1,0:T(8,128)(2,1)S(1)} %bitcast.14), channel_id=1, source_target_pairs={{0,1},{1,2},{2,3},{3,4},{4,5},{5,6},{6,7},{8,9},{9,10},{10,11},{11... | collective-permute-start | bytes 1572872 | tf_op jit(solution)/shard_map/ppermute | solution.py:488
  8.8 0.4 copy_bitcast_fusion.1
  9.2 0.0 copy-done
  9.2 0.0 copy-done.2
  9.2 0.0 copy-done.3
  9.2 3.6 %shard_map.47 = (bf16[4,256,256]{2,1,0:T(8,128)(2,1)S(1)}, f32[16,16,128]{2,1,0:T(8,128)S(1)}) custom-call(bf16[2,4,16,2048]{3,2,1,0:T(8,128)(2,1)S(1)} %get-tuple-element.27.hist_ref.cur_ref, bf16[2,4,16,2048]{3,2,1,0:T(8,128)(2,1)S(1)} %bitcast.20, f32[2,8,2048]{2,1,0:T(8,128)S(1)} %copy-done.3, f32[16,2304]{1,0:T(8,128)S(1)} %copy-done.2, ...), custom_call_target="tpu_custom_call" | custom-call | flops 700000000 | bytes 3145728 | tf_op jit(solution)/shard_map/pallas_call | solution.py:317
  12.8 3.7 %shard_map.49.mixed_ref = bf16[128,2,16,128]{3,2,1,0:T(8,128)(2,1)S(1)} custom-call(bf16[2,4,16,2048]{3,2,1,0:T(8,128)(2,1)S(1)} %get-tuple-element.28.hist_ref.cur_ref, bf16[2,4,16,2048]{3,2,1,0:T(8,128)(2,1)S(1)} %bitcast.15, f32[16,16,128]{2,1,0:T(8,128)S(1)} %get-tuple-element.20.gain_ref, f32[16,2304]{1,0:T(8,128)S(1)} %copy-done.2, ...), custom_call_target="tpu_custom_call" | custom-call | flops 700000000 | bytes 3145728 | tf_op jit(solution)/shard_map/pallas_call | solution.py:317
  16.6 0.0 collective-permute-done.1.hist_ref
  16.6 2.9 %shard_map.48.lower_ref = bf16[4,256,256]{2,1,0:T(8,128)(2,1)S(1)} custom-call(bf16[2,4,16,2048]{3,2,1,0:T(8,128)(2,1)S(1)} %collective-permute-done.1.hist_ref, bf16[2,4,16,2048]{3,2,1,0:T(8,128)(2,1)S(1)} %get-tuple-element.27.hist_ref.cur_ref, f32[16,16,128]{2,1,0:T(8,128)S(1)} %get-tuple-element.20.gain_ref, f32[16,2304]{1,0:T(8,128)S(1)} %copy-done.2, ...), custom_call_target="tpu_custom_call" | custom-call | flops 700000000 | bytes 3145728 | tf_op jit(solution)/shard_map/pallas_call | solution.py:317
  19.5 0.0 collective-permute-done.hist_ref
  19.5 3.9 %shard_map.50 = bf16[128,2,2,16,128]{4,3,2,1,0:T(8,128)(2,1)S(1)} custom-call(bf16[2,4,16,2048]{3,2,1,0:T(8,128)(2,1)S(1)} %collective-permute-done.hist_ref, bf16[2,4,16,2048]{3,2,1,0:T(8,128)(2,1)S(1)} %get-tuple-element.28.hist_ref.cur_ref, f32[16,16,128]{2,1,0:T(8,128)S(1)} %get-tuple-element.20.gain_ref, f32[16,2304]{1,0:T(8,128)S(1)} %copy-done.2, ...), custom_call_target="tpu_custom_call" | custom-call | flops 700000000 | bytes 3145728 | tf_op jit(solution)/shard_map/pallas_call | solution.py:317
  23.4 72.0 %all_to_all.5 = bf16[256,2,16,128]{3,2,1,0:T(8,128)(2,1)S(1)} all-to-all(bf16[256,2,16,128]{3,2,1,0:T(8,128)(2,1)S(1)} %bitcast.13), channel_id=1, replica_groups=mesh['z'=8,'h'=2,'x'=4,'l'=4,'c'=2] {'z','h','x','l'}, dimensions={0} | all-to-all | bytes 4194304 | tf_op jit(solution)/shard_map/all_to_all | solution.py:520
  95.4 1.8 %shard_map.52 = f32[4,2,64,512]{3,2,1,0:T(8,128)S(1)} custom-call(bf16[64,4,2,16,128]{4,3,2,1,0:T(8,128)(2,1)S(1)} %bitcast.16), custom_call_target="tpu_custom_call" | custom-call | flops 1100000000 | bytes 4194304 | tf_op jit(solution)/shard_map/pallas_call | solution.py:373
  97.1 5.0 %collective-permute-start.2 = (f32[4,2,64,512]{3,2,1,0:T(8,128)S(1)}, f32[4,2,64,512]{3,2,1,0:T(8,128)S(1)}, u32[]{:S(2)}, u32[]{:S(2)}) collective-permute-start(f32[4,2,64,512]{3,2,1,0:T(8,128)S(1)} %shard_map.52), channel_id=1, source_target_pairs={{0,1},{1,0},{2,3},{3,2},{4,5},{5,4},{6,7},{7,6},{8,9},{9,8},{10,11... | collective-permute-start | bytes 3145736 | tf_op jit(solution)/shard_map/ppermute | solution.py:522
  102.2 1.7 %shard_map.51.keep_ref = f32[4,2,64,512]{3,2,1,0:T(8,128)S(1)} custom-call(bf16[64,4,2,16,128]{4,3,2,1,0:T(8,128)(2,1)S(1)} %bitcast.17), custom_call_target="tpu_custom_call" | custom-call | flops 1100000000 | bytes 4194304 | tf_op jit(solution)/shard_map/pallas_call | solution.py:373
  103.8 0.6 collective-permute-done.2.received_ref
  104.4 0.3 shard_map.53
  104.8 4.1 %collective-permute-start.5 = (f16[2,64,512]{2,1,0:T(8,128)(2,1)S(1)}, f16[2,64,512]{2,1,0:T(8,128)(2,1)S(1)}, u32[]{:S(2)}, u32[]{:S(2)}) collective-permute-start(f16[2,64,512]{2,1,0:T(8,128)(2,1)S(1)} %convert_element_type.22), channel_id=1, source_target_pairs={{0,6},{2,4},{4,2},{6,0},{1,7},{3,5},{5,3},{7,1},{8,14},{10,12},{12... | collective-permute-start | bytes 393224 | tf_op jit(solution)/shard_map/ppermute | solution.py:468
  108.8 3.0 %collective-permute-start.4 = (f16[2,64,512]{2,1,0:T(8,128)(2,1)S(1)}, f16[2,64,512]{2,1,0:T(8,128)(2,1)S(1)}, u32[]{:S(2)}, u32[]{:S(2)}) collective-permute-start(f16[2,64,512]{2,1,0:T(8,128)(2,1)S(1)} %convert_element_type.20), channel_id=1, source_target_pairs={{0,4},{2,6},{4,0},{6,2},{1,5},{3,7},{5,1},{7,3},{8,12},{10,14},{12... | collective-permute-start | bytes 393224 | tf_op jit(solution)/shard_map/ppermute | solution.py:468
  111.8 0.1 shard_map.54
  111.9 2.2 %collective-permute-start.3 = (f16[2,64,512]{2,1,0:T(8,128)(2,1)S(1)}, f16[2,64,512]{2,1,0:T(8,128)(2,1)S(1)}, u32[]{:S(2)}, u32[]{:S(2)}) collective-permute-start(f16[2,64,512]{2,1,0:T(8,128)(2,1)S(1)} %convert_element_type.18), channel_id=1, source_target_pairs={{0,2},{2,0},{4,6},{6,4},{1,3},{3,1},{5,7},{7,5},{8,10},{10,8},{12,... | collective-permute-start | bytes 393224 | tf_op jit(solution)/shard_map/ppermute | solution.py:468
  114.2 0.0 collective-permute-done.5
  114.2 8.0 %collective-permute-done.4 = f16[2,64,512]{2,1,0:T(8,128)(2,1)S(1)} collective-permute-done((f16[2,64,512]{2,1,0:T(8,128)(2,1)S(1)}, f16[2,64,512]{2,1,0:T(8,128)(2,1)S(1)}, u32[]{:S(2)}, u32[]{:S(2)}) %collective-permute-start.4) | collective-permute-done | bytes 131104 | tf_op jit(solution)/shard_map/ppermute | solution.py:468
  122.2 0.2 shard_map.55.other_ref
  122.4 0.0 collective-permute-done.3
  122.4 0.2 shard_map.56
  122.6 1.2 copy.9
  (6 shorter events, 0.1 us)
Async XLA Ops:
  0.0 1.6 %copy-start.1 = (bf16[8,32,2,2048]{3,2,1,0:T(2,128)(2,1)S(1)}, bf16[8,32,2,2048]{3,2,1,0:T(2,128)(2,1)}, u32[]{:S(2)}) copy-start(bf16[8,32,2,2048]{3,2,1,0:T(2,128)(2,1)} %voltages_ref.1) | copy-start | bytes 6291460
  1.8 7.4 %copy-start = (bf16[5,256,256]{2,1,0:T(8,128)(2,1)S(1)}, bf16[5,256,256]{2,1,0:T(8,128)(2,1)}, u32[]{:S(2)}) copy-start(bf16[5,256,256]{2,1,0:T(8,128)(2,1)} %constant.5.clone.matrix_ref) | copy-start | bytes 1966084
  1.8 7.4 %copy-start.2 = (f32[16,2304]{1,0:T(8,128)S(1)}, f32[16,2304]{1,0:T(8,128)}, u32[]{:S(2)}) copy-start(f32[16,2304]{1,0:T(8,128)} %constant.4.clone.vector_ref) | copy-start | bytes 442372
  1.8 7.4 %copy-start.3 = (f32[2,8,2048]{2,1,0:T(8,128)S(1)}, f32[2,8,2048]{2,1,0:T(8,128)}, u32[]{:S(2)}) copy-start(f32[2,8,2048]{2,1,0:T(8,128)} %gain_ref.1) | copy-start | bytes 393220
  2.0 14.6 %collective-permute-start.1 = (bf16[2,4,16,2048]{3,2,1,0:T(8,128)(2,1)S(1)}, bf16[2,4,16,2048]{3,2,1,0:T(8,128)(2,1)S(1)}, u32[]{:S(2)}, u32[]{:S(2)}) collective-permute-start(bf16[2,4,16,2048]{3,2,1,0:T(8,128)(2,1)S(1)} %bitcast.19), channel_id=1, source_target_pairs={{0,1},{1,2},{2,3},{3,4},{4,5},{5,6},{6,7},{8,9},{9,10},{10,11},{11... | collective-permute-start | bytes 1572872 | tf_op jit(solution)/shard_map/ppermute | solution.py:487
  6.9 12.6 %collective-permute-start = (bf16[2,4,16,2048]{3,2,1,0:T(8,128)(2,1)S(1)}, bf16[2,4,16,2048]{3,2,1,0:T(8,128)(2,1)S(1)}, u32[]{:S(2)}, u32[]{:S(2)}) collective-permute-start(bf16[2,4,16,2048]{3,2,1,0:T(8,128)(2,1)S(1)} %bitcast.14), channel_id=1, source_target_pairs={{0,1},{1,2},{2,3},{3,4},{4,5},{5,6},{6,7},{8,9},{9,10},{10,11},{11... | collective-permute-start | bytes 1572872 | tf_op jit(solution)/shard_map/ppermute | solution.py:488
  97.1 7.3 %collective-permute-start.2 = (f32[4,2,64,512]{3,2,1,0:T(8,128)S(1)}, f32[4,2,64,512]{3,2,1,0:T(8,128)S(1)}, u32[]{:S(2)}, u32[]{:S(2)}) collective-permute-start(f32[4,2,64,512]{3,2,1,0:T(8,128)S(1)} %shard_map.52), channel_id=1, source_target_pairs={{0,1},{1,0},{2,3},{3,2},{4,5},{5,4},{6,7},{7,6},{8,9},{9,8},{10,11... | collective-permute-start | bytes 3145736 | tf_op jit(solution)/shard_map/ppermute | solution.py:522
  104.8 9.4 %collective-permute-start.5 = (f16[2,64,512]{2,1,0:T(8,128)(2,1)S(1)}, f16[2,64,512]{2,1,0:T(8,128)(2,1)S(1)}, u32[]{:S(2)}, u32[]{:S(2)}) collective-permute-start(f16[2,64,512]{2,1,0:T(8,128)(2,1)S(1)} %convert_element_type.22), channel_id=1, source_target_pairs={{0,6},{2,4},{4,2},{6,0},{1,7},{3,5},{5,3},{7,1},{8,14},{10,12},{12... | collective-permute-start | bytes 393224 | tf_op jit(solution)/shard_map/ppermute | solution.py:468
  108.8 13.4 %collective-permute-start.4 = (f16[2,64,512]{2,1,0:T(8,128)(2,1)S(1)}, f16[2,64,512]{2,1,0:T(8,128)(2,1)S(1)}, u32[]{:S(2)}, u32[]{:S(2)}) collective-permute-start(f16[2,64,512]{2,1,0:T(8,128)(2,1)S(1)} %convert_element_type.20), channel_id=1, source_target_pairs={{0,4},{2,6},{4,0},{6,2},{1,5},{3,7},{5,1},{7,3},{8,12},{10,14},{12... | collective-permute-start | bytes 393224 | tf_op jit(solution)/shard_map/ppermute | solution.py:468
  111.9 10.5 %collective-permute-start.3 = (f16[2,64,512]{2,1,0:T(8,128)(2,1)S(1)}, f16[2,64,512]{2,1,0:T(8,128)(2,1)S(1)}, u32[]{:S(2)}, u32[]{:S(2)}) collective-permute-start(f16[2,64,512]{2,1,0:T(8,128)(2,1)S(1)} %convert_element_type.18), channel_id=1, source_target_pairs={{0,2},{2,0},{4,6},{6,4},{1,3},{3,1},{5,7},{7,5},{8,10},{10,8},{12,... | collective-permute-start | bytes 393224 | tf_op jit(solution)/shard_map/ppermute | solution.py:468

commit v6 on v5

--- a/solution.py
+++ b/solution.py
@@ -17,7 +17,7 @@
 HALF = 16
 INPUTS_DEV = 8
 GROUP = 4
-STEPS = 2
+STEPS = 1
 STATIONS = 64
 CHIPS = 4
 MIB = 1024 * 1024
@@ -45,19 +45,17 @@
     full = full.astype(np.float32)
     high = full.astype(ml_dtypes.bfloat16)
     low = (full - high.astype(np.float32)).astype(ml_dtypes.bfloat16)
-    turn = np.zeros((256, 256), np.float32)
     mix = np.zeros((256, 256), np.float32)
     comb = np.zeros((256, 256), np.float32)
-    for c in range(2):
-        for k2 in range(LANES):
-            turn[2 * k2 + c, c * LANES + k2] = 1.0
     for i in range(INPUTS_DEV):
-        for q in range(32):
-            mix[q * INPUTS_DEV + i, i * 32 + q] = 1.0
+        for c in range(2):
+            for k2 in range(16):
+                row = (2 * k2 + c) * INPUTS_DEV + i
+                mix[row, (i // GROUP) * 128 + c * 64 + (i % GROUP) * 16 + k2] = 1.0
     for k1 in range(RADIX):
         for j in range(8):
             comb[j * RADIX + k1, k1 * 8 + j] = 1.0
-    orders = np.stack([turn, mix, comb]).astype(ml_dtypes.bfloat16)
+    orders = np.stack([mix, comb]).astype(ml_dtypes.bfloat16)
     return np.concatenate([np.stack([high, low]), orders])
 
 
@@ -95,7 +93,7 @@
 
 
 def arrange_gains(gain_ref, matrix_ref, arranged_ref):
-    comb = matrix_ref[4, 0:LANES, 0:LANES]
+    comb = matrix_ref[3, 0:LANES, 0:LANES]
     dot = functools.partial(jnp.dot, preferred_element_type=F32)
     both = gain_ref[...].reshape(2 * INPUTS_DEV, CHANNELS)
     high = both.astype(BF16)
@@ -120,8 +118,8 @@
         arranged_ref[k1] = pieces[k1]
 
 
-def analyse(hist_ref, cur_ref, j, stage, scratch):
-    window, twist, ext, filtered = scratch
+def analyse(hist_ref, cur_ref, j, vector_ref, stage, scratch):
+    ext, filtered = scratch
     for n1 in range(RADIX):
         lanes = slice(n1 * LANES, (n1 + 1) * LANES)
         for c in range(2):
@@ -131,7 +129,7 @@
         lanes = slice(n1 * LANES, (n1 + 1) * LANES)
         sums = [None] * 4
         for t in range(TAPS):
-            weight = window[t, :, lanes]
+            weight = vector_ref[t : t + 1, lanes]
             for c in range(2):
                 for block in range(2):
                     begin = block * 8 + 1 + t
@@ -144,7 +142,8 @@
     for block in range(2):
         values = [(filtered[block, n1, 0], filtered[block, n1, 1]) for n1 in range(RADIX)]
         for k1, (re, im) in enumerate(radix16(values)):
-            cosine, sine = twist[k1, 0], twist[k1, 1]
+            cosine = vector_ref[k1 : k1 + 1, CHANNELS : CHANNELS + LANES]
+            sine = vector_ref[k1 : k1 + 1, CHANNELS + LANES : CHANNELS + 2 * LANES]
             rows = slice(k1 * HALF + block * 8, k1 * HALF + block * 8 + 8)
             stage[rows, 0:LANES] = re * cosine - im * sine
             stage[rows, LANES : 2 * LANES] = re * sine + im * cosine
@@ -165,25 +164,19 @@
             gain_im = gain_ref[k1, INPUTS_DEV + place : INPUTS_DEV + place + 1, :]
             equal[rows, 0:LANES] = (re * gain_re - im * gain_im).astype(BF16)
             equal[rows, LANES : 2 * LANES] = (re * gain_im + im * gain_re).astype(BF16)
-    across = lax.dot_general(
-        matrix_ref[2], equal[...], (((1,), (1,)), ((), ())), preferred_element_type=F32
-    ).astype(BF16)
+    across = jnp.transpose(equal[...].astype(F32)).astype(BF16)
     for i in range(GROUP):
         turned[i] = across[:, i * 256 : (i + 1) * 256]
 
 
 def filter_transform(hist_ref, cur_ref, gain_ref, vector_ref, matrix_ref, first, turned, scratch):
-    window, twist, ext, filtered, stage, result, equal = scratch
+    ext, filtered, stage, result, equal = scratch
     step = pl.program_id(0)
-
-    @pl.when(step == 0)
-    def _():
-        spread_tables(vector_ref, window, twist)
 
     for j in range(GROUP // STEPS):
         rows = pl.ds(pl.multiple_of((step * (GROUP // STEPS) + j) * 256, 256), 256)
         analyse(
-            hist_ref, cur_ref, j, stage.at[rows], (window, twist, ext.at[j], filtered.at[j])
+            hist_ref, cur_ref, j, vector_ref, stage.at[rows], (ext.at[j], filtered.at[j])
         )
 
     @pl.when(step == STEPS - 1)
@@ -191,22 +184,14 @@
         finish(gain_ref, matrix_ref, turned, first, stage, result, equal)
 
 
-def spread_tables(vector_ref, window, twist):
-    for t in range(TAPS):
-        window[t] = jnp.broadcast_to(vector_ref[t : t + 1, 0:CHANNELS], (8, CHANNELS))
-        for c in range(2):
-            begin = CHANNELS + c * LANES
-            twist[t, c] = jnp.broadcast_to(
-                vector_ref[t : t + 1, begin : begin + LANES], (8, LANES)
-            )
-
-
 def mix(matrix_ref, lower, upper, group):
-    part = slice(group * 32, (group + 1) * 32)
-    piece = jnp.concatenate(
-        [lower[:, part, :].reshape(128, 256), upper[:, part, :].reshape(128, 256)], axis=0
-    )
-    return jnp.dot(matrix_ref[3], piece, preferred_element_type=F32).astype(BF16)
+    slabs = [
+        half[:, c * LANES + group * 16 : c * LANES + (group + 1) * 16, :].reshape(64, 256)
+        for half in (lower, upper)
+        for c in range(2)
+    ]
+    piece = jnp.concatenate(slabs, axis=0)
+    return jnp.dot(matrix_ref[2], piece, preferred_element_type=F32).astype(BF16)
 
 
 def mix_all(matrix_ref, lower, upper, out_ref):
@@ -322,8 +307,6 @@
         out_shape=out_shapes,
         scratch_shapes=[
             *own_scratch,
-            pltpu.VMEM((TAPS, 8, CHANNELS), F32),
-            pltpu.VMEM((RADIX, 2, 8, LANES), F32),
             pltpu.VMEM((GROUP // STEPS, RADIX, 2, 2 * HALF, LANES), F32),
             pltpu.VMEM((GROUP // STEPS, 2, RADIX, 2, 8, LANES), F32),
             pltpu.VMEM((GROUP * 256, 256), F32),

time: 124 us -> 122 us (0.984)
  Pallas kernels: 18.4 us -> 14.8 us
  waiting for transfers between devices: 8.59 us -> 10.4 us
    pallas_call x4, Pallas kernels: 14.1 us -> 10.6 us  [front(): pl.pallas_call(body, grid=(STEPS,), in_specs=[frame_spec(), frame_spec()]...]
    ppermute x1, waiting for transfers between devices: 0.01 us -> 1.73 us  [on_device(): history_upper = lax.ppermute(late_upper, ('l', 'c'), forward)]
  transfers between devices with their start and end apart: 6 -> 6, of which waited for: 2 -> 3; matrix products, arithmetic and copies ran while one was open for 0% -> 0% of each run, Pallas kernels for 10% -> 8%
where the time goes in v6:
time: 122 us
  blocking collectives  71.1 us (58%)
  starting transfers between devices  21.8 us (18%)
  Pallas kernels  14.8 us (12%)
  waiting for transfers between devices  10.4 us (9%)
  local copies, waits for them, and re-layouts  3.48 us (3%)
    all_to_all x1, blocking collectives, on_device(): arrived = lax.all_to_all(chunks, ('z', 'h', 'x', 'l'), 0, 0, tiled=True)  71.1 us
    pallas_call x4, Pallas kernels, front(): pl.pallas_call(body, grid=(STEPS,), in_specs=[frame_spec(), frame_spec()]...  10.6 us
    ppermute x3, starting transfers between devices, exchange(): return lax.ppermute(values.astype(jnp.float16), 'l', route).astype(F32)  9.27 us
    ppermute x3, waiting for transfers between devices, exchange(): return lax.ppermute(values.astype(jnp.float16), 'l', route).astype(F32)  8.1 us
    ppermute x1, starting transfers between devices, on_device(): received = lax.ppermute(gram(1, spectra), 'c', [(0, 1), (1, 0)])  5.92 us
    ppermute x1, starting transfers between devices, on_device(): history_lower = lax.ppermute(late_lower, ('l', 'c'), forward)  4.73 us
    pallas_call x2, Pallas kernels, gram(): pl.pallas_call(functools.partial(gram_kernel, side), in_specs=[pl.BlockSp...  3.41 us
  transfers between devices with their start and end apart: 6, of which 3 were waited for; matrix products, arithmetic and copies ran while one was open for 0% of the time, Pallas kernels for 8%

profile of v6, /device:TPU:1, one launch (start us, length us, event | category | flops | bytes accessed | tf_op | source)
XLA Modules:
  0.0 122.1 jit_solution(9680571950005182011)
XLA Ops:
  0.0 0.0 copy-start
  0.0 1.6 %copy-done = bf16[8,32,2,2048]{3,2,1,0:T(2,128)(2,1)S(1)} copy-done((bf16[8,32,2,2048]{3,2,1,0:T(2,128)(2,1)S(1)}, bf16[8,32,2,2048]{3,2,1,0:T(2,128)(2,1)}, u32[]{:S(2)}) %copy-start) | copy-done | bytes 2097176
  1.6 0.2 shard_map.46
  1.8 0.0 copy-start.1
  1.8 0.0 copy-start.2
  1.8 0.0 copy-start.3
  1.8 0.2 copy.14
  2.0 4.7 %collective-permute-start.1 = (bf16[2,4,16,2048]{3,2,1,0:T(8,128)(2,1)S(1)}, bf16[2,4,16,2048]{3,2,1,0:T(8,128)(2,1)S(1)}, u32[]{:S(2)}, u32[]{:S(2)}) collective-permute-start(bf16[2,4,16,2048]{3,2,1,0:T(8,128)(2,1)S(1)} %bitcast.19), channel_id=1, source_target_pairs={{0,1},{1,2},{2,3},{3,4},{4,5},{5,6},{6,7},{8,9},{9,10},{10,11},{11... | collective-permute-start | bytes 1572872 | tf_op jit(solution)/shard_map/ppermute | solution.py:470
  6.7 0.2 copy.15
  6.9 1.9 %collective-permute-start = (bf16[2,4,16,2048]{3,2,1,0:T(8,128)(2,1)S(1)}, bf16[2,4,16,2048]{3,2,1,0:T(8,128)(2,1)S(1)}, u32[]{:S(2)}, u32[]{:S(2)}) collective-permute-start(bf16[2,4,16,2048]{3,2,1,0:T(8,128)(2,1)S(1)} %bitcast.17), channel_id=1, source_target_pairs={{0,1},{1,2},{2,3},{3,4},{4,5},{5,6},{6,7},{8,9},{9,10},{10,11},{11... | collective-permute-start | bytes 1572872 | tf_op jit(solution)/shard_map/ppermute | solution.py:471
  8.8 0.4 copy_bitcast_fusion.1
  9.2 0.0 copy-done.1
  9.2 0.0 copy-done.2
  9.2 0.0 copy-done.3
  9.2 2.5 %shard_map.47 = (bf16[4,256,256]{2,1,0:T(8,128)(2,1)S(1)}, f32[16,16,128]{2,1,0:T(8,128)S(1)}) custom-call(bf16[2,4,16,2048]{3,2,1,0:T(8,128)(2,1)S(1)} %get-tuple-element.27.hist_ref.cur_ref, bf16[2,4,16,2048]{3,2,1,0:T(8,128)(2,1)S(1)} %bitcast.20, f32[2,8,2048]{2,1,0:T(8,128)S(1)} %copy-done.3, f32[16,2304]{1,0:T(8,128)S(1)} %copy-done.2, ...), custom_call_target="tpu_custom_call" | custom-call | flops 700000000 | bytes 3145728 | tf_op jit(solution)/shard_map/pallas_call | solution.py:302
  11.7 2.9 %shard_map.49.mixed_ref = bf16[128,2,16,128]{3,2,1,0:T(8,128)(2,1)S(1)} custom-call(bf16[2,4,16,2048]{3,2,1,0:T(8,128)(2,1)S(1)} %get-tuple-element.28.hist_ref.cur_ref, bf16[2,4,16,2048]{3,2,1,0:T(8,128)(2,1)S(1)} %bitcast.18, f32[16,16,128]{2,1,0:T(8,128)S(1)} %get-tuple-element.20.gain_ref, f32[16,2304]{1,0:T(8,128)S(1)} %copy-done.2, ...), custom_call_target="tpu_custom_call" | custom-call | flops 700000000 | bytes 3145728 | tf_op jit(solution)/shard_map/pallas_call | solution.py:302
  14.6 0.0 collective-permute-done.1.hist_ref
  14.6 2.1 %shard_map.48.lower_ref = bf16[4,256,256]{2,1,0:T(8,128)(2,1)S(1)} custom-call(bf16[2,4,16,2048]{3,2,1,0:T(8,128)(2,1)S(1)} %collective-permute-done.1.hist_ref, bf16[2,4,16,2048]{3,2,1,0:T(8,128)(2,1)S(1)} %get-tuple-element.27.hist_ref.cur_ref, f32[16,16,128]{2,1,0:T(8,128)S(1)} %get-tuple-element.20.gain_ref, f32[16,2304]{1,0:T(8,128)S(1)} %copy-done.2, ...), custom_call_target="tpu_custom_call" | custom-call | flops 700000000 | bytes 3145728 | tf_op jit(solution)/shard_map/pallas_call | solution.py:302
  16.7 1.7 %collective-permute-done.hist_ref = bf16[2,4,16,2048]{3,2,1,0:T(8,128)(2,1)S(1)} collective-permute-done((bf16[2,4,16,2048]{3,2,1,0:T(8,128)(2,1)S(1)}, bf16[2,4,16,2048]{3,2,1,0:T(8,128)(2,1)S(1)}, u32[]{:S(2)}, u32[]{:S(2)}) %collective-permute-start) | collective-permute-done | bytes 524320 | tf_op jit(solution)/shard_map/ppermute | solution.py:471
  18.4 3.1 %shard_map.50 = bf16[128,2,2,16,128]{4,3,2,1,0:T(8,128)(2,1)S(1)} custom-call(bf16[2,4,16,2048]{3,2,1,0:T(8,128)(2,1)S(1)} %collective-permute-done.hist_ref, bf16[2,4,16,2048]{3,2,1,0:T(8,128)(2,1)S(1)} %get-tuple-element.28.hist_ref.cur_ref, f32[16,16,128]{2,1,0:T(8,128)S(1)} %get-tuple-element.20.gain_ref, f32[16,2304]{1,0:T(8,128)S(1)} %copy-done.2, ...), custom_call_target="tpu_custom_call" | custom-call | flops 700000000 | bytes 3145728 | tf_op jit(solution)/shard_map/pallas_call | solution.py:302
  21.5 71.1 %all_to_all.5 = bf16[256,2,16,128]{3,2,1,0:T(8,128)(2,1)S(1)} all-to-all(bf16[256,2,16,128]{3,2,1,0:T(8,128)(2,1)S(1)} %bitcast.13), channel_id=1, replica_groups=mesh['z'=8,'h'=2,'x'=4,'l'=4,'c'=2] {'z','h','x','l'}, dimensions={0} | all-to-all | bytes 4194304 | tf_op jit(solution)/shard_map/all_to_all | solution.py:503
  92.7 1.8 %shard_map.52 = f32[4,2,64,512]{3,2,1,0:T(8,128)S(1)} custom-call(bf16[64,4,2,16,128]{4,3,2,1,0:T(8,128)(2,1)S(1)} %bitcast.14), custom_call_target="tpu_custom_call" | custom-call | flops 1100000000 | bytes 4194304 | tf_op jit(solution)/shard_map/pallas_call | solution.py:356
  94.4 5.9 %collective-permute-start.2 = (f32[4,2,64,512]{3,2,1,0:T(8,128)S(1)}, f32[4,2,64,512]{3,2,1,0:T(8,128)S(1)}, u32[]{:S(2)}, u32[]{:S(2)}) collective-permute-start(f32[4,2,64,512]{3,2,1,0:T(8,128)S(1)} %shard_map.52), channel_id=1, source_target_pairs={{0,1},{1,0},{2,3},{3,2},{4,5},{5,4},{6,7},{7,6},{8,9},{9,8},{10,11... | collective-permute-start | bytes 3145736 | tf_op jit(solution)/shard_map/ppermute | solution.py:505
  100.4 1.7 %shard_map.51.keep_ref = f32[4,2,64,512]{3,2,1,0:T(8,128)S(1)} custom-call(bf16[64,4,2,16,128]{4,3,2,1,0:T(8,128)(2,1)S(1)} %bitcast.15), custom_call_target="tpu_custom_call" | custom-call | flops 1100000000 | bytes 4194304 | tf_op jit(solution)/shard_map/pallas_call | solution.py:356
  102.0 0.6 collective-permute-done.2.received_ref
  102.6 0.3 shard_map.53
  103.0 4.2 %collective-permute-start.5 = (f16[2,64,512]{2,1,0:T(8,128)(2,1)S(1)}, f16[2,64,512]{2,1,0:T(8,128)(2,1)S(1)}, u32[]{:S(2)}, u32[]{:S(2)}) collective-permute-start(f16[2,64,512]{2,1,0:T(8,128)(2,1)S(1)} %convert_element_type.22), channel_id=1, source_target_pairs={{0,6},{2,4},{4,2},{6,0},{1,7},{3,5},{5,3},{7,1},{8,14},{10,12},{12... | collective-permute-start | bytes 393224 | tf_op jit(solution)/shard_map/ppermute | solution.py:451
  107.2 2.9 %collective-permute-start.4 = (f16[2,64,512]{2,1,0:T(8,128)(2,1)S(1)}, f16[2,64,512]{2,1,0:T(8,128)(2,1)S(1)}, u32[]{:S(2)}, u32[]{:S(2)}) collective-permute-start(f16[2,64,512]{2,1,0:T(8,128)(2,1)S(1)} %convert_element_type.20), channel_id=1, source_target_pairs={{0,4},{2,6},{4,0},{6,2},{1,5},{3,7},{5,1},{7,3},{8,12},{10,14},{12... | collective-permute-start | bytes 393224 | tf_op jit(solution)/shard_map/ppermute | solution.py:451
  110.1 0.1 shard_map.54
  110.3 2.1 %collective-permute-start.3 = (f16[2,64,512]{2,1,0:T(8,128)(2,1)S(1)}, f16[2,64,512]{2,1,0:T(8,128)(2,1)S(1)}, u32[]{:S(2)}, u32[]{:S(2)}) collective-permute-start(f16[2,64,512]{2,1,0:T(8,128)(2,1)S(1)} %convert_element_type.18), channel_id=1, source_target_pairs={{0,2},{2,0},{4,6},{6,4},{1,3},{3,1},{5,7},{7,5},{8,10},{10,8},{12,... | collective-permute-start | bytes 393224 | tf_op jit(solution)/shard_map/ppermute | solution.py:451
  112.4 0.0 collective-permute-done.5
  112.4 8.1 %collective-permute-done.4 = f16[2,64,512]{2,1,0:T(8,128)(2,1)S(1)} collective-permute-done((f16[2,64,512]{2,1,0:T(8,128)(2,1)S(1)}, f16[2,64,512]{2,1,0:T(8,128)(2,1)S(1)}, u32[]{:S(2)}, u32[]{:S(2)}) %collective-permute-start.4) | collective-permute-done | bytes 131104 | tf_op jit(solution)/shard_map/ppermute | solution.py:451
  120.5 0.2 shard_map.55.other_ref
  120.7 0.0 collective-permute-done.3
  120.7 0.2 shard_map.56
  120.9 1.2 copy.9
  (6 shorter events, 0.1 us)
Async XLA Ops:
  0.0 1.6 %copy-start = (bf16[8,32,2,2048]{3,2,1,0:T(2,128)(2,1)S(1)}, bf16[8,32,2,2048]{3,2,1,0:T(2,128)(2,1)}, u32[]{:S(2)}) copy-start(bf16[8,32,2,2048]{3,2,1,0:T(2,128)(2,1)} %voltages_ref.1) | copy-start | bytes 6291460
  1.8 7.4 %copy-start.1 = (bf16[4,256,256]{2,1,0:T(8,128)(2,1)S(1)}, bf16[4,256,256]{2,1,0:T(8,128)(2,1)}, u32[]{:S(2)}) copy-start(bf16[4,256,256]{2,1,0:T(8,128)(2,1)} %constant.5.clone.matrix_ref) | copy-start | bytes 1572868
  1.8 7.4 %copy-start.2 = (f32[16,2304]{1,0:T(8,128)S(1)}, f32[16,2304]{1,0:T(8,128)}, u32[]{:S(2)}) copy-start(f32[16,2304]{1,0:T(8,128)} %constant.4.clone.vector_ref) | copy-start | bytes 442372
  1.8 7.4 %copy-start.3 = (f32[2,8,2048]{2,1,0:T(8,128)S(1)}, f32[2,8,2048]{2,1,0:T(8,128)}, u32[]{:S(2)}) copy-start(f32[2,8,2048]{2,1,0:T(8,128)} %gain_ref.1) | copy-start | bytes 393220
  2.0 12.6 %collective-permute-start.1 = (bf16[2,4,16,2048]{3,2,1,0:T(8,128)(2,1)S(1)}, bf16[2,4,16,2048]{3,2,1,0:T(8,128)(2,1)S(1)}, u32[]{:S(2)}, u32[]{:S(2)}) collective-permute-start(bf16[2,4,16,2048]{3,2,1,0:T(8,128)(2,1)S(1)} %bitcast.19), channel_id=1, source_target_pairs={{0,1},{1,2},{2,3},{3,4},{4,5},{5,6},{6,7},{8,9},{9,10},{10,11},{11... | collective-permute-start | bytes 1572872 | tf_op jit(solution)/shard_map/ppermute | solution.py:470
  6.9 11.6 %collective-permute-start = (bf16[2,4,16,2048]{3,2,1,0:T(8,128)(2,1)S(1)}, bf16[2,4,16,2048]{3,2,1,0:T(8,128)(2,1)S(1)}, u32[]{:S(2)}, u32[]{:S(2)}) collective-permute-start(bf16[2,4,16,2048]{3,2,1,0:T(8,128)(2,1)S(1)} %bitcast.17), channel_id=1, source_target_pairs={{0,1},{1,2},{2,3},{3,4},{4,5},{5,6},{6,7},{8,9},{9,10},{10,11},{11... | collective-permute-start | bytes 1572872 | tf_op jit(solution)/shard_map/ppermute | solution.py:471
  94.4 8.2 %collective-permute-start.2 = (f32[4,2,64,512]{3,2,1,0:T(8,128)S(1)}, f32[4,2,64,512]{3,2,1,0:T(8,128)S(1)}, u32[]{:S(2)}, u32[]{:S(2)}) collective-permute-start(f32[4,2,64,512]{3,2,1,0:T(8,128)S(1)} %shard_map.52), channel_id=1, source_target_pairs={{0,1},{1,0},{2,3},{3,2},{4,5},{5,4},{6,7},{7,6},{8,9},{9,8},{10,11... | collective-permute-start | bytes 3145736 | tf_op jit(solution)/shard_map/ppermute | solution.py:505
  103.0 9.4 %collective-permute-start.5 = (f16[2,64,512]{2,1,0:T(8,128)(2,1)S(1)}, f16[2,64,512]{2,1,0:T(8,128)(2,1)S(1)}, u32[]{:S(2)}, u32[]{:S(2)}) collective-permute-start(f16[2,64,512]{2,1,0:T(8,128)(2,1)S(1)} %convert_element_type.22), channel_id=1, source_target_pairs={{0,6},{2,4},{4,2},{6,0},{1,7},{3,5},{5,3},{7,1},{8,14},{10,12},{12... | collective-permute-start | bytes 393224 | tf_op jit(solution)/shard_map/ppermute | solution.py:451
  107.2 13.3 %collective-permute-start.4 = (f16[2,64,512]{2,1,0:T(8,128)(2,1)S(1)}, f16[2,64,512]{2,1,0:T(8,128)(2,1)S(1)}, u32[]{:S(2)}, u32[]{:S(2)}) collective-permute-start(f16[2,64,512]{2,1,0:T(8,128)(2,1)S(1)} %convert_element_type.20), channel_id=1, source_target_pairs={{0,4},{2,6},{4,0},{6,2},{1,5},{3,7},{5,1},{7,3},{8,12},{10,14},{12... | collective-permute-start | bytes 393224 | tf_op jit(solution)/shard_map/ppermute | solution.py:451
  110.3 10.4 %collective-permute-start.3 = (f16[2,64,512]{2,1,0:T(8,128)(2,1)S(1)}, f16[2,64,512]{2,1,0:T(8,128)(2,1)S(1)}, u32[]{:S(2)}, u32[]{:S(2)}) collective-permute-start(f16[2,64,512]{2,1,0:T(8,128)(2,1)S(1)} %convert_element_type.18), channel_id=1, source_target_pairs={{0,2},{2,0},{4,6},{6,4},{1,3},{3,1},{5,7},{7,5},{8,10},{10,8},{12,... | collective-permute-start | bytes 393224 | tf_op jit(solution)/shard_map/ppermute | solution.py:451

commit v7 on v6

--- a/solution.py
+++ b/solution.py
@@ -284,7 +284,7 @@
         out_specs=[pl.BlockSpec(memory_space=pltpu.VMEM)] * 4,
         out_shape=[shape] * 4,
         scratch_shapes=[pltpu.SemaphoreType.DMA((4,))],
-        compiler_params=pltpu.CompilerParams(vmem_limit_bytes=4 * MIB),
+        compiler_params=pltpu.CompilerParams(vmem_limit_bytes=56 * MIB),
     )(voltages)
 
 

time: 122 us -> 125 us (1.025)
  Pallas kernels: 14.8 us -> 17.6 us
    pallas_call x1, Pallas kernels: 0.18 us -> 2.89 us  [load(): pl.pallas_call(load_kernel, in_specs=[pl.BlockSpec(memory_space=pltpu.HBM...]
    pallas_call x2, local copies, waits for them, and re-layouts: 0.32 us -> 2.52 us  [load(): pl.pallas_call(load_kernel, in_specs=[pl.BlockSpec(memory_space=pltpu.HBM...]
    unnamed x8 -> x10, local copies, waits for them, and re-layouts: 1.61 us -> 0.03 us
  transfers between devices with their start and end apart: 6 -> 6, of which waited for: 3 -> 3; matrix products, arithmetic and copies ran while one was open for 0% -> 1% of each run, Pallas kernels for 8% -> 8%
where the time goes in v7:
time: 125 us; the launch traced here: 124 us
  blocking collectives  71.1 us (57%)
  starting transfers between devices  21.7 us (17%)
  Pallas kernels  17.6 us (14%)
  waiting for transfers between devices  9.38 us (8%)
  local copies, waits for them, and re-layouts  4.11 us (3%)
    all_to_all x1, blocking collectives, on_device(): arrived = lax.all_to_all(chunks, ('z', 'h', 'x', 'l'), 0, 0, tiled=True)  71.1 us
    pallas_call x4, Pallas kernels, front(): pl.pallas_call(body, grid=(STEPS,), in_specs=[frame_spec(), frame_spec()]...  10.6 us
    ppermute x3, starting transfers between devices, exchange(): return lax.ppermute(values.astype(jnp.float16), 'l', route).astype(F32)  9.27 us
    ppermute x3, waiting for transfers between devices, exchange(): return lax.ppermute(values.astype(jnp.float16), 'l', route).astype(F32)  8.1 us
    ppermute x1, starting transfers between devices, on_device(): received = lax.ppermute(gram(1, spectra), 'c', [(0, 1), (1, 0)])  5.92 us
    ppermute x1, starting transfers between devices, on_device(): history_lower = lax.ppermute(late_lower, ('l', 'c'), forward)  4.59 us
    pallas_call x2, Pallas kernels, gram(): pl.pallas_call(functools.partial(gram_kernel, side), in_specs=[pl.BlockSp...  3.41 us
    pallas_call x1, Pallas kernels, load(): pl.pallas_call(load_kernel, in_specs=[pl.BlockSpec(memory_space=pltpu.HBM...  2.89 us
  transfers between devices with their start and end apart: 6, of which 3 were waited for; matrix products, arithmetic and copies ran while one was open for 1% of the time, Pallas kernels for 8%

profile of v7, /device:TPU:1, one launch (start us, length us, event | category | flops | bytes accessed | tf_op | source)
XLA Modules:
  0.0 124.3 jit_solution(569471774699891487)
XLA Ops:
  0.0 2.9 %shard_map.46 = (bf16[4,16,2,2048]{3,2,1,0:T(2,128)(2,1)}, bf16[4,16,2,2048]{3,2,1,0:T(2,128)(2,1)}, bf16[4,16,2,2048]{3,2,1,0:T(2,128)(2,1)}, bf16[4,16,2,2048]{3,2,1,0:T(2,128)(2,1)}) custom-call(bf16[8,32,2,2048]{3,2,1,0:T(2,128)(2,1)} %voltages_ref.1), custom_call_target="tpu_custom_call" | custom-call | tf_op jit(solution)/shard_map/pallas_call | solution.py:281
  2.9 0.0 copy-start.3
  2.9 0.0 copy-start.4
  2.9 0.0 copy-start
  2.9 0.0 copy-start.1
  2.9 0.0 copy-start.2
  3.0 1.3 %copy.14 = bf16[4,16,2,2048]{3,1,0,2:T(8,128)(2,1)S(1)} copy(bf16[4,16,2,2048]{3,2,1,0:T(2,128)(2,1)} %get-tuple-element.19) | data formatting | bytes 1048576 | tf_op jit(solution)/shard_map/pallas_call | solution.py:281
  4.3 4.6 %collective-permute-start.1 = (bf16[2,4,16,2048]{3,2,1,0:T(8,128)(2,1)S(1)}, bf16[2,4,16,2048]{3,2,1,0:T(8,128)(2,1)S(1)}, u32[]{:S(2)}, u32[]{:S(2)}) collective-permute-start(bf16[2,4,16,2048]{3,2,1,0:T(8,128)(2,1)S(1)} %bitcast.19), channel_id=1, source_target_pairs={{0,1},{1,2},{2,3},{3,4},{4,5},{5,6},{6,7},{8,9},{9,10},{10,11},{11... | collective-permute-start | bytes 1572872 | tf_op jit(solution)/shard_map/ppermute | solution.py:470
  8.9 1.2 copy.15
  10.1 1.9 %collective-permute-start = (bf16[2,4,16,2048]{3,2,1,0:T(8,128)(2,1)S(1)}, bf16[2,4,16,2048]{3,2,1,0:T(8,128)(2,1)S(1)}, u32[]{:S(2)}, u32[]{:S(2)}) collective-permute-start(bf16[2,4,16,2048]{3,2,1,0:T(8,128)(2,1)S(1)} %bitcast.17), channel_id=1, source_target_pairs={{0,1},{1,2},{2,3},{3,4},{4,5},{5,6},{6,7},{8,9},{9,10},{10,11},{11... | collective-permute-start | bytes 1572872 | tf_op jit(solution)/shard_map/ppermute | solution.py:471
  12.0 0.0 copy-done.3
  12.0 0.0 copy-done.4
  12.0 0.4 copy_bitcast_fusion.1
  12.4 0.0 copy-done
  12.4 0.0 copy-done.1
  12.4 0.0 copy-done.2
  12.4 2.5 %shard_map.47 = (bf16[4,256,256]{2,1,0:T(8,128)(2,1)S(1)}, f32[16,16,128]{2,1,0:T(8,128)S(1)}) custom-call(bf16[2,4,16,2048]{3,2,1,0:T(8,128)(2,1)S(1)} %get-tuple-element.27.hist_ref.cur_ref, bf16[2,4,16,2048]{3,2,1,0:T(8,128)(2,1)S(1)} %bitcast.20, f32[2,8,2048]{2,1,0:T(8,128)S(1)} %copy-done.2, f32[16,2304]{1,0:T(8,128)S(1)} %copy-done.1, ...), custom_call_target="tpu_custom_call" | custom-call | flops 700000000 | bytes 3145728 | tf_op jit(solution)/shard_map/pallas_call | solution.py:302
  14.9 2.9 %shard_map.49.mixed_ref = bf16[128,2,16,128]{3,2,1,0:T(8,128)(2,1)S(1)} custom-call(bf16[2,4,16,2048]{3,2,1,0:T(8,128)(2,1)S(1)} %get-tuple-element.28.hist_ref.cur_ref, bf16[2,4,16,2048]{3,2,1,0:T(8,128)(2,1)S(1)} %bitcast.18, f32[16,16,128]{2,1,0:T(8,128)S(1)} %get-tuple-element.20.gain_ref, f32[16,2304]{1,0:T(8,128)S(1)} %copy-done.1, ...), custom_call_target="tpu_custom_call" | custom-call | flops 700000000 | bytes 3145728 | tf_op jit(solution)/shard_map/pallas_call | solution.py:302
  17.8 0.0 collective-permute-done.1.hist_ref
  17.8 2.1 %shard_map.48.lower_ref = bf16[4,256,256]{2,1,0:T(8,128)(2,1)S(1)} custom-call(bf16[2,4,16,2048]{3,2,1,0:T(8,128)(2,1)S(1)} %collective-permute-done.1.hist_ref, bf16[2,4,16,2048]{3,2,1,0:T(8,128)(2,1)S(1)} %get-tuple-element.27.hist_ref.cur_ref, f32[16,16,128]{2,1,0:T(8,128)S(1)} %get-tuple-element.20.gain_ref, f32[16,2304]{1,0:T(8,128)S(1)} %copy-done.1, ...), custom_call_target="tpu_custom_call" | custom-call | flops 700000000 | bytes 3145728 | tf_op jit(solution)/shard_map/pallas_call | solution.py:302
  19.9 0.7 collective-permute-done.hist_ref
  20.6 3.1 %shard_map.50 = bf16[128,2,2,16,128]{4,3,2,1,0:T(8,128)(2,1)S(1)} custom-call(bf16[2,4,16,2048]{3,2,1,0:T(8,128)(2,1)S(1)} %collective-permute-done.hist_ref, bf16[2,4,16,2048]{3,2,1,0:T(8,128)(2,1)S(1)} %get-tuple-element.28.hist_ref.cur_ref, f32[16,16,128]{2,1,0:T(8,128)S(1)} %get-tuple-element.20.gain_ref, f32[16,2304]{1,0:T(8,128)S(1)} %copy-done.1, ...), custom_call_target="tpu_custom_call" | custom-call | flops 700000000 | bytes 3145728 | tf_op jit(solution)/shard_map/pallas_call | solution.py:302
  23.7 71.1 %all_to_all.5 = bf16[256,2,16,128]{3,2,1,0:T(8,128)(2,1)S(1)} all-to-all(bf16[256,2,16,128]{3,2,1,0:T(8,128)(2,1)S(1)} %bitcast.13), channel_id=1, replica_groups=mesh['z'=8,'h'=2,'x'=4,'l'=4,'c'=2] {'z','h','x','l'}, dimensions={0} | all-to-all | bytes 4194304 | tf_op jit(solution)/shard_map/all_to_all | solution.py:503
  94.9 1.8 %shard_map.52 = f32[4,2,64,512]{3,2,1,0:T(8,128)S(1)} custom-call(bf16[64,4,2,16,128]{4,3,2,1,0:T(8,128)(2,1)S(1)} %bitcast.14), custom_call_target="tpu_custom_call" | custom-call | flops 1100000000 | bytes 4194304 | tf_op jit(solution)/shard_map/pallas_call | solution.py:356
  96.6 5.9 %collective-permute-start.2 = (f32[4,2,64,512]{3,2,1,0:T(8,128)S(1)}, f32[4,2,64,512]{3,2,1,0:T(8,128)S(1)}, u32[]{:S(2)}, u32[]{:S(2)}) collective-permute-start(f32[4,2,64,512]{3,2,1,0:T(8,128)S(1)} %shard_map.52), channel_id=1, source_target_pairs={{0,1},{1,0},{2,3},{3,2},{4,5},{5,4},{6,7},{7,6},{8,9},{9,8},{10,11... | collective-permute-start | bytes 3145736 | tf_op jit(solution)/shard_map/ppermute | solution.py:505
  102.5 1.7 %shard_map.51.keep_ref = f32[4,2,64,512]{3,2,1,0:T(8,128)S(1)} custom-call(bf16[64,4,2,16,128]{4,3,2,1,0:T(8,128)(2,1)S(1)} %bitcast.15), custom_call_target="tpu_custom_call" | custom-call | flops 1100000000 | bytes 4194304 | tf_op jit(solution)/shard_map/pallas_call | solution.py:356
  104.2 0.6 collective-permute-done.2.received_ref
  104.8 0.3 shard_map.53
  105.1 4.2 %collective-permute-start.5 = (f16[2,64,512]{2,1,0:T(8,128)(2,1)S(1)}, f16[2,64,512]{2,1,0:T(8,128)(2,1)S(1)}, u32[]{:S(2)}, u32[]{:S(2)}) collective-permute-start(f16[2,64,512]{2,1,0:T(8,128)(2,1)S(1)} %convert_element_type.22), channel_id=1, source_target_pairs={{0,6},{2,4},{4,2},{6,0},{1,7},{3,5},{5,3},{7,1},{8,14},{10,12},{12... | collective-permute-start | bytes 393224 | tf_op jit(solution)/shard_map/ppermute | solution.py:451
  109.3 2.9 %collective-permute-start.4 = (f16[2,64,512]{2,1,0:T(8,128)(2,1)S(1)}, f16[2,64,512]{2,1,0:T(8,128)(2,1)S(1)}, u32[]{:S(2)}, u32[]{:S(2)}) collective-permute-start(f16[2,64,512]{2,1,0:T(8,128)(2,1)S(1)} %convert_element_type.20), channel_id=1, source_target_pairs={{0,4},{2,6},{4,0},{6,2},{1,5},{3,7},{5,1},{7,3},{8,12},{10,14},{12... | collective-permute-start | bytes 393224 | tf_op jit(solution)/shard_map/ppermute | solution.py:451
  112.3 0.1 shard_map.54
  112.4 2.1 %collective-permute-start.3 = (f16[2,64,512]{2,1,0:T(8,128)(2,1)S(1)}, f16[2,64,512]{2,1,0:T(8,128)(2,1)S(1)}, u32[]{:S(2)}, u32[]{:S(2)}) collective-permute-start(f16[2,64,512]{2,1,0:T(8,128)(2,1)S(1)} %convert_element_type.18), channel_id=1, source_target_pairs={{0,2},{2,0},{4,6},{6,4},{1,3},{3,1},{5,7},{7,5},{8,10},{10,8},{12,... | collective-permute-start | bytes 393224 | tf_op jit(solution)/shard_map/ppermute | solution.py:451
  114.5 0.0 collective-permute-done.5
  114.6 8.1 %collective-permute-done.4 = f16[2,64,512]{2,1,0:T(8,128)(2,1)S(1)} collective-permute-done((f16[2,64,512]{2,1,0:T(8,128)(2,1)S(1)}, f16[2,64,512]{2,1,0:T(8,128)(2,1)S(1)}, u32[]{:S(2)}, u32[]{:S(2)}) %collective-permute-start.4) | collective-permute-done | bytes 131104 | tf_op jit(solution)/shard_map/ppermute | solution.py:451
  122.7 0.2 shard_map.55.other_ref
  122.9 0.0 collective-permute-done.3
  122.9 0.2 shard_map.56
  123.1 1.2 copy.9
  (6 shorter events, 0.1 us)
Async XLA Ops:
  2.9 9.1 %copy-start.3 = (bf16[4,16,2,2048]{3,2,1,0:T(2,128)(2,1)S(1)}, bf16[4,16,2,2048]{3,2,1,0:T(2,128)(2,1)}, u32[]{:S(2)}) copy-start(bf16[4,16,2,2048]{3,2,1,0:T(2,128)(2,1)} %get-tuple-element.18) | copy-start | bytes 1572868
  2.9 9.1 %copy-start.4 = (bf16[4,16,2,2048]{3,2,1,0:T(2,128)(2,1)S(1)}, bf16[4,16,2,2048]{3,2,1,0:T(2,128)(2,1)}, u32[]{:S(2)}) copy-start(bf16[4,16,2,2048]{3,2,1,0:T(2,128)(2,1)} %get-tuple-element.17) | copy-start | bytes 1572868
  2.9 9.5 %copy-start = (bf16[4,256,256]{2,1,0:T(8,128)(2,1)S(1)}, bf16[4,256,256]{2,1,0:T(8,128)(2,1)}, u32[]{:S(2)}) copy-start(bf16[4,256,256]{2,1,0:T(8,128)(2,1)} %constant.5.clone.matrix_ref) | copy-start | bytes 1572868
  2.9 9.5 %copy-start.1 = (f32[16,2304]{1,0:T(8,128)S(1)}, f32[16,2304]{1,0:T(8,128)}, u32[]{:S(2)}) copy-start(f32[16,2304]{1,0:T(8,128)} %constant.4.clone.vector_ref) | copy-start | bytes 442372
  2.9 9.5 %copy-start.2 = (f32[2,8,2048]{2,1,0:T(8,128)S(1)}, f32[2,8,2048]{2,1,0:T(8,128)}, u32[]{:S(2)}) copy-start(f32[2,8,2048]{2,1,0:T(8,128)} %gain_ref.1) | copy-start | bytes 393220
  4.3 13.5 %collective-permute-start.1 = (bf16[2,4,16,2048]{3,2,1,0:T(8,128)(2,1)S(1)}, bf16[2,4,16,2048]{3,2,1,0:T(8,128)(2,1)S(1)}, u32[]{:S(2)}, u32[]{:S(2)}) collective-permute-start(bf16[2,4,16,2048]{3,2,1,0:T(8,128)(2,1)S(1)} %bitcast.19), channel_id=1, source_target_pairs={{0,1},{1,2},{2,3},{3,4},{4,5},{5,6},{6,7},{8,9},{9,10},{10,11},{11... | collective-permute-start | bytes 1572872 | tf_op jit(solution)/shard_map/ppermute | solution.py:470
  10.1 10.5 %collective-permute-start = (bf16[2,4,16,2048]{3,2,1,0:T(8,128)(2,1)S(1)}, bf16[2,4,16,2048]{3,2,1,0:T(8,128)(2,1)S(1)}, u32[]{:S(2)}, u32[]{:S(2)}) collective-permute-start(bf16[2,4,16,2048]{3,2,1,0:T(8,128)(2,1)S(1)} %bitcast.17), channel_id=1, source_target_pairs={{0,1},{1,2},{2,3},{3,4},{4,5},{5,6},{6,7},{8,9},{9,10},{10,11},{11... | collective-permute-start | bytes 1572872 | tf_op jit(solution)/shard_map/ppermute | solution.py:471
  96.6 8.2 %collective-permute-start.2 = (f32[4,2,64,512]{3,2,1,0:T(8,128)S(1)}, f32[4,2,64,512]{3,2,1,0:T(8,128)S(1)}, u32[]{:S(2)}, u32[]{:S(2)}) collective-permute-start(f32[4,2,64,512]{3,2,1,0:T(8,128)S(1)} %shard_map.52), channel_id=1, source_target_pairs={{0,1},{1,0},{2,3},{3,2},{4,5},{5,4},{6,7},{7,6},{8,9},{9,8},{10,11... | collective-permute-start | bytes 3145736 | tf_op jit(solution)/shard_map/ppermute | solution.py:505
  105.1 9.4 %collective-permute-start.5 = (f16[2,64,512]{2,1,0:T(8,128)(2,1)S(1)}, f16[2,64,512]{2,1,0:T(8,128)(2,1)S(1)}, u32[]{:S(2)}, u32[]{:S(2)}) collective-permute-start(f16[2,64,512]{2,1,0:T(8,128)(2,1)S(1)} %convert_element_type.22), channel_id=1, source_target_pairs={{0,6},{2,4},{4,2},{6,0},{1,7},{3,5},{5,3},{7,1},{8,14},{10,12},{12... | collective-permute-start | bytes 393224 | tf_op jit(solution)/shard_map/ppermute | solution.py:451
  109.3 13.3 %collective-permute-start.4 = (f16[2,64,512]{2,1,0:T(8,128)(2,1)S(1)}, f16[2,64,512]{2,1,0:T(8,128)(2,1)S(1)}, u32[]{:S(2)}, u32[]{:S(2)}) collective-permute-start(f16[2,64,512]{2,1,0:T(8,128)(2,1)S(1)} %convert_element_type.20), channel_id=1, source_target_pairs={{0,4},{2,6},{4,0},{6,2},{1,5},{3,7},{5,1},{7,3},{8,12},{10,14},{12... | collective-permute-start | bytes 393224 | tf_op jit(solution)/shard_map/ppermute | solution.py:451
  112.4 10.5 %collective-permute-start.3 = (f16[2,64,512]{2,1,0:T(8,128)(2,1)S(1)}, f16[2,64,512]{2,1,0:T(8,128)(2,1)S(1)}, u32[]{:S(2)}, u32[]{:S(2)}) collective-permute-start(f16[2,64,512]{2,1,0:T(8,128)(2,1)S(1)} %convert_element_type.18), channel_id=1, source_target_pairs={{0,2},{2,0},{4,6},{6,4},{1,3},{3,1},{5,7},{7,5},{8,10},{10,8},{12,... | collective-permute-start | bytes 393224 | tf_op jit(solution)/shard_map/ppermute | solution.py:451
